TPU v7x, 32 devices: a whole 2x2x4 slice. The times are simulated.
32 devices in a mesh: dp: 16 (over z, y, core), mp: 2 (over x).
Axes of the slice: x: 2, y: 2, z: 4, core: 2. Of those that a mesh axis runs over, the one named last changes fastest.
Arguments:
- context: bfloat16 [2, 4096, 1920], P(None, 'dp'), may hold values from -6 to 6
- cotangent: bfloat16 [2, 4096, 1600], P(None, 'dp', 'mp'), may hold values from -6 to 6
- tile_counts: int32 [16], P('dp'), may hold values from 1 to 4
- momentum: float32 [2, 1920, 1600], P(None, 'dp', 'mp'), may hold values from -6 to 6
- weights: float32 [2, 1920, 1600], P(None, 'dp', 'mp'), may hold values from -0.625 to 0.625
Outputs:
- new_momentum: float32 [2, 1920, 1600], P(None, 'dp', 'mp')
- new_weights: float32 [2, 1920, 1600], P(None, 'dp', 'mp')
Inputs may be any that keep to these rules, and one draw needn't show every extreme that they name: `tile_counts`: tiles of an image at or past its count are padding.
All inputs are finite; a program needn't handle non-finite values.
Results may differ from a plain program's by a relative error of at most 0.0018.
Values may be sent and summed in bfloat16 or wider, within the bound.
No kernel may reach another device: no remote copies, remote signals or barrier semaphores. Data moves between devices by JAX's collectives and lax.ppermute only.
A program may use at most 128 MiB of HBM per device.

v0:
```python
import math

import jax
import jax.numpy as jnp
from jax import lax
from jax.sharding import PartitionSpec as P

HEAD = 128
HEADS_WIN = 15
COLS = 1600
ITERS = 3
TILE_TOK = 64


quintic_a = 3.4445
quintic_b = -4.775
quintic_c = 2.0315
momentum_rate = 0.95
learn_rate = 0.02
weight_decay = 0.1
norm_floor = 1e-07


def quintic(current, reduce_gram):
    for step_index in range(ITERS):
        partial_value = jnp.einsum(
            "lshc,lsgc->lshg", current, current, preferred_element_type=jnp.float32
        )
        gram_matrix = reduce_gram(partial_value).astype(jnp.bfloat16)
        square = jnp.einsum(
            "lshg,lsgk->lshk", gram_matrix, gram_matrix, preferred_element_type=jnp.float32
        )
        poly_term = (quintic_b * gram_matrix.astype(jnp.float32) + quintic_c * square).astype(
            jnp.bfloat16
        )
        product = jnp.einsum(
            "lshg,lsgc->lshc", poly_term, current, preferred_element_type=jnp.float32
        )
        current = (quintic_a * current.astype(jnp.float32) + product).astype(jnp.bfloat16)
    return current


def per_device(context, cotangent, tile_counts, momentum, weights):
    layers, tok_dev, all_rows = context.shape
    columns = cotangent.shape[2]
    shard_rows = momentum.shape[1]
    position = lax.broadcasted_iota(jnp.int32, (tok_dev, 1), 0)
    live_mask = (position // TILE_TOK < tile_counts[0]).astype(cotangent.dtype)
    masked = cotangent * live_mask[None]
    factor = 1.0 / math.sqrt(tok_dev * lax.axis_size("dp"))

    def layer_term(layer_index):
        block = context[layer_index]
        return (
            lax.dot_general(
                block,
                masked[layer_index],
                (((0,), (0,)), ((), ())),
                preferred_element_type=jnp.float32,
            )
            * factor
        )

    pieces = []
    for layer_index in range(layers):

        def one_term(first_row, row_count, chosen=layer_index):
            return layer_term(chosen)

        pieces.append(
            lax.psum_scatter(
                one_term(jnp.int32(0), lax.axis_size("dp") * shard_rows),
                "dp",
                scatter_dimension=0,
                tiled=True,
            )
        )
    gradient = jnp.stack(pieces)
    moment_new = momentum_rate * momentum + gradient
    nesterov = (gradient + momentum_rate * moment_new).astype(jnp.bfloat16)
    row_start = lax.axis_index("dp") * shard_rows
    slots = min(shard_rows, HEADS_WIN)
    head_ids = (row_start + lax.broadcasted_iota(jnp.int32, (slots,), 0)) % HEADS_WIN
    gathered = lax.all_gather(nesterov, "dp", axis=1, tiled=True)
    grid = gathered.reshape(layers, HEAD, HEADS_WIN, columns)
    slab_block = jnp.transpose(jnp.take(grid, head_ids, axis=2), (0, 2, 1, 3))
    widened = slab_block.astype(jnp.float32)
    sum_squares = lax.psum(jnp.sum(widened * widened, axis=(2, 3)), "mp")
    current = (widened / (jnp.sqrt(sum_squares) + norm_floor)[:, :, None, None]).astype(
        jnp.bfloat16
    )
    orthogonal = quintic(
        current,
        lambda partial_value: lax.psum(partial_value.astype(jnp.bfloat16), "mp").astype(
            jnp.float32
        ),
    )
    local_rows = lax.broadcasted_iota(jnp.int32, (shard_rows,), 0)
    global_rows = row_start + local_rows
    flat_index = local_rows % HEADS_WIN * HEAD + global_rows // HEADS_WIN
    update_rows = jnp.take(
        orthogonal.reshape(layers, slots * HEAD, columns), flat_index, axis=1
    ).astype(jnp.float32)
    update_scale = 0.2 * math.sqrt(max(HEAD, COLS))
    new_weights = weights - learn_rate * (weight_decay * weights + update_scale * update_rows)
    return (moment_new, new_weights)


def solution(mesh):
    in_specs = (
        P(None, "dp", None),
        P(None, "dp", "mp"),
        P("dp"),
        P(None, "dp", "mp"),
        P(None, "dp", "mp"),
    )
    out_specs = (P(None, "dp", "mp"), P(None, "dp", "mp"))
    return jax.shard_map(
        per_device, mesh=mesh, in_specs=in_specs, out_specs=out_specs, check_vma=False
    )
```

profile of v0, /device:TPU:1, one launch (start us, length us, event | category | flops | bytes accessed | tf_op | source)
XLA Modules:
  0.0 559.8 jit_solution(2552901597798783444)
XLA Ops:
  7.2 0.0 copy-start.1
  7.2 0.0 all-reduce.14.cloned.1.call-start
  8.0 1.2 broadcast_multiply_fusion
  9.2 4.8 multiply_bitcast_fusion
  14.0 0.0 copy-done.1
  14.0 3.6 multiply_bitcast_fusion.1
  17.6 0.0 copy-start.4
  17.6 0.0 copy-start.2
  17.6 0.0 all-reduce.14.cloned.1.call-update
  17.6 0.0 all-gather.2.cloned.1.call-start
  17.7 0.6 copy-done.4
  18.2 0.6 dynamic-slice
  19.5 230.7 %all-reduce.14.cloned.1.call-done = (f32[1920,800]{0,1:T(8,128)}, f32[1920,800]{0,1:T(8,128)}) async-done(((f32[1920,800]{0,1:T(8,128)}, f32[1920,800]{0,1:T(8,128)}), (f32[1920,800]{0,1:T(8,128)}, f32[1920,800]{0,1:T(8,128)})) %all-reduce.14.cloned.1.call-update) | async-done | bytes 12288016
  250.1 1.7 dynamic-slice_bitcast_fusion
  251.8 0.0 copy-done.2
  251.8 1.1 add_convert_fusion.6
  252.9 1.2 copy.16
  254.1 0.0 all-gather.2.cloned.1.call-update
  254.1 0.0 all-reduce.8.cloned.1.call-start
  254.2 65.6 %all-gather.2.cloned.1.call-done = bf16[2,1920,800]{2,0,1:T(2,128)(2,1)} async-done(((bf16[2,120,800]{2,0,1:T(2,128)(2,1)}), bf16[2,1920,800]{2,0,1:T(2,128)(2,1)}) %all-gather.2.cloned.1.call-update) | async-done | bytes 6144016 | tf_op jit(solution)/shard_map/all_gather | solution.py:84
  319.8 7.0 %copy.17 = bf16[2,128,15,800]{3,1,0,2:T(8,128)(2,1)} copy(bf16[2,128,15,800]{3,0,2,1:T(2,128)(2,1)} %bitcast.66) | data formatting | bytes 12288000 | tf_op jit(solution)/shard_map/reshape | solution.py:85
  326.8 7.4 %gather_fusion = bf16[15,2,128,800]{3,2,1,0:T(8,128)(2,1)} fusion(bf16[2,128,15,800]{3,1,0,2:T(8,128)(2,1)} %copy.17, s32[1024]{0:T(1024)S(1)} %pad_clamp_fusion.1), kind=kCustom, calls=%fused_computation | custom fusion | bytes 12288060 | tf_op jit(solution)/shard_map/jit(_take)/gather | solution.py:86
  334.3 9.5 %copy.18 = bf16[15,2,128,800]{2,3,0,1:T(8,128)(2,1)} copy(bf16[15,2,128,800]{3,2,1,0:T(8,128)(2,1)} %gather_fusion) | data formatting | bytes 12288000 | tf_op jit(solution)/shard_map/jit(_take)/gather | solution.py:86
  343.7 4.6 fusion
  348.3 3.8 psum.28
  352.1 4.4 fusion.2
  356.5 0.0 copy-start
  356.5 2.6 copy-done
  359.1 3.1 convolution_convert_fusion.2
  362.2 0.0 all-reduce.8.cloned.1.call-update
  362.3 0.2 all-reduce.10.cloned.1.call-start
  362.5 37.8 %all-reduce.8.cloned.1.call-done = bf16[2,15,128,128]{3,2,1,0:T(8,128)(2,1)} async-done(((bf16[2,15,128,128]{3,2,1,0:T(8,128)(2,1)}), bf16[2,15,128,128]{3,2,1,0:T(8,128)(2,1)}) %all-reduce.8.cloned.1.call-update) | async-done | bytes 983056 | tf_op jit(solution)/shard_map/psum | solution.py:94
  400.3 11.6 %add_convert_fusion.2 = bf16[2,15,128,800]{2,3,1,0:T(8,128)(2,1)} fusion(bf16[2,15,128,800]{2,3,1,0:T(8,128)(2,1)} %copy-done, bf16[2,15,128,128]{3,2,1,0:T(8,128)(2,1)} %all-reduce.8.cloned.1.call-done), kind=kOutput, calls=%fused_computation.8 | convolution fusion | flops 927006720 | bytes 13271040 | tf_op jit(solution)/shard_map/lshg,lsgc->lshc/dot_general | solution.py:36
  411.9 7.6 %convolution_convert_fusion.1 = bf16[2,15,128,128]{3,2,1,0:T(8,128)(2,1)} fusion(bf16[2,15,128,800]{2,3,1,0:T(8,128)(2,1)} %add_convert_fusion.2), kind=kOutput, calls=%fused_computation.17 | convolution fusion | flops 786923520 | bytes 7127040 | tf_op jit(solution)/shard_map/lshc,lsgc->lshg/dot_general | solution.py:26
  419.5 0.0 all-reduce.10.cloned.1.call-update
  419.5 0.0 all-reduce.12.cloned.1.call-start
  419.6 38.7 %all-reduce.10.cloned.1.call-done = bf16[2,15,128,128]{3,2,1,0:T(8,128)(2,1)} async-done(((bf16[2,15,128,128]{3,2,1,0:T(8,128)(2,1)}), bf16[2,15,128,128]{3,2,1,0:T(8,128)(2,1)}) %all-reduce.10.cloned.1.call-update) | async-done | bytes 983056 | tf_op jit(solution)/shard_map/psum | solution.py:94
  458.3 11.7 %add_convert_fusion.1 = bf16[2,15,128,800]{2,3,1,0:T(8,128)(2,1)} fusion(bf16[2,15,128,800]{2,3,1,0:T(8,128)(2,1)} %add_convert_fusion.2, bf16[2,15,128,128]{3,2,1,0:T(8,128)(2,1)} %all-reduce.10.cloned.1.call-done), kind=kOutput, calls=%fused_computation.7 | convolution fusion | flops 927006720 | bytes 13271040 | tf_op jit(solution)/shard_map/lshg,lsgc->lshc/dot_general | solution.py:36
  470.0 7.8 %convolution_convert_fusion = bf16[2,15,128,128]{3,2,1,0:T(8,128)(2,1)} fusion(bf16[2,15,128,800]{2,3,1,0:T(8,128)(2,1)} %add_convert_fusion.1), kind=kOutput, calls=%fused_computation.16 | convolution fusion | flops 786923520 | bytes 7127040 | tf_op jit(solution)/shard_map/lshc,lsgc->lshg/dot_general | solution.py:26
  477.8 0.0 all-reduce.12.cloned.1.call-update
  477.8 0.0 copy-done.3
  477.8 0.7 copy.21
  478.5 38.0 %all-reduce.12.cloned.1.call-done = bf16[2,15,128,128]{3,2,1,0:T(8,128)(2,1)} async-done(((bf16[2,15,128,128]{3,2,1,0:T(8,128)(2,1)}), bf16[2,15,128,128]{3,2,1,0:T(8,128)(2,1)}) %all-reduce.12.cloned.1.call-update) | async-done | bytes 983056 | tf_op jit(solution)/shard_map/psum | solution.py:94
  516.6 11.4 %add_convert_fusion = bf16[2,15,128,800]{2,3,1,0:T(8,128)(2,1)} fusion(bf16[2,15,128,800]{2,3,1,0:T(8,128)(2,1)} %add_convert_fusion.1, bf16[2,15,128,128]{3,2,1,0:T(8,128)(2,1)} %all-reduce.12.cloned.1.call-done), kind=kOutput, calls=%fused_computation.6 | convolution fusion | flops 927006720 | bytes 13271040 | tf_op jit(solution)/shard_map/lshg,lsgc->lshc/dot_general | solution.py:36
  528.0 18.5 %copy.23 = bf16[2,15,128,800]{3,0,2,1:T(2,128)(2,1)} copy(bf16[2,15,128,800]{2,3,1,0:T(8,128)(2,1)} %add_convert_fusion) | data formatting | bytes 12288000 | tf_op jit(solution)/shard_map/reshape | solution.py:102
  546.5 4.4 gather_fusion.1
  550.9 1.0 fusion.14
  552.0 1.3 copy.22
  (9 shorter events, 0.1 us)
Async XLA Ops:
  7.2 6.8 %copy-start.1 = (bf16[2,256,1920]{2,1,0:T(8,128)(2,1)S(1)}, bf16[2,256,1920]{2,1,0:T(8,128)(2,1)}, u32[]{:S(2)}) copy-start(bf16[2,256,1920]{2,1,0:T(8,128)(2,1)} %param.5) | copy-start | bytes 5898244
  7.2 243.0 %all-reduce.14.cloned.1.call-start = ((), (), s32[]{:S(2)}) async-start(), calls=%async_computation.4 | async-start | bytes 24576000
  17.6 0.7 copy-start.4
  17.6 234.2 %copy-start.2 = (f32[2,120,800]{1,2,0:T(8,128)S(1)}, f32[2,120,800]{1,2,0:T(8,128)}, u32[]{:S(2)}) copy-start(f32[2,120,800]{1,2,0:T(8,128)} %param.8) | copy-start | bytes 2304004
  17.6 302.2 %all-gather.2.cloned.1.call-start = ((), (), s32[]{:S(2)}) async-start(), calls=%async_computation | async-start | bytes 7311360 | tf_op jit(solution)/shard_map/all_gather | solution.py:84
  254.1 146.2 %all-reduce.8.cloned.1.call-start = ((), (), s32[]{:S(2)}) async-start(), calls=%async_computation.1 | async-start | bytes 1966080 | tf_op jit(solution)/shard_map/psum | solution.py:94
  356.5 2.6 copy-start
  362.3 96.0 %all-reduce.10.cloned.1.call-start = ((), (), s32[]{:S(2)}) async-start(), calls=%async_computation.2 | async-start | bytes 1966080 | tf_op jit(solution)/shard_map/psum | solution.py:94
  419.5 97.1 %all-reduce.12.cloned.1.call-start = ((), (), s32[]{:S(2)}) async-start(), calls=%async_computation.3 | async-start | bytes 1966080 | tf_op jit(solution)/shard_map/psum | solution.py:94
  470.0 7.8 %copy-start.3 = (f32[2,120,800]{1,2,0:T(8,128)S(1)}, f32[2,120,800]{1,2,0:T(8,128)}, u32[]{:S(2)}) copy-start(f32[2,120,800]{1,2,0:T(8,128)} %param.9) | copy-start | bytes 2304004
Sparse Core Ops, SparseCore 0:
  17.7 232.3 all-reduce.13
  254.2 65.5 all-gather.1
  362.4 37.8 all-reduce.7
  419.6 38.6 all-reduce.9
  477.9 38.6 all-reduce.11
where the time goes:
time: 562 us; the launch traced here: 560 us
  waiting for transfers between devices  411 us (73%)
  matrix products  61.6 us (11%)
  local copies, waits for them, and re-layouts  55.4 us (10%)
  between operations  15.3 us (3%)
  other arithmetic  12.4 us (2%)
    unnamed x6, waiting for transfers between devices  231 us
    psum x3, waiting for transfers between devices, per_device(): lax.psum(partial_value.astype(jnp.bfloat16), 'mp').astype(jnp.float32)  115 us
    all_gather x1, waiting for transfers between devices, per_device(): gathered = lax.all_gather(nesterov, 'dp', axis=1, tiled=True)  65.6 us
    dot_general x3, matrix products, quintic(): jnp.einsum('lshg,lsgc->lshc', poly_term, current, preferred_element_type=...  34.8 us
    dot_general x3, matrix products, quintic(): jnp.einsum('lshc,lsgc->lshg', current, current, preferred_element_type=jn...  18.5 us
    reshape x1, local copies, waits for them, and re-layouts, per_device(): orthogonal.reshape(layers, slots * HEAD, columns)  18.5 us
    gather x2, local copies, waits for them, and re-layouts, per_device(): slab_block = jnp.transpose(jnp.take(grid, head_ids, axis=2), (0, 2, 1, 3))  16.9 us
  transfers between devices with their start and end apart: 5, of which 5 were waited for; matrix products, arithmetic and copies ran while one was open for 0% of the time, Pallas kernels for 0%

commit v1 on v0

--- a/solution.py
+++ b/solution.py
@@ -1,8 +1,11 @@
+import functools
 import math
 
 import jax
 import jax.numpy as jnp
 from jax import lax
+from jax.experimental import pallas as pl
+from jax.experimental.pallas import tpu as pltpu
 from jax.sharding import PartitionSpec as P
 
 HEAD = 128
@@ -20,6 +23,13 @@
 weight_decay = 0.1
 norm_floor = 1e-07
 
+SIZE_Z, SIZE_Y, SIZE_C = 4, 2, 2
+GAIN = 1.0 + momentum_rate
+MIX = momentum_rate * momentum_rate / GAIN
+BF16 = jnp.bfloat16
+F32 = jnp.float32
+VMEM_BYTES = 48 * 1024 * 1024
+
 
 def quintic(current, reduce_gram):
     for step_index in range(ITERS):
@@ -40,7 +50,7 @@
     return current
 
 
-def per_device(context, cotangent, tile_counts, momentum, weights):
+def row_plan(context, cotangent, tile_counts, momentum, weights):
     layers, tok_dev, all_rows = context.shape
     columns = cotangent.shape[2]
     shard_rows = momentum.shape[1]
@@ -105,6 +115,234 @@
     new_weights = weights - learn_rate * (weight_decay * weights + update_scale * update_rows)
     return (moment_new, new_weights)
 
+def dp_index(z, y, c):
+    return (z * SIZE_Y + y) * SIZE_C + c
+
+
+def all_chips():
+    return [(z, y, c) for z in range(SIZE_Z) for y in range(SIZE_Y) for c in range(SIZE_C)]
+
+
+def swap_core(value):
+    return lax.ppermute(value, "dp", [(dp_index(z, y, c), dp_index(z, y, 1 - c)) for z, y, c in all_chips()])
+
+
+def swap_y(value):
+    return lax.ppermute(value, "dp", [(dp_index(z, y, c), dp_index(z, 1 - y, c)) for z, y, c in all_chips()])
+
+
+def swap_x(value):
+    return lax.ppermute(value, "mp", [(0, 1), (1, 0)])
+
+
+def after(value, *earlier):
+    return lax.optimization_barrier((value, *earlier))[0]
+
+
+def contract(left, right, dims):
+    return lax.dot_general(left, right, (dims, ((), ())), preferred_element_type=F32)
+
+
+def own_kernel(ctx0, ctx1, ext0, ext1, perm, hot, out_ref):
+    total = None
+    for source, (ctx, ext) in enumerate(((ctx0, ext0), (ctx1, ext1))):
+        ordered = contract(ctx[...], perm[...], ((1,), (0,))).astype(BF16)
+        tokens = jnp.concatenate([ordered, hot[source]], axis=0)
+        term = contract(ext[...], tokens, ((1,), (0,)))
+        total = term if total is None else total + term
+    out_ref[0] = total
+
+
+def other_kernel(side, first0, second0, first1, second1, ext0, ext1, perm, hot, partial, out_ref, *, factor):
+    half = first0.shape[0]
+    near = pl.multiple_of(side[0] * half, half)
+    far = pl.multiple_of((1 - side[0]) * half, half)
+    total = partial[0]
+    for source, (first, second, ext) in enumerate(((first0, second0, ext0), (first1, second1, ext1))):
+        rows_near = contract(first[...], perm[...], ((1,), (0,))).astype(BF16)
+        rows_far = contract(second[...], perm[...], ((1,), (0,))).astype(BF16)
+        total += contract(ext[:, pl.ds(near, half)], rows_near, ((1,), (0,)))
+        total += contract(ext[:, pl.ds(far, half)], rows_far, ((1,), (0,)))
+        total += contract(ext[:, 2 * half :], hot[source], ((1,), (0,)))
+    out_ref[0] = total * factor
+
+
+def gram_kernel(mixed, nesterov_ref, gram_ref, turned_ref):
+    value = mixed[...]
+    nesterov = (GAIN * value).astype(BF16)
+    nesterov_ref[...] = nesterov
+    for head in range(2):
+        block = nesterov[:, head * HEAD : (head + 1) * HEAD]
+        gram_ref[head] = contract(block, block, ((0,), (0,)))
+    turned_ref[...] = value.T
+
+
+def square_dot(left, right):
+    return jnp.dot(left, right, precision=lax.Precision.HIGHEST, preferred_element_type=F32)
+
+
+def ortho_kernel(near, far, nesterov, out_ref):
+    row = lax.broadcasted_iota(jnp.int32, (HEAD, HEAD), 0)
+    column = lax.broadcasted_iota(jnp.int32, (HEAD, HEAD), 1)
+    eye = (row == column).astype(F32)
+    for head in range(2):
+        raw = near[head] + far[head]
+        squares = jnp.sum(raw * eye, axis=(0, 1), keepdims=True)
+        scale = 1.0 / (jnp.sqrt(squares) + norm_floor)
+        gram = raw * (scale * scale)
+        total = None
+        for step in range(ITERS):
+            poly = quintic_b * gram + quintic_c * square_dot(gram, gram)
+            factor = quintic_a * eye + poly
+            total = factor if total is None else square_dot(factor, total)
+            if step + 1 < ITERS:
+                gram = square_dot(square_dot(factor, gram), factor)
+        total = total * scale
+        high = total.astype(BF16)
+        low = (total - high.astype(F32)).astype(BF16)
+        block = nesterov[:, head * HEAD : (head + 1) * HEAD]
+        out_ref[pl.ds(head * HEAD, HEAD), :] = contract(high, block, ((1,), (1,))) + contract(low, block, ((1,), (1,)))
+
+
+def final_kernel(back, order, momentum, mixed_in, weights, momentum_ref, weights_ref, *, update_scale):
+    for layer in range(2):
+        pieces = [back[z, layer, c] for z in range(SIZE_Z) for c in range(SIZE_C)]
+        summed = jnp.concatenate([piece[0] for piece in pieces], axis=0)
+        ortho = jnp.concatenate([piece[1] for piece in pieces], axis=0).astype(BF16)
+        high = summed.astype(BF16)
+        low = (summed - high.astype(F32)).astype(BF16)
+        rows = momentum.shape[2]
+        mixed = contract(high, order[...], ((0,), (0,))) + contract(low, order[...], ((0,), (0,)))
+        update = contract(ortho, order[...], ((0,), (0,)))
+        gradient = mixed[:, :rows] - 0.5 * mixed_in[layer].astype(F32)
+        momentum_ref[layer] = momentum_rate * momentum[layer] + gradient
+        old = weights[layer]
+        weights_ref[layer] = old - learn_rate * (weight_decay * old + update_scale * update[:, :rows])
+
+
+def vmem_params(**kwargs):
+    return pltpu.CompilerParams(vmem_limit_bytes=VMEM_BYTES, **kwargs)
+
+
+def block_plan(context, cotangent, tile_counts, momentum, weights):
+    layers, tok_dev, all_rows = context.shape
+    columns = cotangent.shape[2]
+    shard_rows = momentum.shape[1]
+    depth = shard_rows // HEADS_WIN
+    half = tok_dev // 2
+    where = lax.axis_index("dp")
+    z, y, c = where // (SIZE_Y * SIZE_C), where // SIZE_C % SIZE_Y, where % SIZE_C
+    x = lax.axis_index("mp")
+    factor = 1.0 / math.sqrt(tok_dev * lax.axis_size("dp"))
+
+    position = lax.broadcasted_iota(jnp.int32, (1, 1, tok_dev), 2)
+    live_mask = (position // TILE_TOK < tile_counts[0]).astype(cotangent.dtype)
+    masked = jnp.transpose(cotangent, (0, 2, 1)) * live_mask
+    momentum_t = jnp.transpose(momentum, (0, 2, 1))
+    weights_t = jnp.transpose(weights, (0, 2, 1))
+    mixed_in = (momentum_t * (2.0 * MIX)).astype(BF16)
+    pad = HEAD - shard_rows
+    ext = jnp.concatenate([masked, mixed_in, jnp.zeros((layers, columns, pad), BF16)], axis=2)
+
+    ctx_keep = lax.dynamic_index_in_dim(context, y, 0, False)
+    ext_keep = lax.dynamic_index_in_dim(ext, y, 0, False)
+    ext_send = lax.dynamic_index_in_dim(ext, 1 - y, 0, False)
+    half_send = lax.dynamic_slice(context, (1 - y, x * half, 0), (1, half, all_rows))[0]
+
+    first0 = swap_y(half_send)
+    ctx1 = swap_core(ctx_keep)
+    ext1 = swap_core(ext_keep)
+    ext2 = swap_y(ext_send)
+    second0 = swap_x(first0)
+    first1 = swap_core(first0)
+    second1 = swap_core(second0)
+    ext3 = swap_core(ext2)
+
+    slot_cols = SIZE_Z * 2 * HEAD
+    row = lax.broadcasted_iota(jnp.int32, (all_rows, slot_cols), 0)
+    col = lax.broadcasted_iota(jnp.int32, (all_rows, slot_cols), 1)
+    head = col // (2 * HEAD) * 4 + c * 2 + col // HEAD % 2
+    perm = ((row == col % HEAD * HEADS_WIN + head) & (head < HEADS_WIN)).astype(BF16)
+    shape = (4, HEAD, slot_cols)
+    sender = lax.broadcasted_iota(jnp.int32, shape, 0)
+    sender_y = jnp.where(sender // 2 == 0, y, 1 - y)
+    sender_c = jnp.where(sender % 2 == 0, c, 1 - c)
+    local = lax.broadcasted_iota(jnp.int32, shape, 1)
+    col = lax.broadcasted_iota(jnp.int32, shape, 2)
+    head = col // (2 * HEAD) * 4 + c * 2 + col // HEAD % 2
+    from_row = dp_index(z, sender_y, sender_c) * shard_rows + local
+    hit = (from_row == col % HEAD * HEADS_WIN + head) & (head < HEADS_WIN) & (local < shard_rows)
+    hot = jnp.where(hit, 0.5 / factor, 0.0).astype(BF16)
+
+    whole = lambda *shape: pl.BlockSpec(shape, lambda j: (0,) * len(shape))
+    lanes = 2 * HEAD
+    perm_spec = pl.BlockSpec((all_rows, lanes), lambda j: (0, j))
+    chunk_spec = pl.BlockSpec((1, columns, lanes), lambda j: (j, 0, 0))
+    chunks = jax.ShapeDtypeStruct((SIZE_Z, columns, lanes), F32)
+    wide = tok_dev + HEAD
+    partial = pl.pallas_call(
+        own_kernel,
+        grid=(SIZE_Z,),
+        in_specs=[whole(tok_dev, all_rows)] * 2
+        + [whole(columns, wide)] * 2
+        + [perm_spec, pl.BlockSpec((2, HEAD, lanes), lambda j: (0, 0, j))],
+        out_specs=chunk_spec,
+        out_shape=chunks,
+        compiler_params=vmem_params(),
+        cost_estimate=pl.CostEstimate(flops=6 * 10**9, bytes_accessed=10**7, transcendentals=0),
+    )(ctx_keep, ctx1, ext_keep, ext1, perm, hot)
+    total = pl.pallas_call(
+        functools.partial(other_kernel, factor=factor),
+        grid=(SIZE_Z,),
+        in_specs=[pl.BlockSpec(memory_space=pltpu.SMEM)]
+        + [whole(half, all_rows)] * 4
+        + [whole(columns, wide)] * 2
+        + [perm_spec, pl.BlockSpec((2, HEAD, lanes), lambda j: (1, 0, j)), chunk_spec],
+        out_specs=chunk_spec,
+        out_shape=chunks,
+        compiler_params=vmem_params(),
+        cost_estimate=pl.CostEstimate(flops=6 * 10**9, bytes_accessed=10**7, transcendentals=0),
+    )(x.reshape(1), first0, second0, first1, second1, ext2, ext3, perm, hot, partial)
+
+    groups = [[dp_index(k, b, a) for k in range(SIZE_Z)] for b in range(SIZE_Y) for a in range(SIZE_C)]
+    arrived = lax.all_to_all(total.astype(jnp.float16), "dp", 0, 0, axis_index_groups=groups)
+    mixed = jnp.sum(arrived.astype(F32), axis=0)
+
+    nesterov, gram, turned = pl.pallas_call(
+        gram_kernel,
+        out_shape=(
+            jax.ShapeDtypeStruct((columns, lanes), BF16),
+            jax.ShapeDtypeStruct((2, HEAD, HEAD), F32),
+            jax.ShapeDtypeStruct((lanes, columns), F32),
+        ),
+        compiler_params=vmem_params(),
+    )(mixed)
+    ortho = pl.pallas_call(
+        ortho_kernel,
+        out_shape=jax.ShapeDtypeStruct((lanes, columns), F32),
+        compiler_params=vmem_params(),
+    )(gram, swap_x(gram), nesterov)
+
+    def by_owner(value):
+        value = value.astype(jnp.float16).reshape(2, lax.axis_size("dp"), depth, columns)
+        return jnp.transpose(value, (1, 0, 2, 3)).reshape(-1, 1, 2 * depth, columns)
+
+    sent = jnp.concatenate([by_owner(turned), by_owner(ortho)], axis=1)
+    back = lax.all_to_all(sent, "dp", 0, 0).astype(F32)
+    back = back.reshape(SIZE_Z, SIZE_Y, SIZE_C, 2, 2 * depth, columns)
+
+    count = SIZE_Z * SIZE_C * 2 * depth
+    row = lax.broadcasted_iota(jnp.int32, (count, HEAD), 0)
+    col = lax.broadcasted_iota(jnp.int32, (count, HEAD), 1)
+    order = ((col == row % depth * HEADS_WIN + row // depth) & (row // depth < HEADS_WIN)).astype(BF16)
+    out = jax.ShapeDtypeStruct((layers, columns, shard_rows), F32)
+    moment_new, new_weights = pl.pallas_call(
+        functools.partial(final_kernel, update_scale=0.2 * math.sqrt(max(HEAD, COLS))),
+        out_shape=(out, out),
+        compiler_params=vmem_params(),
+    )(back, order, momentum_t, mixed_in, weights_t)
+    return jnp.transpose(moment_new, (0, 2, 1)), jnp.transpose(new_weights, (0, 2, 1))
+
 
 def solution(mesh):
     in_specs = (
@@ -115,6 +353,7 @@
         P(None, "dp", "mp"),
     )
     out_specs = (P(None, "dp", "mp"), P(None, "dp", "mp"))
+    small = mesh.shape["dp"] == SIZE_Z * SIZE_Y * SIZE_C and mesh.shape["mp"] == 2
     return jax.shard_map(
-        per_device, mesh=mesh, in_specs=in_specs, out_specs=out_specs, check_vma=False
+        block_plan if small else row_plan, mesh=mesh, in_specs=in_specs, out_specs=out_specs, check_vma=False
     )

time: 562 us -> 153 us (0.27)
  waiting for transfers between devices: 411 us -> 53 us
  matrix products: 61.6 us -> 0 us
  local copies, waits for them, and re-layouts: 55.4 us -> 2.38 us
  blocking collectives: 3.78 us -> 42.2 us
  Pallas kernels: 0 us -> 25.3 us
  starting transfers between devices: 0.39 us -> 15.5 us
  between operations: 15.3 us -> 1.53 us
    unnamed x6 -> x0, waiting for transfers between devices: 231 us -> none
    psum x3 -> x0, waiting for transfers between devices: 115 us -> none  [per_device(): lax.psum(partial_value.astype(jnp.bfloat16), 'mp').astype(jnp.float32)]
    all_gather x1 -> x0, waiting for transfers between devices: 65.6 us -> none  [per_device(): gathered = lax.all_gather(nesterov, 'dp', axis=1, tiled=True)]
    dot_general x8 -> x0, matrix products: 61.6 us -> none  [the longest x3 34.8 us: quintic(): jnp.einsum('lshg,lsgc->lshc', poly_term, current, preferred_element_type=...]
    all_to_all x0 -> x1, blocking collectives: none -> 42.2 us  [block_plan(): lax.all_to_all(total.astype(jnp.float16), 'dp', 0, 0, axis_index_groups=g...]
    ppermute x0 -> x9, waiting for transfers between devices: none -> 32.2 us  [the longest x2 21.1 us: swap_y(): lax.ppermute(value, 'dp', [(dp_index(z, y, c), dp_index(z, 1 - y, c)) for...]
    reshape x2 -> x0, local copies, waits for them, and re-layouts: 25.5 us -> none  [the longest x1 18.5 us: per_device(): orthogonal.reshape(layers, slots * HEAD, columns)]
    pallas_call x0 -> x5, Pallas kernels: none -> 25.3 us  [the longest x1 11 us: block_plan(): pl.pallas_call(functools.partial(other_kernel, factor=factor), grid=(SIZE...]
  transfers between devices with their start and end apart: 5 -> 10, of which waited for: 5 -> 4; matrix products, arithmetic and copies ran while one was open for 0% -> 3% of each run, Pallas kernels for 0% -> 5%
where the time goes in v1:
time: 153 us; the launch traced here: 151 us
  waiting for transfers between devices  53 us (35%)
  blocking collectives  42.2 us (28%)
  Pallas kernels  25.3 us (17%)
  starting transfers between devices  15.5 us (10%)
  other arithmetic  11.5 us (8%)
  local copies, waits for them, and re-layouts  2.38 us (2%)
  between operations  1.53 us (1%)
    all_to_all x1, blocking collectives, block_plan(): lax.all_to_all(total.astype(jnp.float16), 'dp', 0, 0, axis_index_groups=g...  42.2 us
    ppermute x2, waiting for transfers between devices, swap_y(): lax.ppermute(value, 'dp', [(dp_index(z, y, c), dp_index(z, 1 - y, c)) for...  21.1 us
    all_to_all x1, waiting for transfers between devices, block_plan(): back = lax.all_to_all(sent, 'dp', 0, 0).astype(F32)  20.8 us
    ppermute x2, waiting for transfers between devices, swap_x(): return lax.ppermute(value, 'mp', [(0, 1), (1, 0)])  11.1 us
    pallas_call x1, Pallas kernels, block_plan(): pl.pallas_call(functools.partial(other_kernel, factor=factor), grid=(SIZE...  11 us
    pallas_call x1, Pallas kernels, block_plan(): pl.pallas_call(own_kernel, grid=(SIZE_Z,), in_specs=[whole(tok_dev, all_r...  8.23 us
    all_to_all x1, starting transfers between devices, block_plan(): back = lax.all_to_all(sent, 'dp', 0, 0).astype(F32)  6.74 us
    ppermute x5, starting transfers between devices, swap_core(): lax.ppermute(value, 'dp', [(dp_index(z, y, c), dp_index(z, y, 1 - c)) for...  4.06 us
  transfers between devices with their start and end apart: 10, of which 4 were waited for; matrix products, arithmetic and copies ran while one was open for 3% of the time, Pallas kernels for 5%

profile of v1, /device:TPU:1, one launch (start us, length us, event | category | flops | bytes accessed | tf_op | source)
XLA Modules:
  0.0 151.5 jit_solution(13901665549164905731)
XLA Ops:
  0.6 0.0 copy-start
  0.7 1.4 multiply_convert_fusion.mixed_in
  2.7 1.2 multiply_bitcast_fusion
  3.9 0.1 pad.4.clone
  4.0 0.3 maximum_maximum_fusion
  4.3 1.2 dynamic-slice_bitcast_fusion.1
  5.5 0.1 collective-permute-start.7
  5.6 0.0 copy-done
  5.6 0.1 dynamic-slice_bitcast_fusion.ctx0
  5.7 0.5 collective-permute-start.6
  6.2 2.3 %collective-permute-start.4 = (bf16[800,384]{1,0:T(8,128)(2,1)}, bf16[800,384]{1,0:T(8,128)(2,1)}, u32[]{:S(2)}, u32[]{:S(2)}) collective-permute-start(bf16[800,384]{1,0:T(8,128)(2,1)} %get-tuple-element.13), channel_id=1, source_target_pairs={{0,4},{2,6},{4,0},{6,2},{8,12},{10,14},{12,8},{14,10},{16,20},{18,... | collective-permute-start | bytes 1843208 | tf_op jit(solution)/shard_map/ppermute | solution.py:131
  8.5 0.8 dynamic-slice_bitcast_fusion.3
  9.3 0.0 collective-permute-start
  9.4 2.7 %fusion.3.perm = bf16[1920,1024]{1,0:T(8,128)(2,1)} fusion(s32[1024]{0:T(1024)S(1)} %get-tuple-element.19, s32[1024]{0:T(1024)S(1)} %get-tuple-element.24, s32[]{:T(128)S(6)} %mul.64, s32[1024]{0:T(1024)S(1)} %get-tuple-element.18, s32[1024]{0:T(1024)S(1)} %get-tuple-element.25, s32[1024]{0:T(1024)S(1)} %get-tuple-element.22, s32[1024]{0:T(1024)S(1)} %get-tuple-element.23, ...), kind=kLoop, calls=%fused_computation.9 | loop fusion | flops 45219840 | bytes 3959812 | tf_op jit(solution)/shard_map/convert_element_type | solution.py:265
  12.1 21.1 %collective-permute-done.first0 = bf16[128,1920]{1,0:T(8,128)(2,1)} collective-permute-done((bf16[128,1920]{1,0:T(8,128)(2,1)}, bf16[128,1920]{1,0:T(8,128)(2,1)}, u32[]{:S(2)}, u32[]{:S(2)}) %collective-permute-start) | collective-permute-done | bytes 491552 | tf_op jit(solution)/shard_map/ppermute | solution.py:131
  33.2 1.1 collective-permute-start.1
  34.3 0.0 collective-permute-done.4.ext0
  34.3 1.6 %collective-permute-start.5 = (bf16[800,384]{1,0:T(8,128)(2,1)}, bf16[800,384]{1,0:T(8,128)(2,1)S(1)}, u32[]{:S(2)}, u32[]{:S(2)}) collective-permute-start(bf16[800,384]{1,0:T(8,128)(2,1)} %collective-permute-done.4.ext0), channel_id=1, source_target_pairs={{0,2},{2,0},{4,6},{6,4},{8,10},{10,8},{12,14},{14,12},{16,18},{18,... | collective-permute-start | bytes 1843208 | tf_op jit(solution)/shard_map/ppermute | solution.py:127
  35.9 0.6 select_convert_fusion.hot
  36.5 0.1 collective-permute-start.2
  36.5 8.6 %collective-permute-done.1.second0 = bf16[128,1920]{1,0:T(8,128)(2,1)S(1)} collective-permute-done((bf16[128,1920]{1,0:T(8,128)(2,1)}, bf16[128,1920]{1,0:T(8,128)(2,1)S(1)}, u32[]{:S(2)}, u32[]{:S(2)}) %collective-permute-start.1) | collective-permute-done | bytes 491552 | tf_op jit(solution)/shard_map/ppermute | solution.py:135
  45.2 1.9 %collective-permute-start.3 = (bf16[128,1920]{1,0:T(8,128)(2,1)S(1)}, bf16[128,1920]{1,0:T(8,128)(2,1)S(1)}, u32[]{:S(2)}, u32[]{:S(2)}) collective-permute-start(bf16[128,1920]{1,0:T(8,128)(2,1)S(1)} %collective-permute-done.1.second0), channel_id=1, source_target_pairs={{0,2},{2,0},{4,6},{6,4},{8,10},{10,8},{12,14},{14,12},{16,18},{18,... | collective-permute-start | bytes 1474568 | tf_op jit(solution)/shard_map/ppermute | solution.py:127
  47.0 0.0 collective-permute-done.7.ext1
  47.1 0.0 collective-permute-done.6.ctx1
  47.1 8.2 %shard_map.68.partial = f32[4,800,256]{2,1,0:T(8,128)} custom-call(bf16[256,1920]{1,0:T(8,128)(2,1)S(1)} %dynamic-slice_bitcast_fusion.ctx0, bf16[256,1920]{1,0:T(8,128)(2,1)} %collective-permute-done.6.ctx1, bf16[800,384]{1,0:T(8,128)(2,1)} %get-tuple-element.12.ext0, bf16[800,384]{1,0:T(8,128)(2,1)} %collective-permute-done.7.ext1, ...), custom_call_target="tpu_custom_call" | custom-call | flops 6000000000 | bytes 10000000 | tf_op jit(solution)/shard_map/pallas_call | solution.py:283
  55.3 0.0 collective-permute-done.2.first1
  55.3 0.0 collective-permute-done.5.ext1
  55.3 0.0 collective-permute-done.3.second1
  55.3 11.0 %shard_map.69 = f32[4,800,256]{2,1,0:T(8,128)} custom-call(s32[1]{0:T(128)} %bitcast.side, bf16[128,1920]{1,0:T(8,128)(2,1)} %collective-permute-done.first0, bf16[128,1920]{1,0:T(8,128)(2,1)S(1)} %collective-permute-done.1.second0, bf16[128,1920]{1,0:T(8,128)(2,1)S(1)} %collective-permute-done.2.first1, ...), custom_call_target="tpu_custom_call" | custom-call | flops 6000000000 | bytes 10000000 | tf_op jit(solution)/shard_map/pallas_call | solution.py:294
  66.3 2.2 %convert_element_type.37 = f16[4,800,256]{2,1,0:T(8,128)(2,1)S(1)} convert(f32[4,800,256]{2,1,0:T(8,128)} %shard_map.69) | non-fusion elementwise | flops 819200 | bytes 4915200 | tf_op jit(solution)/shard_map/convert_element_type | solution.py:308
  68.4 42.2 %all_to_all.10 = f16[4,800,256]{2,1,0:T(8,128)(2,1)S(1)} all-to-all(f16[4,800,256]{2,1,0:T(8,128)(2,1)S(1)} %convert_element_type.37), channel_id=1, replica_groups={{0,8,16,24},{2,10,18,26},{4,12,20,28},{6,14,22,30},{1,9,17,25},{3,11,19..., dimensions={0} | all-to-all | bytes 3276800 | tf_op jit(solution)/shard_map/all_to_all | solution.py:308
  110.6 0.2 convert_reduce_fusion.mixed
  110.9 0.5 shard_map.70
  111.3 1.3 collective-permute-start.8
  112.6 0.1 convert_element_type.39
  112.7 0.1 copy.12
  112.7 2.5 %collective-permute-done.8.far = f32[2,128,128]{2,1,0:T(8,128)S(1)} collective-permute-done((f32[2,128,128]{2,1,0:T(8,128)S(1)}, f32[2,128,128]{2,1,0:T(8,128)S(1)}, u32[]{:S(2)}, u32[]{:S(2)}) %collective-permute-start.8) | collective-permute-done | bytes 131104 | tf_op jit(solution)/shard_map/ppermute | solution.py:135
  115.2 3.9 %shard_map.71 = f32[256,800]{1,0:T(8,128)S(1)} custom-call(f32[2,128,128]{2,1,0:T(8,128)S(1)} %get-tuple-element.8.near, f32[2,128,128]{2,1,0:T(8,128)S(1)} %collective-permute-done.8.far, bf16[800,256]{1,0:T(8,128)(2,1)S(1)} %get-tuple-element.9.nesterov), custom_call_target="tpu_custom_call" | custom-call | tf_op jit(solution)/shard_map/pallas_call | solution.py:320
  119.1 0.1 convert_element_type.40
  119.2 0.1 copy.11
  119.3 1.2 pad_maximum_fusion
  120.5 6.7 %all-to-all-start.1 = ((f16[16,2,16,800]{3,2,1,0:T(8,128)(2,1)}), f16[16,2,16,800]{3,2,1,0:T(8,128)(2,1)}, u32[]{:S(2)}, u32[]{:S(2)}) async-start(f16[16,2,16,800]{3,2,1,0:T(8,128)(2,1)} %pad_maximum_fusion), calls=%async_computation.1 | async-start | bytes 1835008 | tf_op jit(solution)/shard_map/all_to_all | solution.py:331
  127.2 0.2 fusion.8.order
  127.4 20.8 %all-to-all-done.1 = f16[16,2,16,800]{3,2,1,0:T(8,128)(2,1)} async-done(((f16[16,2,16,800]{3,2,1,0:T(8,128)(2,1)}), f16[16,2,16,800]{3,2,1,0:T(8,128)(2,1)}, u32[]{:S(2)}, u32[]{:S(2)}) %all-to-all-start.1) | async-done | bytes 819232 | tf_op jit(solution)/shard_map/all_to_all | solution.py:331
  148.2 1.4 convert.1.back
  149.7 0.0 copy-done.1
  149.7 0.0 copy-done.2
  149.7 1.8 %shard_map.72 = (f32[2,800,120]{2,1,0:T(8,128)}, f32[2,800,120]{2,1,0:T(8,128)}) custom-call(f32[4,2,2,2,16,800]{5,4,3,2,1,0:T(8,128)S(1)} %convert.1.back, bf16[128,128]{1,0:T(8,128)(2,1)S(1)} %fusion.8.order, f32[2,800,120]{2,1,0:T(8,128)S(1)} %bitcast.32, bf16[2,800,120]{2,1,0:T(8,128)(2,1)S(1)} %multiply_convert_fusion.mixed_in, f32[2,800,120]{2,1,0:T(8,128)S(1)} %bitcast.33), custom_call_target="tpu_custom_call" | custom-call | tf_op jit(solution)/shard_map/pallas_call | solution.py:339
  (16 shorter events, 0.1 us)
Async XLA Ops:
  0.6 5.0 %copy-start = (bf16[2,256,1920]{2,1,0:T(8,128)(2,1)S(1)}, bf16[2,256,1920]{2,1,0:T(8,128)(2,1)}, u32[]{:S(2)}) copy-start(bf16[2,256,1920]{2,1,0:T(8,128)(2,1)} %param.5) | copy-start | bytes 5898244
  5.5 41.5 %collective-permute-start.7 = (bf16[800,384]{1,0:T(8,128)(2,1)}, bf16[800,384]{1,0:T(8,128)(2,1)}, u32[]{:S(2)}, u32[]{:S(2)}) collective-permute-start(bf16[800,384]{1,0:T(8,128)(2,1)} %get-tuple-element.12.ext0), channel_id=1, source_target_pairs={{0,2},{2,0},{4,6},{6,4},{8,10},{10,8},{12,14},{14,12},{16,18},{18,... | collective-permute-start | bytes 1843208 | tf_op jit(solution)/shard_map/ppermute | solution.py:127
  5.7 41.4 %collective-permute-start.6 = (bf16[256,1920]{1,0:T(8,128)(2,1)S(1)}, bf16[256,1920]{1,0:T(8,128)(2,1)}, u32[]{:S(2)}, u32[]{:S(2)}) collective-permute-start(bf16[256,1920]{1,0:T(8,128)(2,1)S(1)} %dynamic-slice_bitcast_fusion.ctx0), channel_id=1, source_target_pairs={{0,2},{2,0},{4,6},{6,4},{8,10},{10,8},{12,14},{14,12},{16,18},{18,... | collective-permute-start | bytes 2949128 | tf_op jit(solution)/shard_map/ppermute | solution.py:127
  6.2 28.1 %collective-permute-start.4 = (bf16[800,384]{1,0:T(8,128)(2,1)}, bf16[800,384]{1,0:T(8,128)(2,1)}, u32[]{:S(2)}, u32[]{:S(2)}) collective-permute-start(bf16[800,384]{1,0:T(8,128)(2,1)} %get-tuple-element.13), channel_id=1, source_target_pairs={{0,4},{2,6},{4,0},{6,2},{8,12},{10,14},{12,8},{14,10},{16,20},{18,... | collective-permute-start | bytes 1843208 | tf_op jit(solution)/shard_map/ppermute | solution.py:131
  9.3 23.9 %collective-permute-start = (bf16[128,1920]{1,0:T(8,128)(2,1)}, bf16[128,1920]{1,0:T(8,128)(2,1)}, u32[]{:S(2)}, u32[]{:S(2)}) collective-permute-start(bf16[128,1920]{1,0:T(8,128)(2,1)} %dynamic-slice_bitcast_fusion.3), channel_id=1, source_target_pairs={{0,4},{2,6},{4,0},{6,2},{8,12},{10,14},{12,8},{14,10},{16,20},{18,... | collective-permute-start | bytes 1474568 | tf_op jit(solution)/shard_map/ppermute | solution.py:131
  33.2 12.0 %collective-permute-start.1 = (bf16[128,1920]{1,0:T(8,128)(2,1)}, bf16[128,1920]{1,0:T(8,128)(2,1)S(1)}, u32[]{:S(2)}, u32[]{:S(2)}) collective-permute-start(bf16[128,1920]{1,0:T(8,128)(2,1)} %collective-permute-done.first0), channel_id=1, source_target_pairs={{0,1},{1,0},{2,3},{3,2},{4,5},{5,4},{6,7},{7,6},{8,9},{9,8},{10,11... | collective-permute-start | bytes 1474568 | tf_op jit(solution)/shard_map/ppermute | solution.py:135
  34.3 21.0 %collective-permute-start.5 = (bf16[800,384]{1,0:T(8,128)(2,1)}, bf16[800,384]{1,0:T(8,128)(2,1)S(1)}, u32[]{:S(2)}, u32[]{:S(2)}) collective-permute-start(bf16[800,384]{1,0:T(8,128)(2,1)} %collective-permute-done.4.ext0), channel_id=1, source_target_pairs={{0,2},{2,0},{4,6},{6,4},{8,10},{10,8},{12,14},{14,12},{16,18},{18,... | collective-permute-start | bytes 1843208 | tf_op jit(solution)/shard_map/ppermute | solution.py:127
  36.5 18.8 %collective-permute-start.2 = (bf16[128,1920]{1,0:T(8,128)(2,1)}, bf16[128,1920]{1,0:T(8,128)(2,1)S(1)}, u32[]{:S(2)}, u32[]{:S(2)}) collective-permute-start(bf16[128,1920]{1,0:T(8,128)(2,1)} %collective-permute-done.first0), channel_id=1, source_target_pairs={{0,2},{2,0},{4,6},{6,4},{8,10},{10,8},{12,14},{14,12},{16,18},{18,... | collective-permute-start | bytes 1474568 | tf_op jit(solution)/shard_map/ppermute | solution.py:127
  45.2 10.1 %collective-permute-start.3 = (bf16[128,1920]{1,0:T(8,128)(2,1)S(1)}, bf16[128,1920]{1,0:T(8,128)(2,1)S(1)}, u32[]{:S(2)}, u32[]{:S(2)}) collective-permute-start(bf16[128,1920]{1,0:T(8,128)(2,1)S(1)} %collective-permute-done.1.second0), channel_id=1, source_target_pairs={{0,2},{2,0},{4,6},{6,4},{8,10},{10,8},{12,14},{14,12},{16,18},{18,... | collective-permute-start | bytes 1474568 | tf_op jit(solution)/shard_map/ppermute | solution.py:127
  111.3 3.9 %collective-permute-start.8 = (f32[2,128,128]{2,1,0:T(8,128)S(1)}, f32[2,128,128]{2,1,0:T(8,128)S(1)}, u32[]{:S(2)}, u32[]{:S(2)}) collective-permute-start(f32[2,128,128]{2,1,0:T(8,128)S(1)} %get-tuple-element.8.near), channel_id=1, source_target_pairs={{0,1},{1,0},{2,3},{3,2},{4,5},{5,4},{6,7},{7,6},{8,9},{9,8},{10,11... | collective-permute-start | bytes 393224 | tf_op jit(solution)/shard_map/ppermute | solution.py:135
  120.5 29.2 %copy-start.1 = (f32[2,120,800]{1,2,0:T(8,128)S(1)}, f32[2,120,800]{1,2,0:T(8,128)}, u32[]{:S(2)}) copy-start(f32[2,120,800]{1,2,0:T(8,128)} %param.8) | copy-start | bytes 2304004
  120.5 27.7 %all-to-all-start.1 = ((f16[16,2,16,800]{3,2,1,0:T(8,128)(2,1)}), f16[16,2,16,800]{3,2,1,0:T(8,128)(2,1)}, u32[]{:S(2)}, u32[]{:S(2)}) async-start(f16[16,2,16,800]{3,2,1,0:T(8,128)(2,1)} %pad_maximum_fusion), calls=%async_computation.1 | async-start | bytes 1835008 | tf_op jit(solution)/shard_map/all_to_all | solution.py:331
  148.2 1.5 copy-start.2

commit v2 on v1

--- a/solution.py
+++ b/solution.py
@@ -143,27 +143,40 @@
     return lax.dot_general(left, right, (dims, ((), ())), preferred_element_type=F32)
 
 
-def own_kernel(ctx0, ctx1, ext0, ext1, perm, hot, out_ref):
-    total = None
-    for source, (ctx, ext) in enumerate(((ctx0, ext0), (ctx1, ext1))):
-        ordered = contract(ctx[...], perm[...], ((1,), (0,))).astype(BF16)
-        tokens = jnp.concatenate([ordered, hot[source]], axis=0)
-        term = contract(ext[...], tokens, ((1,), (0,)))
-        total = term if total is None else total + term
-    out_ref[0] = total
-
-
-def other_kernel(side, first0, second0, first1, second1, ext0, ext1, perm, hot, partial, out_ref, *, factor):
-    half = first0.shape[0]
-    near = pl.multiple_of(side[0] * half, half)
-    far = pl.multiple_of((1 - side[0]) * half, half)
-    total = partial[0]
-    for source, (first, second, ext) in enumerate(((first0, second0, ext0), (first1, second1, ext1))):
-        rows_near = contract(first[...], perm[...], ((1,), (0,))).astype(BF16)
-        rows_far = contract(second[...], perm[...], ((1,), (0,))).astype(BF16)
-        total += contract(ext[:, pl.ds(near, half)], rows_near, ((1,), (0,)))
-        total += contract(ext[:, pl.ds(far, half)], rows_far, ((1,), (0,)))
-        total += contract(ext[:, 2 * half :], hot[source], ((1,), (0,)))
+def ext_kernel(pick, cotangent, momentum, counts, out_ref):
+    tokens, rows = cotangent.shape[2], momentum.shape[2]
+    position = lax.broadcasted_iota(jnp.int32, (1, tokens), 1)
+    live = (position // TILE_TOK < counts[0]).astype(F32)
+    out_ref[:, :tokens] = (cotangent[0].astype(F32) * live).astype(BF16)
+    mixed_in = mixed_part(momentum[0])
+    pad = jnp.zeros((mixed_in.shape[0], HEAD - rows), BF16)
+    out_ref[:, tokens:] = jnp.concatenate([mixed_in, pad], axis=1)
+
+
+def mixed_part(momentum):
+    return (momentum * (2.0 * MIX)).astype(BF16)
+
+
+def slot_kernel(first, second, perm, out_ref):
+    tokens = jnp.concatenate([first[...], second[...]], axis=0)
+    out_ref[...] = contract(tokens, perm[...], ((1,), (0,))).astype(BF16)
+
+
+def chunk_kernel(table, ext0, ext1, ext2, ext3, own, near, far, hot, out_ref, *, factor):
+    tokens = own.shape[0] // 2
+    half = tokens // 2
+    low_first = table[SIZE_Z] == 0
+    total = contract(ext0[:, :tokens], own[:tokens], ((1,), (0,)))
+    total += contract(ext1[:, :tokens], own[tokens:], ((1,), (0,)))
+    for source, ext in enumerate((ext2, ext3)):
+        here = near[source * half : (source + 1) * half]
+        there = far[source * half : (source + 1) * half]
+        low = jnp.where(low_first, here, there)
+        high = jnp.where(low_first, there, here)
+        total += contract(ext[:, :tokens], jnp.concatenate([low, high], axis=0), ((1,), (0,)))
+    for source, (left, right) in enumerate(((ext0, ext1), (ext2, ext3))):
+        rows = jnp.concatenate([left[:, tokens:], right[:, tokens:]], axis=1)
+        total += contract(rows, hot[2 * source : 2 * source + 2].reshape(2 * HEAD, -1), ((1,), (0,)))
     out_ref[0] = total * factor
 
 
@@ -204,18 +217,19 @@
         out_ref[pl.ds(head * HEAD, HEAD), :] = contract(high, block, ((1,), (1,))) + contract(low, block, ((1,), (1,)))
 
 
-def final_kernel(back, order, momentum, mixed_in, weights, momentum_ref, weights_ref, *, update_scale):
+def final_kernel(mixed_back, ortho_back, order, momentum, weights, momentum_ref, weights_ref, *, update_scale):
     for layer in range(2):
-        pieces = [back[z, layer, c] for z in range(SIZE_Z) for c in range(SIZE_C)]
-        summed = jnp.concatenate([piece[0] for piece in pieces], axis=0)
-        ortho = jnp.concatenate([piece[1] for piece in pieces], axis=0).astype(BF16)
+        places = [(z, layer, c) for z in range(SIZE_Z) for c in range(SIZE_C)]
+        summed = jnp.concatenate([mixed_back[place] for place in places], axis=0)
+        ortho = jnp.concatenate([ortho_back[place] for place in places], axis=0).astype(BF16)
         high = summed.astype(BF16)
         low = (summed - high.astype(F32)).astype(BF16)
         rows = momentum.shape[2]
         mixed = contract(high, order[...], ((0,), (0,))) + contract(low, order[...], ((0,), (0,)))
         update = contract(ortho, order[...], ((0,), (0,)))
-        gradient = mixed[:, :rows] - 0.5 * mixed_in[layer].astype(F32)
-        momentum_ref[layer] = momentum_rate * momentum[layer] + gradient
+        old = momentum[layer]
+        gradient = mixed[:, :rows] - 0.5 * mixed_part(old).astype(F32)
+        momentum_ref[layer] = momentum_rate * old + gradient
         old = weights[layer]
         weights_ref[layer] = old - learn_rate * (weight_decay * old + update_scale * update[:, :rows])
 
@@ -235,28 +249,37 @@
     x = lax.axis_index("mp")
     factor = 1.0 / math.sqrt(tok_dev * lax.axis_size("dp"))
 
-    position = lax.broadcasted_iota(jnp.int32, (1, 1, tok_dev), 2)
-    live_mask = (position // TILE_TOK < tile_counts[0]).astype(cotangent.dtype)
-    masked = jnp.transpose(cotangent, (0, 2, 1)) * live_mask
+    half_send = lax.dynamic_slice(context, (1 - y, x * half, 0), (1, half, all_rows))[0]
+    first0 = swap_y(half_send)
+    ctx_keep = lax.dynamic_index_in_dim(context, y, 0, False)
+    ctx1 = swap_core(ctx_keep)
+
+    cotangent_t = jnp.transpose(cotangent, (0, 2, 1))
     momentum_t = jnp.transpose(momentum, (0, 2, 1))
     weights_t = jnp.transpose(weights, (0, 2, 1))
-    mixed_in = (momentum_t * (2.0 * MIX)).astype(BF16)
-    pad = HEAD - shard_rows
-    ext = jnp.concatenate([masked, mixed_in, jnp.zeros((layers, columns, pad), BF16)], axis=2)
-
-    ctx_keep = lax.dynamic_index_in_dim(context, y, 0, False)
-    ext_keep = lax.dynamic_index_in_dim(ext, y, 0, False)
-    ext_send = lax.dynamic_index_in_dim(ext, 1 - y, 0, False)
-    half_send = lax.dynamic_slice(context, (1 - y, x * half, 0), (1, half, all_rows))[0]
-
-    first0 = swap_y(half_send)
-    ctx1 = swap_core(ctx_keep)
+    wide = tok_dev + HEAD
+
+    def ext_of(layer):
+        return pl.pallas_call(
+            ext_kernel,
+            grid_spec=pltpu.PrefetchScalarGridSpec(
+                num_scalar_prefetch=1,
+                grid=(1,),
+                in_specs=[
+                    pl.BlockSpec((1, columns, tok_dev), lambda i, pick: (pick[0], 0, 0)),
+                    pl.BlockSpec((1, columns, shard_rows), lambda i, pick: (pick[0], 0, 0)),
+                    pl.BlockSpec(memory_space=pltpu.SMEM),
+                ],
+                out_specs=pl.BlockSpec((columns, wide), lambda i, pick: (0, 0)),
+            ),
+            out_shape=jax.ShapeDtypeStruct((columns, wide), BF16),
+            compiler_params=vmem_params(),
+            cost_estimate=pl.CostEstimate(flops=10**6, bytes_accessed=2 * 10**6, transcendentals=0),
+        )(layer.reshape(1), cotangent_t, momentum_t, tile_counts)
+
+    ext2 = swap_y(ext_of(1 - y))
+    ext_keep = ext_of(y)
     ext1 = swap_core(ext_keep)
-    ext2 = swap_y(ext_send)
-    second0 = swap_x(first0)
-    first1 = swap_core(first0)
-    second1 = swap_core(second0)
-    ext3 = swap_core(ext2)
 
     slot_cols = SIZE_Z * 2 * HEAD
     row = lax.broadcasted_iota(jnp.int32, (all_rows, slot_cols), 0)
@@ -274,39 +297,70 @@
     hit = (from_row == col % HEAD * HEADS_WIN + head) & (head < HEADS_WIN) & (local < shard_rows)
     hot = jnp.where(hit, 0.5 / factor, 0.0).astype(BF16)
 
-    whole = lambda *shape: pl.BlockSpec(shape, lambda j: (0,) * len(shape))
     lanes = 2 * HEAD
-    perm_spec = pl.BlockSpec((all_rows, lanes), lambda j: (0, j))
-    chunk_spec = pl.BlockSpec((1, columns, lanes), lambda j: (j, 0, 0))
-    chunks = jax.ShapeDtypeStruct((SIZE_Z, columns, lanes), F32)
-    wide = tok_dev + HEAD
-    partial = pl.pallas_call(
-        own_kernel,
-        grid=(SIZE_Z,),
-        in_specs=[whole(tok_dev, all_rows)] * 2
-        + [whole(columns, wide)] * 2
-        + [perm_spec, pl.BlockSpec((2, HEAD, lanes), lambda j: (0, 0, j))],
-        out_specs=chunk_spec,
-        out_shape=chunks,
-        compiler_params=vmem_params(),
-        cost_estimate=pl.CostEstimate(flops=6 * 10**9, bytes_accessed=10**7, transcendentals=0),
-    )(ctx_keep, ctx1, ext_keep, ext1, perm, hot)
-    total = pl.pallas_call(
-        functools.partial(other_kernel, factor=factor),
-        grid=(SIZE_Z,),
-        in_specs=[pl.BlockSpec(memory_space=pltpu.SMEM)]
-        + [whole(half, all_rows)] * 4
-        + [whole(columns, wide)] * 2
-        + [perm_spec, pl.BlockSpec((2, HEAD, lanes), lambda j: (1, 0, j)), chunk_spec],
-        out_specs=chunk_spec,
-        out_shape=chunks,
-        compiler_params=vmem_params(),
-        cost_estimate=pl.CostEstimate(flops=6 * 10**9, bytes_accessed=10**7, transcendentals=0),
-    )(x.reshape(1), first0, second0, first1, second1, ext2, ext3, perm, hot, partial)
-
-    groups = [[dp_index(k, b, a) for k in range(SIZE_Z)] for b in range(SIZE_Y) for a in range(SIZE_C)]
-    arrived = lax.all_to_all(total.astype(jnp.float16), "dp", 0, 0, axis_index_groups=groups)
-    mixed = jnp.sum(arrived.astype(F32), axis=0)
+
+    def slots_of(first, second):
+        tokens = first.shape[0]
+        return pl.pallas_call(
+            slot_kernel,
+            grid=(SIZE_Z,),
+            in_specs=[pl.BlockSpec((tokens, all_rows), lambda j: (0, 0))] * 2
+            + [pl.BlockSpec((all_rows, lanes), lambda j: (0, j))],
+            out_specs=pl.BlockSpec((2 * tokens, lanes), lambda j: (0, j)),
+            out_shape=jax.ShapeDtypeStruct((2 * tokens, slot_cols), BF16),
+            compiler_params=vmem_params(),
+            cost_estimate=pl.CostEstimate(
+                flops=4 * tokens * all_rows * slot_cols, bytes_accessed=6 * 10**6, transcendentals=0
+            ),
+        )(first, second, perm)
+
+    own = slots_of(ctx_keep, ctx1)
+    first0 = after(first0, own)
+    second0 = swap_x(first0)
+    first1 = swap_core(first0)
+    near = slots_of(first0, first1)
+    second0 = after(second0, near)
+    second1 = swap_core(second0)
+    ext3 = swap_core(ext2)
+    far = slots_of(second0, second1)
+
+    orders = jnp.array([[3, 2, 1, 0], [2, 0, 3, 1], [3, 1, 0, 2], [0, 1, 2, 3]], jnp.int32)
+    table = jnp.concatenate([lax.dynamic_index_in_dim(orders, z, 0, False), x.reshape(1)])
+
+    def chunks_of(first):
+        full = lambda rows, cols: pl.BlockSpec((rows, cols), lambda j, table: (0, 0))
+        part = lambda rows: pl.BlockSpec((rows, lanes), lambda j, table: (0, table[first + j]))
+        return pl.pallas_call(
+            functools.partial(chunk_kernel, factor=factor),
+            grid_spec=pltpu.PrefetchScalarGridSpec(
+                num_scalar_prefetch=1,
+                grid=(2,),
+                in_specs=[full(columns, wide)] * 4
+                + [part(2 * tok_dev), part(tok_dev), part(tok_dev)]
+                + [pl.BlockSpec((4, HEAD, lanes), lambda j, table: (0, 0, table[first + j]))],
+                out_specs=pl.BlockSpec((1, columns, lanes), lambda j, table: (j, 0, 0)),
+            ),
+            out_shape=jax.ShapeDtypeStruct((2, columns, lanes), F32),
+            compiler_params=vmem_params(),
+            cost_estimate=pl.CostEstimate(
+                flops=4 * columns * (4 * tok_dev + 4 * HEAD) * lanes, bytes_accessed=5 * 10**6, transcendentals=0
+            ),
+        )(table, ext_keep, ext1, ext2, ext3, own, near, far, hot)
+
+    def along_z(value, pairs):
+        pairs = [(dp_index(p, b, a), dp_index(q, b, a)) for p, q in pairs for b in range(SIZE_Y) for a in range(SIZE_C)]
+        return lax.ppermute(value.astype(jnp.float16), "dp", pairs)
+
+    early = chunks_of(0)
+    up = along_z(early[0], [(0, 1), (1, 2), (2, 3)])
+    down = along_z(jnp.where(z == 3, early[0], early[1]), [(3, 2), (2, 1), (1, 0)])
+    jump = along_z(early[1], [(0, 2), (3, 1)])
+    late = chunks_of(2)
+    zero = jnp.zeros((), F32)
+    merged = late[0] + jnp.where(z == 1, up.astype(F32), zero) + jnp.where(z == 2, down.astype(F32), zero)
+    last = along_z(merged, [(0, 1), (1, 3), (3, 2), (2, 0)])
+    mixed = late[1] + jnp.where(z >= 2, up.astype(F32), zero) + jnp.where(z <= 1, down.astype(F32), zero)
+    mixed = mixed + jump.astype(F32) + last.astype(F32)
 
     nesterov, gram, turned = pl.pallas_call(
         gram_kernel,
@@ -323,13 +377,14 @@
         compiler_params=vmem_params(),
     )(gram, swap_x(gram), nesterov)
 
-    def by_owner(value):
+    def returned(value):
         value = value.astype(jnp.float16).reshape(2, lax.axis_size("dp"), depth, columns)
-        return jnp.transpose(value, (1, 0, 2, 3)).reshape(-1, 1, 2 * depth, columns)
-
-    sent = jnp.concatenate([by_owner(turned), by_owner(ortho)], axis=1)
-    back = lax.all_to_all(sent, "dp", 0, 0).astype(F32)
-    back = back.reshape(SIZE_Z, SIZE_Y, SIZE_C, 2, 2 * depth, columns)
+        value = jnp.transpose(value, (1, 0, 2, 3)).reshape(-1, 2 * depth, columns)
+        value = lax.all_to_all(value, "dp", 0, 0).astype(F32)
+        return value.reshape(SIZE_Z, SIZE_Y, SIZE_C, 2 * depth, columns)
+
+    mixed_back = returned(turned)
+    ortho_back = returned(ortho)
 
     count = SIZE_Z * SIZE_C * 2 * depth
     row = lax.broadcasted_iota(jnp.int32, (count, HEAD), 0)
@@ -340,7 +395,7 @@
         functools.partial(final_kernel, update_scale=0.2 * math.sqrt(max(HEAD, COLS))),
         out_shape=(out, out),
         compiler_params=vmem_params(),
-    )(back, order, momentum_t, mixed_in, weights_t)
+    )(mixed_back, ortho_back, order, momentum_t, weights_t)
     return jnp.transpose(moment_new, (0, 2, 1)), jnp.transpose(new_weights, (0, 2, 1))
 
 

time: 153 us -> 130 us (0.85)
  blocking collectives: 42.2 us -> 0 us
  local copies, waits for them, and re-layouts: 2.38 us -> 15.8 us
  starting transfers between devices: 15.5 us -> 26 us
  waiting for transfers between devices: 53 us -> 45.3 us
  Pallas kernels: 25.3 us -> 27.7 us
    all_to_all x1 -> x0, blocking collectives: 42.2 us -> none  [block_plan(): lax.all_to_all(total.astype(jnp.float16), 'dp', 0, 0, axis_index_groups=g...]
    ppermute x0 -> x4, waiting for transfers between devices: none -> 15.7 us  [along_z(): return lax.ppermute(value.astype(jnp.float16), 'dp', pairs)]
    ppermute x2, waiting for transfers between devices: 21.1 us -> 9.55 us  [swap_y(): lax.ppermute(value, 'dp', [(dp_index(z, y, c), dp_index(z, 1 - y, c)) for...]
    unnamed x6 -> x56, local copies, waits for them, and re-layouts: 0.02 us -> 11.5 us
    ppermute x0 -> x4, starting transfers between devices: none -> 10.6 us  [along_z(): return lax.ppermute(value.astype(jnp.float16), 'dp', pairs)]
    ppermute x2, waiting for transfers between devices: 11.1 us -> 3.6 us  [swap_x(): return lax.ppermute(value, 'mp', [(0, 1), (1, 0)])]
    all_to_all x1 -> x2, waiting for transfers between devices: 20.8 us -> 15.3 us  [returned(): value = lax.all_to_all(value, 'dp', 0, 0).astype(F32)]
    ppermute x5, starting transfers between devices: 4.06 us -> 1.22 us  [swap_core(): lax.ppermute(value, 'dp', [(dp_index(z, y, c), dp_index(z, y, 1 - c)) for...]
  transfers between devices with their start and end apart: 10 -> 15, of which waited for: 4 -> 7; matrix products, arithmetic and copies ran while one was open for 3% -> 7% of each run, Pallas kernels for 5% -> 16%
where the time goes in v2:
time: 130 us; the launch traced here: 129 us
  waiting for transfers between devices  45.3 us (35%)
  Pallas kernels  27.7 us (21%)
  starting transfers between devices  26 us (20%)
  local copies, waits for them, and re-layouts  15.8 us (12%)
  other arithmetic  12.3 us (9%)
  between operations  1.83 us (1%)
    ppermute x4, waiting for transfers between devices, along_z(): return lax.ppermute(value.astype(jnp.float16), 'dp', pairs)  15.7 us
    all_to_all x2, waiting for transfers between devices, returned(): value = lax.all_to_all(value, 'dp', 0, 0).astype(F32)  15.3 us
    unnamed x56, local copies, waits for them, and re-layouts  11.5 us
    pallas_call x3, Pallas kernels, slots_of(): pl.pallas_call(slot_kernel, grid=(SIZE_Z,), in_specs=[pl.BlockSpec((token...  11 us
    ppermute x4, starting transfers between devices, along_z(): return lax.ppermute(value.astype(jnp.float16), 'dp', pairs)  10.6 us
    ppermute x2, waiting for transfers between devices, swap_y(): lax.ppermute(value, 'dp', [(dp_index(z, y, c), dp_index(z, 1 - y, c)) for...  9.55 us
    pallas_call x2, Pallas kernels, chunks_of(): pl.pallas_call(functools.partial(chunk_kernel, factor=factor), grid_spec=...  9.45 us
    all_to_all x2, starting transfers between devices, returned(): value = lax.all_to_all(value, 'dp', 0, 0).astype(F32)  8.71 us
  transfers between devices with their start and end apart: 15, of which 7 were waited for; matrix products, arithmetic and copies ran while one was open for 7% of the time, Pallas kernels for 16%

profile of v2, /device:TPU:1, one launch (start us, length us, event | category | flops | bytes accessed | tf_op | source)
XLA Modules:
  0.0 128.8 jit_solution(13015145494555036224)
XLA Ops:
  0.7 1.5 %copy-done = bf16[2,256,1920]{2,1,0:T(8,128)(2,1)S(1)} copy-done((bf16[2,256,1920]{2,1,0:T(8,128)(2,1)S(1)}, bf16[2,256,1920]{2,1,0:T(8,128)(2,1)}, u32[]{:S(2)}) %copy-start) | copy-done | bytes 1966104
  2.2 1.1 dynamic-slice_bitcast_fusion.first
  3.3 0.8 dynamic-slice_bitcast_fusion.1
  4.1 2.7 %collective-permute-start.4 = (bf16[128,1920]{1,0:T(8,128)(2,1)}, bf16[128,1920]{1,0:T(8,128)(2,1)}, u32[]{:S(2)}, u32[]{:S(2)}) collective-permute-start(bf16[128,1920]{1,0:T(8,128)(2,1)} %dynamic-slice_bitcast_fusion.1), channel_id=1, source_target_pairs={{0,4},{2,6},{4,0},{6,2},{8,12},{10,14},{12,8},{14,10},{16,20},{18,... | collective-permute-start | bytes 1474568 | tf_op jit(solution)/shard_map/ppermute | solution.py:131
  7.5 1.1 copy-done.10
  8.8 0.9 shard_map.77.ext0
  9.8 0.3 collective-permute-start
  10.2 2.7 %fusion.3.perm = bf16[1920,1024]{1,0:T(8,128)(2,1)} fusion(s32[1024]{0:T(1024)S(1)} %get-tuple-element.24, s32[1024]{0:T(1024)S(1)} %get-tuple-element.28, s32[]{:T(128)S(6)} %mul.41, s32[1024]{0:T(1024)S(1)} %get-tuple-element.23, s32[1024]{0:T(1024)S(1)} %broadcast_add_fusion.1, s32[1024]{0:T(1024)S(1)} %iota_and_fusion.1, s32[1024]{0:T(1024)S(1)} %get-tuple-element.27, ...), kind=kLoop, calls=%fused_computation.9 | loop fusion | flops 45219840 | bytes 3959812 | tf_op jit(solution)/shard_map/convert_element_type | solution.py:288
  12.9 0.5 iota_compare_fusion
  13.4 5.3 %shard_map.79.own = bf16[512,1024]{1,0:T(8,128)(2,1)S(1)} custom-call(bf16[256,1920]{1,0:T(8,128)(2,1)} %dynamic-slice_bitcast_fusion.first, bf16[256,1920]{1,0:T(8,128)(2,1)} %collective-permute-done.3.second, bf16[1920,1024]{1,0:T(8,128)(2,1)} %fusion.3.perm), custom_call_target="tpu_custom_call" | custom-call | flops 2013265920 | bytes 6000000 | tf_op jit(solution)/shard_map/pallas_call | solution.py:304
  18.8 1.0 copy-done.6
  20.0 0.7 fusion.27
  20.7 1.5 %collective-permute-start.6 = (bf16[128,1920]{1,0:T(8,128)(2,1)}, bf16[128,1920]{1,0:T(8,128)(2,1)S(1)}, u32[]{:S(2)}, u32[]{:S(2)}) collective-permute-start(bf16[128,1920]{1,0:T(8,128)(2,1)} %collective-permute-done.4.first), channel_id=1, source_target_pairs={{0,1},{1,0},{2,3},{3,2},{4,5},{5,4},{6,7},{7,6},{8,9},{9,8},{10,11... | collective-permute-start | bytes 1474568 | tf_op jit(solution)/shard_map/ppermute | solution.py:135
  22.4 9.5 %collective-permute-done.1.ext2 = bf16[800,384]{1,0:T(8,128)(2,1)} collective-permute-done((bf16[800,384]{1,0:T(8,128)(2,1)S(1)}, bf16[800,384]{1,0:T(8,128)(2,1)}, u32[]{:S(2)}, u32[]{:S(2)}) %collective-permute-start.1) | collective-permute-done | bytes 614432 | tf_op jit(solution)/shard_map/ppermute | solution.py:131
  31.9 0.6 collective-permute-start.2
  32.5 2.1 %copy-done.1 = bf16[1920,1024]{1,0:T(8,128)(2,1)S(1)} copy-done((bf16[1920,1024]{1,0:T(8,128)(2,1)S(1)}, bf16[1920,1024]{1,0:T(8,128)(2,1)}, u32[]{:S(2)}) %copy-start.1) | copy-done | bytes 3932184
  34.6 3.3 %shard_map.80.near = bf16[256,1024]{1,0:T(8,128)(2,1)S(1)} custom-call(bf16[128,1920]{1,0:T(8,128)(2,1)} %collective-permute-done.4.first, bf16[128,1920]{1,0:T(8,128)(2,1)S(1)} %collective-permute-done.5.second, bf16[1920,1024]{1,0:T(8,128)(2,1)S(1)} %copy-done.1), custom_call_target="tpu_custom_call" | custom-call | flops 1006632960 | bytes 6000000 | tf_op jit(solution)/shard_map/pallas_call | solution.py:304
  38.1 0.6 select_convert_fusion.hot
  38.7 1.1 collective-permute-done.7.second
  39.8 2.4 %shard_map.81.far = bf16[256,1024]{1,0:T(8,128)(2,1)S(1)} custom-call(bf16[128,1920]{1,0:T(8,128)(2,1)S(1)} %collective-permute-done.6.first, bf16[128,1920]{1,0:T(8,128)(2,1)S(1)} %collective-permute-done.7.second, bf16[1920,1024]{1,0:T(8,128)(2,1)S(1)} %copy-done.1), custom_call_target="tpu_custom_call" | custom-call | flops 1006632960 | bytes 6000000 | tf_op jit(solution)/shard_map/pallas_call | solution.py:304
  42.3 4.7 %shard_map.83 = f32[2,800,256]{2,1,0:T(8,128)} custom-call(s32[5]{0:T(128)S(1)} %pad_add_fusion.table, bf16[800,384]{1,0:T(8,128)(2,1)} %shard_map.77.ext0, bf16[800,384]{1,0:T(8,128)(2,1)} %collective-permute-done.ext1, bf16[800,384]{1,0:T(8,128)(2,1)} %collective-permute-done.1.ext2, bf16[800,384]{1,0:T(8,128)(2,1)S(1)} %collective-permute-done.2.ext3, ...), custom_call_target="tpu_custom_call" | custom-call | flops 1258291200 | bytes 5000000 | tf_op jit(solution)/shard_map/pallas_call | solution.py:333
  47.1 2.5 %fusion.14 = (f16[800,256]{1,0:T(8,128)(2,1)}, f16[800,256]{1,0:T(8,128)(2,1)}, f16[800,256]{1,0:T(8,128)(2,1)}) fusion(f32[2,800,256]{2,1,0:T(8,128)} %shard_map.83, pred[]{:T(512)S(6)} %eq.40), kind=kLoop, calls=%fused_computation.42 | loop fusion | flops 819200 | bytes 2867201 | tf_op jit(solution)/shard_map/convert_element_type | solution.py:352
  49.6 4.2 %collective-permute-start.8 = (f16[800,256]{1,0:T(8,128)(2,1)}, f16[800,256]{1,0:T(8,128)(2,1)}, u32[]{:S(2)}, u32[]{:S(2)}) collective-permute-start(f16[800,256]{1,0:T(8,128)(2,1)} %get-tuple-element.18), channel_id=1, source_target_pairs={{0,8},{2,10},{4,12},{6,14},{8,16},{10,18},{12,20},{14,22},{16,24},... | collective-permute-start | bytes 1228808 | tf_op jit(solution)/shard_map/ppermute | solution.py:352
  53.8 1.3 collective-permute-start.9
  55.1 5.1 %collective-permute-start.10 = (f16[800,256]{1,0:T(8,128)(2,1)}, f16[800,256]{1,0:T(8,128)(2,1)}, u32[]{:S(2)}, u32[]{:S(2)}) collective-permute-start(f16[800,256]{1,0:T(8,128)(2,1)} %get-tuple-element.16), channel_id=1, source_target_pairs={{0,16},{2,18},{4,20},{6,22},{24,8},{26,10},{28,12},{30,14},{1,17},... | collective-permute-start | bytes 1228808 | tf_op jit(solution)/shard_map/ppermute | solution.py:352
  60.2 1.0 copy-done.5
  61.2 1.2 copy-done.8
  62.4 1.1 copy-done.13
  63.5 4.7 %shard_map.82 = f32[2,800,256]{2,1,0:T(8,128)} custom-call(s32[5]{0:T(128)S(1)} %pad_add_fusion.table, bf16[800,384]{1,0:T(8,128)(2,1)} %shard_map.77.ext0, bf16[800,384]{1,0:T(8,128)(2,1)} %collective-permute-done.ext1, bf16[800,384]{1,0:T(8,128)(2,1)} %collective-permute-done.1.ext2, bf16[800,384]{1,0:T(8,128)(2,1)S(1)} %copy-done.13, ...), custom_call_target="tpu_custom_call" | custom-call | flops 1258291200 | bytes 5000000 | tf_op jit(solution)/shard_map/pallas_call | solution.py:333
  68.2 1.6 %fusion.12 = f16[800,256]{1,0:T(8,128)(2,1)S(1)} fusion(f16[800,256]{1,0:T(8,128)(2,1)} %collective-permute-done.8, f16[800,256]{1,0:T(8,128)(2,1)} %collective-permute-done.9, f32[2,800,256]{2,1,0:T(8,128)} %shard_map.82, pred[]{:T(512)S(6)} %eq.42, pred[]{:T(512)S(6)} %eq.41), kind=kLoop, calls=%fused_computation.32 | loop fusion | flops 1433600 | bytes 2048002 | tf_op jit(solution)/shard_map/convert_element_type | solution.py:352
  69.9 1.0 collective-permute-done.10
  70.9 14.7 %collective-permute-done.11 = f16[800,256]{1,0:T(8,128)(2,1)S(1)} collective-permute-done((f16[800,256]{1,0:T(8,128)(2,1)S(1)}, f16[800,256]{1,0:T(8,128)(2,1)S(1)}, u32[]{:S(2)}, u32[]{:S(2)}) %collective-permute-start.11) | collective-permute-done | bytes 409632 | tf_op jit(solution)/shard_map/ppermute | solution.py:352
  85.6 1.8 %fusion.9.mixed = f32[800,256]{1,0:T(8,128)S(1)} fusion(f16[800,256]{1,0:T(8,128)(2,1)} %collective-permute-done.8, f16[800,256]{1,0:T(8,128)(2,1)} %collective-permute-done.9, f32[2,800,256]{2,1,0:T(8,128)} %shard_map.82, f16[800,256]{1,0:T(8,128)(2,1)S(1)} %collective-permute-done.11, f16[800,256]{1,0:T(8,128)(2,1)} %collective-permute-done.10, ...), kind=kLoop, calls=%fused_computation.29 | loop fusion | flops 2048000 | bytes 3276802 | tf_op jit(solution)/shard_map/add | solution.py:363
  87.4 0.5 shard_map.84
  87.9 0.8 copy.13
  88.7 4.4 %all-to-all-start = ((f16[16,16,800]{2,1,0:T(8,128)(2,1)}), f16[16,16,800]{2,1,0:T(8,128)(2,1)S(1)}, u32[]{:S(2)}, u32[]{:S(2)}) async-start(f16[16,16,800]{2,1,0:T(8,128)(2,1)} %bitcast.43), calls=%async_computation | async-start | bytes 917504 | tf_op jit(solution)/shard_map/all_to_all | solution.py:383
  93.1 1.2 collective-permute-start.12
  94.3 3.6 %collective-permute-done.12.far = f32[2,128,128]{2,1,0:T(8,128)S(1)} collective-permute-done((f32[2,128,128]{2,1,0:T(8,128)S(1)}, f32[2,128,128]{2,1,0:T(8,128)S(1)}, u32[]{:S(2)}, u32[]{:S(2)}) %collective-permute-start.12) | collective-permute-done | bytes 131104 | tf_op jit(solution)/shard_map/ppermute | solution.py:135
  97.9 3.9 %shard_map.85 = f32[256,800]{1,0:T(8,128)S(1)} custom-call(f32[2,128,128]{2,1,0:T(8,128)S(1)} %get-tuple-element.12.near, f32[2,128,128]{2,1,0:T(8,128)S(1)} %collective-permute-done.12.far, bf16[800,256]{1,0:T(8,128)(2,1)S(1)} %get-tuple-element.13.nesterov), custom_call_target="tpu_custom_call" | custom-call | tf_op jit(solution)/shard_map/pallas_call | solution.py:374
  101.9 0.8 copy.12
  102.8 3.4 %all-to-all-done = f16[16,16,800]{2,1,0:T(8,128)(2,1)S(1)} async-done(((f16[16,16,800]{2,1,0:T(8,128)(2,1)}), f16[16,16,800]{2,1,0:T(8,128)(2,1)S(1)}, u32[]{:S(2)}, u32[]{:S(2)}) %all-to-all-start) | async-done | bytes 409632 | tf_op jit(solution)/shard_map/all_to_all | solution.py:383
  106.1 4.4 %all-to-all-start.1 = ((f16[16,16,800]{2,1,0:T(8,128)(2,1)}), f16[16,16,800]{2,1,0:T(8,128)(2,1)}, u32[]{:S(2)}, u32[]{:S(2)}) async-start(f16[16,16,800]{2,1,0:T(8,128)(2,1)} %bitcast.42), calls=%async_computation.1 | async-start | bytes 917504 | tf_op jit(solution)/shard_map/all_to_all | solution.py:383
  110.7 1.0 convert.2.mixed_back
  111.7 11.9 %all-to-all-done.1 = f16[16,16,800]{2,1,0:T(8,128)(2,1)} async-done(((f16[16,16,800]{2,1,0:T(8,128)(2,1)}), f16[16,16,800]{2,1,0:T(8,128)(2,1)}, u32[]{:S(2)}, u32[]{:S(2)}) %all-to-all-start.1) | async-done | bytes 409632 | tf_op jit(solution)/shard_map/all_to_all | solution.py:383
  123.6 1.1 convert.3.ortho_back
  124.8 1.2 copy-done.9
  125.9 1.1 copy-done.14
  127.1 1.8 %shard_map.86 = (f32[2,800,120]{2,1,0:T(8,128)}, f32[2,800,120]{2,1,0:T(8,128)}) custom-call(f32[4,2,2,16,800]{4,3,2,1,0:T(8,128)S(1)} %copy-done.9, f32[4,2,2,16,800]{4,3,2,1,0:T(8,128)S(1)} %convert.3.ortho_back, bf16[128,128]{1,0:T(8,128)(2,1)S(1)} %fusion.18.order, f32[2,800,120]{2,1,0:T(8,128)S(1)} %bitcast.46, f32[2,800,120]{2,1,0:T(8,128)S(1)} %bitcast.49), custom_call_target="tpu_custom_call" | custom-call | tf_op jit(solution)/shard_map/pallas_call | solution.py:394
  (77 shorter events, 1.1 us)
Async XLA Ops:
  0.6 1.6 %copy-start = (bf16[2,256,1920]{2,1,0:T(8,128)(2,1)S(1)}, bf16[2,256,1920]{2,1,0:T(8,128)(2,1)}, u32[]{:S(2)}) copy-start(bf16[2,256,1920]{2,1,0:T(8,128)(2,1)} %param.6) | copy-start | bytes 5898244
  0.6 6.8 %copy-start.2 = (f32[2,120,800]{1,2,0:T(8,128)S(1)}, f32[2,120,800]{1,2,0:T(8,128)}, u32[]{:S(2)}) copy-start(f32[2,120,800]{1,2,0:T(8,128)} %param.9) | copy-start | bytes 2304004
  3.3 10.2 %collective-permute-start.3 = (bf16[256,1920]{1,0:T(8,128)(2,1)}, bf16[256,1920]{1,0:T(8,128)(2,1)}, u32[]{:S(2)}, u32[]{:S(2)}) collective-permute-start(bf16[256,1920]{1,0:T(8,128)(2,1)} %dynamic-slice_bitcast_fusion.first), channel_id=1, source_target_pairs={{0,2},{2,0},{4,6},{6,4},{8,10},{10,8},{12,14},{14,12},{16,18},{18,... | collective-permute-start | bytes 2949128 | tf_op jit(solution)/shard_map/ppermute | solution.py:127
  3.3 5.5 %copy-start.11 = (bf16[2,256,800]{1,2,0:T(8,128)(2,1)S(1)}, bf16[2,256,800]{1,2,0:T(8,128)(2,1)}, u32[]{:S(2)}) copy-start(bf16[2,256,800]{1,2,0:T(8,128)(2,1)} %param.7) | copy-start | bytes 2457604
  4.1 15.7 %collective-permute-start.4 = (bf16[128,1920]{1,0:T(8,128)(2,1)}, bf16[128,1920]{1,0:T(8,128)(2,1)}, u32[]{:S(2)}, u32[]{:S(2)}) collective-permute-start(bf16[128,1920]{1,0:T(8,128)(2,1)} %dynamic-slice_bitcast_fusion.1), channel_id=1, source_target_pairs={{0,4},{2,6},{4,0},{6,2},{8,12},{10,14},{12,8},{14,10},{16,20},{18,... | collective-permute-start | bytes 1474568 | tf_op jit(solution)/shard_map/ppermute | solution.py:131
  7.5 1.1 copy-start.10
  8.8 23.1 %collective-permute-start.1 = (bf16[800,384]{1,0:T(8,128)(2,1)S(1)}, bf16[800,384]{1,0:T(8,128)(2,1)}, u32[]{:S(2)}, u32[]{:S(2)}) collective-permute-start(bf16[800,384]{1,0:T(8,128)(2,1)S(1)} %shard_map.78), channel_id=1, source_target_pairs={{0,4},{2,6},{4,0},{6,2},{8,12},{10,14},{12,8},{14,10},{16,20},{18,... | collective-permute-start | bytes 1843208 | tf_op jit(solution)/shard_map/ppermute | solution.py:131
  9.8 32.5 %collective-permute-start = (bf16[800,384]{1,0:T(8,128)(2,1)}, bf16[800,384]{1,0:T(8,128)(2,1)}, u32[]{:S(2)}, u32[]{:S(2)}) collective-permute-start(bf16[800,384]{1,0:T(8,128)(2,1)} %shard_map.77.ext0), channel_id=1, source_target_pairs={{0,2},{2,0},{4,6},{6,4},{8,10},{10,8},{12,14},{14,12},{16,18},{18,... | collective-permute-start | bytes 1843208 | tf_op jit(solution)/shard_map/ppermute | solution.py:127
  10.1 8.7 %copy-start.15 = (s32[1024]{0:T(1024)}, s32[1024]{0:T(1024)S(1)}, u32[]{:S(2)}) copy-start(s32[1024]{0:T(1024)S(1)} %get-tuple-element.28) | copy-start | bytes 12292
  10.1 8.7 %copy-start.21 = (pred[1024]{0:T(1024)(128)(4,1)}, pred[1024]{0:T(1024)(128)(4,1)S(1)}, u32[]{:S(2)}) copy-start(pred[1024]{0:T(1024)(128)(4,1)S(1)} %get-tuple-element.25) | copy-start | bytes 3076
  10.1 8.7 %copy-start.23 = (pred[1024]{0:T(1024)(128)(4,1)}, pred[1024]{0:T(1024)(128)(4,1)S(1)}, u32[]{:S(2)}) copy-start(pred[1024]{0:T(1024)(128)(4,1)S(1)} %get-tuple-element.26) | copy-start | bytes 3076
  10.1 8.6 %copy-start.17 = (s32[1024]{0:T(1024)}, s32[1024]{0:T(1024)S(1)}, u32[]{:S(2)}) copy-start(s32[1024]{0:T(1024)S(1)} %broadcast_add_fusion.1) | copy-start | bytes 12292
  10.2 8.6 %copy-start.19 = (s32[1024]{0:T(1024)}, s32[1024]{0:T(1024)S(1)}, u32[]{:S(2)}) copy-start(s32[1024]{0:T(1024)S(1)} %iota_and_fusion.1) | copy-start | bytes 12292
  10.2 8.6 %copy-start.25 = (pred[1024]{0:T(1024)(128)(4,1)}, pred[1024]{0:T(1024)(128)(4,1)S(1)}, u32[]{:S(2)}) copy-start(pred[1024]{0:T(1024)(128)(4,1)S(1)} %fusion.26) | copy-start | bytes 3076
  18.8 1.0 copy-start.6
  19.8 12.7 %collective-permute-start.5 = (bf16[128,1920]{1,0:T(8,128)(2,1)}, bf16[128,1920]{1,0:T(8,128)(2,1)S(1)}, u32[]{:S(2)}, u32[]{:S(2)}) collective-permute-start(bf16[128,1920]{1,0:T(8,128)(2,1)} %collective-permute-done.4.first), channel_id=1, source_target_pairs={{0,2},{2,0},{4,6},{6,4},{8,10},{10,8},{12,14},{14,12},{16,18},{18,... | collective-permute-start | bytes 1474568 | tf_op jit(solution)/shard_map/ppermute | solution.py:127
  20.7 17.2 %collective-permute-start.6 = (bf16[128,1920]{1,0:T(8,128)(2,1)}, bf16[128,1920]{1,0:T(8,128)(2,1)S(1)}, u32[]{:S(2)}, u32[]{:S(2)}) collective-permute-start(bf16[128,1920]{1,0:T(8,128)(2,1)} %collective-permute-done.4.first), channel_id=1, source_target_pairs={{0,1},{1,0},{2,3},{3,2},{4,5},{5,4},{6,7},{7,6},{8,9},{9,8},{10,11... | collective-permute-start | bytes 1474568 | tf_op jit(solution)/shard_map/ppermute | solution.py:135
  22.3 15.7 %copy-start.24 = (pred[1024]{0:T(1024)(128)(4,1)S(1)}, pred[1024]{0:T(1024)(128)(4,1)}, u32[]{:S(2)}) copy-start(pred[1024]{0:T(1024)(128)(4,1)} %copy-done.23) | copy-start | bytes 3076
  22.3 15.7 %copy-start.26 = (pred[1024]{0:T(1024)(128)(4,1)S(1)}, pred[1024]{0:T(1024)(128)(4,1)}, u32[]{:S(2)}) copy-start(pred[1024]{0:T(1024)(128)(4,1)} %copy-done.25) | copy-start | bytes 3076
  22.3 15.7 %copy-start.22 = (pred[1024]{0:T(1024)(128)(4,1)S(1)}, pred[1024]{0:T(1024)(128)(4,1)}, u32[]{:S(2)}) copy-start(pred[1024]{0:T(1024)(128)(4,1)} %copy-done.21) | copy-start | bytes 3076
  22.3 15.7 %copy-start.27 = (pred[128]{0:T(512)(128)(4,1)S(1)}, pred[128]{0:T(512)(128)(4,1)}, u32[]{:S(2)}) copy-start(pred[128]{0:T(512)(128)(4,1)} %iota_compare_fusion) | copy-start | bytes 388
  31.9 10.4 %collective-permute-start.2 = (bf16[800,384]{1,0:T(8,128)(2,1)}, bf16[800,384]{1,0:T(8,128)(2,1)S(1)}, u32[]{:S(2)}, u32[]{:S(2)}) collective-permute-start(bf16[800,384]{1,0:T(8,128)(2,1)} %collective-permute-done.1.ext2), channel_id=1, source_target_pairs={{0,2},{2,0},{4,6},{6,4},{8,10},{10,8},{12,14},{14,12},{16,18},{18,... | collective-permute-start | bytes 1843208 | tf_op jit(solution)/shard_map/ppermute | solution.py:127
  32.5 2.1 %copy-start.1 = (bf16[1920,1024]{1,0:T(8,128)(2,1)S(1)}, bf16[1920,1024]{1,0:T(8,128)(2,1)}, u32[]{:S(2)}) copy-start(bf16[1920,1024]{1,0:T(8,128)(2,1)} %fusion.3.perm) | copy-start | bytes 11796484
  34.6 3.4 %copy-start.16 = (s32[1024]{0:T(1024)S(1)}, s32[1024]{0:T(1024)}, u32[]{:S(2)}) copy-start(s32[1024]{0:T(1024)} %copy-done.15) | copy-start | bytes 12292
  34.6 3.4 %copy-start.18 = (s32[1024]{0:T(1024)S(1)}, s32[1024]{0:T(1024)}, u32[]{:S(2)}) copy-start(s32[1024]{0:T(1024)} %copy-done.17) | copy-start | bytes 12292
  34.6 3.4 %copy-start.20 = (s32[1024]{0:T(1024)S(1)}, s32[1024]{0:T(1024)}, u32[]{:S(2)}) copy-start(s32[1024]{0:T(1024)} %copy-done.19) | copy-start | bytes 12292
  37.9 1.9 %collective-permute-start.7 = (bf16[128,1920]{1,0:T(8,128)(2,1)S(1)}, bf16[128,1920]{1,0:T(8,128)(2,1)S(1)}, u32[]{:S(2)}, u32[]{:S(2)}) collective-permute-start(bf16[128,1920]{1,0:T(8,128)(2,1)S(1)} %collective-permute-done.6.first), channel_id=1, source_target_pairs={{0,2},{2,0},{4,6},{6,4},{8,10},{10,8},{12,14},{14,12},{16,18},{18,... | collective-permute-start | bytes 1474568 | tf_op jit(solution)/shard_map/ppermute | solution.py:127
  38.7 3.6 %copy-start.7 = (bf16[512,1024]{1,0:T(8,128)(2,1)S(1)}, bf16[512,1024]{1,0:T(8,128)(2,1)}, u32[]{:S(2)}) copy-start(bf16[512,1024]{1,0:T(8,128)(2,1)} %copy-done.6) | copy-start | bytes 3145732
  42.3 4.8 %copy-start.4 = (bf16[256,1024]{1,0:T(8,128)(2,1)}, bf16[256,1024]{1,0:T(8,128)(2,1)S(1)}, u32[]{:S(2)}) copy-start(bf16[256,1024]{1,0:T(8,128)(2,1)S(1)} %shard_map.81.far) | copy-start | bytes 1572868
  42.3 4.7 %copy-start.12 = (bf16[800,384]{1,0:T(8,128)(2,1)}, bf16[800,384]{1,0:T(8,128)(2,1)S(1)}, u32[]{:S(2)}) copy-start(bf16[800,384]{1,0:T(8,128)(2,1)S(1)} %collective-permute-done.2.ext3) | copy-start | bytes 1843204
  49.6 18.6 %collective-permute-start.8 = (f16[800,256]{1,0:T(8,128)(2,1)}, f16[800,256]{1,0:T(8,128)(2,1)}, u32[]{:S(2)}, u32[]{:S(2)}) collective-permute-start(f16[800,256]{1,0:T(8,128)(2,1)} %get-tuple-element.18), channel_id=1, source_target_pairs={{0,8},{2,10},{4,12},{6,14},{8,16},{10,18},{12,20},{14,22},{16,24},... | collective-permute-start | bytes 1228808 | tf_op jit(solution)/shard_map/ppermute | solution.py:352
  53.8 14.4 %collective-permute-start.9 = (f16[800,256]{1,0:T(8,128)(2,1)}, f16[800,256]{1,0:T(8,128)(2,1)}, u32[]{:S(2)}, u32[]{:S(2)}) collective-permute-start(f16[800,256]{1,0:T(8,128)(2,1)} %get-tuple-element.17), channel_id=1, source_target_pairs={{24,16},{26,18},{28,20},{30,22},{16,8},{18,10},{20,12},{22,14},{8,... | collective-permute-start | bytes 1228808 | tf_op jit(solution)/shard_map/ppermute | solution.py:352
  55.1 15.8 %collective-permute-start.10 = (f16[800,256]{1,0:T(8,128)(2,1)}, f16[800,256]{1,0:T(8,128)(2,1)}, u32[]{:S(2)}, u32[]{:S(2)}) collective-permute-start(f16[800,256]{1,0:T(8,128)(2,1)} %get-tuple-element.16), channel_id=1, source_target_pairs={{0,16},{2,18},{4,20},{6,22},{24,8},{26,10},{28,12},{30,14},{1,17},... | collective-permute-start | bytes 1228808 | tf_op jit(solution)/shard_map/ppermute | solution.py:352
  60.2 1.0 copy-start.5
  61.2 1.2 copy-start.8
  62.4 1.1 copy-start.13
  69.8 15.8 %collective-permute-start.11 = (f16[800,256]{1,0:T(8,128)(2,1)S(1)}, f16[800,256]{1,0:T(8,128)(2,1)S(1)}, u32[]{:S(2)}, u32[]{:S(2)}) collective-permute-start(f16[800,256]{1,0:T(8,128)(2,1)S(1)} %fusion.12), channel_id=1, source_target_pairs={{0,8},{2,10},{4,12},{6,14},{8,24},{10,26},{12,28},{14,30},{24,16},... | collective-permute-start | bytes 1228808 | tf_op jit(solution)/shard_map/ppermute | solution.py:352
  88.7 17.4 %all-to-all-start = ((f16[16,16,800]{2,1,0:T(8,128)(2,1)}), f16[16,16,800]{2,1,0:T(8,128)(2,1)S(1)}, u32[]{:S(2)}, u32[]{:S(2)}) async-start(f16[16,16,800]{2,1,0:T(8,128)(2,1)} %bitcast.43), calls=%async_computation | async-start | bytes 917504 | tf_op jit(solution)/shard_map/all_to_all | solution.py:383
  93.1 4.8 %collective-permute-start.12 = (f32[2,128,128]{2,1,0:T(8,128)S(1)}, f32[2,128,128]{2,1,0:T(8,128)S(1)}, u32[]{:S(2)}, u32[]{:S(2)}) collective-permute-start(f32[2,128,128]{2,1,0:T(8,128)S(1)} %get-tuple-element.12.near), channel_id=1, source_target_pairs={{0,1},{1,0},{2,3},{3,2},{4,5},{5,4},{6,7},{7,6},{8,9},{9,8},{10,11... | collective-permute-start | bytes 393224 | tf_op jit(solution)/shard_map/ppermute | solution.py:135
  101.9 22.8 %copy-start.3 = (f32[2,120,800]{1,2,0:T(8,128)S(1)}, f32[2,120,800]{1,2,0:T(8,128)}, u32[]{:S(2)}) copy-start(f32[2,120,800]{1,2,0:T(8,128)} %param.9) | copy-start | bytes 2304004
  106.1 17.5 %all-to-all-start.1 = ((f16[16,16,800]{2,1,0:T(8,128)(2,1)}), f16[16,16,800]{2,1,0:T(8,128)(2,1)}, u32[]{:S(2)}, u32[]{:S(2)}) async-start(f16[16,16,800]{2,1,0:T(8,128)(2,1)} %bitcast.42), calls=%async_computation.1 | async-start | bytes 917504 | tf_op jit(solution)/shard_map/all_to_all | solution.py:383
  124.7 1.2 copy-start.9
  125.9 1.1 copy-start.14

commit v3 on v0

--- a/solution.py
+++ b/solution.py
@@ -1,8 +1,11 @@
+import functools
 import math
 
 import jax
 import jax.numpy as jnp
 from jax import lax
+from jax.experimental import pallas as pl
+from jax.experimental.pallas import tpu as pltpu
 from jax.sharding import PartitionSpec as P
 
 HEAD = 128
@@ -20,6 +23,19 @@
 weight_decay = 0.1
 norm_floor = 1e-07
 
+SIZE_Z, SIZE_Y, SIZE_C = 4, 2, 2
+GAIN = 1.0 + momentum_rate
+MIX = momentum_rate * momentum_rate / GAIN
+BF16 = jnp.bfloat16
+F32 = jnp.float32
+VMEM_BYTES = 20 * 1024 * 1024
+COL_PARTS = 1
+HALF_PARTS = 1
+CHUNK_ORDERS = ((3, 2, 1, 0), (0, 2, 3, 1), (3, 1, 0, 2), (0, 1, 2, 3))
+CHUNK_STEPS = len(CHUNK_ORDERS[0])
+CHUNK_SENDS = 2
+NO_HEAD = -(1 << 20)
+
 
 def quintic(current, reduce_gram):
     for step_index in range(ITERS):
@@ -40,7 +56,7 @@
     return current
 
 
-def per_device(context, cotangent, tile_counts, momentum, weights):
+def row_plan(context, cotangent, tile_counts, momentum, weights):
     layers, tok_dev, all_rows = context.shape
     columns = cotangent.shape[2]
     shard_rows = momentum.shape[1]
@@ -105,6 +121,368 @@
     new_weights = weights - learn_rate * (weight_decay * weights + update_scale * update_rows)
     return (moment_new, new_weights)
 
+def dp_index(z, y, c):
+    return (z * SIZE_Y + y) * SIZE_C + c
+
+
+def all_chips():
+    return [(z, y, c) for z in range(SIZE_Z) for y in range(SIZE_Y) for c in range(SIZE_C)]
+
+
+def swap_core(value):
+    return lax.ppermute(value, "dp", [(dp_index(z, y, c), dp_index(z, y, 1 - c)) for z, y, c in all_chips()])
+
+
+def swap_y(value):
+    return lax.ppermute(value, "dp", [(dp_index(z, y, c), dp_index(z, 1 - y, c)) for z, y, c in all_chips()])
+
+
+def swap_x(value):
+    return lax.ppermute(value, "mp", [(0, 1), (1, 0)])
+
+
+def after(value, *earlier):
+    return lax.optimization_barrier((value, *earlier))[0]
+
+
+def contract(left, right, dims):
+    return lax.dot_general(left, right, (dims, ((), ())), preferred_element_type=F32)
+
+
+def ext_kernel(pick, cotangent, momentum, counts, *out_refs):
+    tokens, rows = cotangent.shape[2], momentum.shape[2]
+    position = lax.broadcasted_iota(jnp.int32, (1, tokens), 1)
+    live = (position // TILE_TOK < counts[0]).astype(F32)
+    start = 0
+    for out_ref in out_refs:
+        part = slice(start, start + out_ref.shape[0])
+        start = part.stop
+        out_ref[:, :tokens] = (cotangent[0, part].astype(F32) * live).astype(BF16)
+        pad = jnp.zeros((out_ref.shape[0], HEAD - rows), BF16)
+        out_ref[:, tokens:] = jnp.concatenate([mixed_part(momentum[0, part]), pad], axis=1)
+
+
+def mixed_part(momentum):
+    return (momentum * (2.0 * MIX)).astype(BF16)
+
+
+def head_of(step, c, index):
+    head = step * 4 + c * 2 + index
+    return jnp.where(head < HEADS_WIN, head, NO_HEAD)
+
+
+def slot_kernel(core, *refs):
+    *pieces, out_ref, lead = refs
+    step = pl.program_id(0)
+
+    @pl.when(step == 0)
+    def _():
+        row = lax.broadcasted_iota(jnp.int32, lead.shape, 0)
+        lead[...] = row - HEADS_WIN * lax.broadcasted_iota(jnp.int32, lead.shape, 1)
+
+    places = [(lead[...] == head_of(step, core[0], index)).astype(F32).astype(BF16) for index in range(2)]
+    tokens = jnp.concatenate([piece[...] for piece in pieces], axis=0)
+    out_ref[0] = contract(tokens, jnp.concatenate(places, axis=1), ((1,), (0,))).astype(BF16)
+
+
+def chunk_kernel(table, ext0, ext1, ext2, ext3, own, near, far, send_ref, keep_ref, *, factor, rows):
+    step = pl.program_id(0)
+    x, z, y, c = (table[CHUNK_STEPS + index] for index in range(4))
+    tokens = own.shape[1] // 2
+    half = tokens // 2
+    low_first = x == 0
+    total = contract(ext0[:, :tokens], own[0, :tokens], ((1,), (0,)))
+    total += contract(ext1[:, :tokens], own[0, tokens:], ((1,), (0,)))
+    for source, ext in enumerate((ext2, ext3)):
+        here = near[0, source * half : (source + 1) * half]
+        there = far[0, source * half : (source + 1) * half]
+        low = jnp.where(low_first, here, there)
+        high = jnp.where(low_first, there, here)
+        total += contract(ext[:, :tokens], jnp.concatenate([low, high], axis=0), ((1,), (0,)))
+    local = lax.broadcasted_iota(jnp.int32, (HEAD, HEAD), 0)
+    lead = jnp.where(local < rows, local - HEADS_WIN * lax.broadcasted_iota(jnp.int32, (HEAD, HEAD), 1), 2 * NO_HEAD)
+    for sender_y, left, right in ((y, ext0, ext1), (1 - y, ext2, ext3)):
+        places = []
+        for sender_c in (c, 1 - c):
+            first_row = dp_index(z, sender_y, sender_c) * rows
+            hits = [lead + first_row == head_of(table[step], c, index) for index in range(2)]
+            hits = jnp.concatenate([jnp.where(hit, 0.5 / factor, 0.0) for hit in hits], axis=1)
+            places.append(hits.astype(BF16))
+        mixed_in = jnp.concatenate([left[:, tokens:], right[:, tokens:]], axis=1)
+        total += contract(mixed_in, jnp.concatenate(places, axis=0), ((1,), (0,)))
+    total = total * factor
+
+    @pl.when(step < CHUNK_SENDS)
+    def _():
+        send_ref[0] = total
+
+    @pl.when(step >= CHUNK_SENDS)
+    def _():
+        keep_ref[0] = total
+
+
+def gram_kernel(*refs):
+    *parts, near_ref, far_ref = refs
+    for head in range(2):
+        total = None
+        for part in parts:
+            block = (GAIN * part[:, head * HEAD : (head + 1) * HEAD]).astype(BF16)
+            term = contract(block, block, ((0,), (0,)))
+            total = term if total is None else total + term
+        near_ref[head] = total
+        far_ref[head] = total.astype(BF16)
+
+
+def turn_kernel(*refs):
+    *parts, turned_ref, owner_ref = refs
+    value = jnp.concatenate([part[...] for part in parts], axis=0).T
+    turned_ref[...] = value
+    store_by_owner(owner_ref, [value[:HEAD], value[HEAD:]])
+
+
+def store_by_owner(owner_ref, blocks):
+    owners = owner_ref.shape[0]
+    depth = HEAD // owners
+    for owner in range(owners):
+        rows = [block[owner * depth : (owner + 1) * depth] for block in blocks]
+        owner_ref[owner] = jnp.concatenate(rows, axis=0).astype(owner_ref.dtype)
+
+
+def square_dot(left, right):
+    return jnp.dot(left, right, precision=lax.Precision.HIGHEST, preferred_element_type=F32)
+
+
+def ortho_kernel(near, far, turned, out_ref):
+    row = lax.broadcasted_iota(jnp.int32, (HEAD, HEAD), 0)
+    column = lax.broadcasted_iota(jnp.int32, (HEAD, HEAD), 1)
+    eye = (row == column).astype(F32)
+    blocks = []
+    for head in range(2):
+        raw = near[head] + far[head].astype(F32)
+        squares = jnp.sum(raw * eye, axis=(0, 1), keepdims=True)
+        scale = 1.0 / (jnp.sqrt(squares) + norm_floor)
+        gram = raw * (scale * scale)
+        total = None
+        for step in range(ITERS):
+            poly = quintic_b * gram + quintic_c * square_dot(gram, gram)
+            factor = quintic_a * eye + poly
+            total = factor if total is None else square_dot(factor, total)
+            if step + 1 < ITERS:
+                gram = square_dot(square_dot(factor, gram), factor)
+        total = total * scale
+        high = total.astype(BF16)
+        low = (total - high.astype(F32)).astype(BF16)
+        block = (GAIN * turned[head * HEAD : (head + 1) * HEAD]).astype(BF16)
+        blocks.append(contract(high, block, ((1,), (0,))) + contract(low, block, ((1,), (0,))))
+    store_by_owner(out_ref, blocks)
+
+
+def to_rows(back, layer):
+    places = [(z, layer, c) for z in range(SIZE_Z) for c in range(SIZE_C)]
+    value = jnp.concatenate([back[place] for place in places], axis=0)
+    depth = back.shape[3] // 2
+    row = lax.broadcasted_iota(jnp.int32, (value.shape[0], HEAD), 0)
+    col = lax.broadcasted_iota(jnp.int32, (value.shape[0], HEAD), 1)
+    order = (col == row % depth * HEADS_WIN + row // depth) & (row // depth < HEADS_WIN)
+    order = order.astype(F32).astype(BF16)
+    high = value.astype(BF16)
+    result = contract(high, order, ((0,), (0,)))
+    if value.dtype == F32:
+        result += contract((value - high.astype(F32)).astype(BF16), order, ((0,), (0,)))
+    return result
+
+
+def momentum_kernel(mixed_back, momentum, out_ref):
+    for layer in range(2):
+        old = momentum[layer]
+        gradient = to_rows(mixed_back, layer)[:, : old.shape[1]] - 0.5 * mixed_part(old).astype(F32)
+        out_ref[layer] = momentum_rate * old + gradient
+
+
+def weights_kernel(ortho_back, weights, out_ref, *, update_scale):
+    for layer in range(2):
+        old = weights[layer]
+        update = to_rows(ortho_back, layer)[:, : old.shape[1]]
+        out_ref[layer] = old - learn_rate * (weight_decay * old + update_scale * update)
+
+
+def vmem_params(**kwargs):
+    return pltpu.CompilerParams(vmem_limit_bytes=VMEM_BYTES, **kwargs)
+
+
+def block_plan(context, cotangent, tile_counts, momentum, weights):
+    layers, tok_dev, all_rows = context.shape
+    columns = cotangent.shape[2]
+    shard_rows = momentum.shape[1]
+    depth = shard_rows // HEADS_WIN
+    half = tok_dev // 2
+    where = lax.axis_index("dp")
+    z, y, c = where // (SIZE_Y * SIZE_C), where // SIZE_C % SIZE_Y, where % SIZE_C
+    x = lax.axis_index("mp")
+    factor = 1.0 / math.sqrt(tok_dev * lax.axis_size("dp"))
+
+    size = half // HALF_PARTS
+    half_send = [
+        lax.dynamic_slice(context, (1 - y, x * half + index * size, 0), (1, size, all_rows))[0]
+        for index in range(HALF_PARTS)
+    ]
+    first0 = [swap_y(piece) for piece in half_send]
+
+    cotangent_t = jnp.transpose(cotangent, (0, 2, 1))
+    momentum_t = jnp.transpose(momentum, (0, 2, 1))
+    weights_t = jnp.transpose(weights, (0, 2, 1))
+    wide = tok_dev + HEAD
+
+    part_cols = [columns // COL_PARTS] * COL_PARTS
+
+    def ext_of(layer):
+        return pl.pallas_call(
+            ext_kernel,
+            grid_spec=pltpu.PrefetchScalarGridSpec(
+                num_scalar_prefetch=1,
+                grid=(1,),
+                in_specs=[
+                    pl.BlockSpec((1, columns, tok_dev), lambda i, pick: (pick[0], 0, 0)),
+                    pl.BlockSpec((1, columns, shard_rows), lambda i, pick: (pick[0], 0, 0)),
+                    pl.BlockSpec(memory_space=pltpu.SMEM),
+                ],
+                out_specs=[pl.BlockSpec((size, wide), lambda i, pick: (0, 0)) for size in part_cols],
+            ),
+            out_shape=[jax.ShapeDtypeStruct((size, wide), BF16) for size in part_cols],
+            compiler_params=vmem_params(),
+            cost_estimate=pl.CostEstimate(flops=10**10, bytes_accessed=2 * 10**6, transcendentals=0),
+        )(layer.reshape(1), cotangent_t, momentum_t, tile_counts)
+
+    ext_send = ext_of(after(1 - y, *half_send))
+    ext2 = [swap_y(part) for part in ext_send]
+    ctx_keep = lax.dynamic_index_in_dim(context, after(y, *half_send), 0, False)
+    ctx1 = swap_core(ctx_keep)
+    ext_keep = ext_of(after(y, *ext_send))
+    ext1 = [swap_core(part) for part in ext_keep]
+
+    lanes = 2 * HEAD
+
+    def slots_of(*pieces, flops):
+        tokens = sum(piece.shape[0] for piece in pieces)
+        return pl.pallas_call(
+            slot_kernel,
+            grid_spec=pltpu.PrefetchScalarGridSpec(
+                num_scalar_prefetch=1,
+                grid=(SIZE_Z,),
+                in_specs=[pl.BlockSpec(piece.shape, lambda j, core: (0, 0)) for piece in pieces],
+                out_specs=pl.BlockSpec((1, tokens, lanes), lambda j, core: (j, 0, 0)),
+                scratch_shapes=[pltpu.VMEM((all_rows, HEAD), jnp.int32)],
+            ),
+            out_shape=jax.ShapeDtypeStruct((SIZE_Z, tokens, lanes), BF16),
+            compiler_params=vmem_params(),
+            cost_estimate=pl.CostEstimate(flops=flops, bytes_accessed=10**6, transcendentals=0),
+        )(c.reshape(1), *pieces)
+
+    own = slots_of(after(ctx_keep, *ext_send), ctx1, flops=10**6)
+    second0, first1 = [], []
+    for index in range(HALF_PARTS):
+        if index + 1 == HALF_PARTS:
+            first0[index] = after(first0[index], own)
+        second0.append(swap_x(first0[index]))
+        first1.append(swap_core(first0[index]))
+    near = slots_of(*first0, *first1, flops=10**10)
+    second0 = [after(piece, near) for piece in second0]
+    second1 = [swap_core(piece) for piece in second0]
+    far = slots_of(*second0, *second1, flops=10**10)
+    ext2 = [after(part, near) for part in ext2]
+    ext3 = [swap_core(part) for part in ext2]
+
+    table = lax.dynamic_index_in_dim(jnp.array(CHUNK_ORDERS, jnp.int32), z, 0, False)
+    table = jnp.concatenate([table, jnp.stack([x, z, y, c])])
+
+    def chunks_of(ext0, ext1, ext2, ext3):
+        size = ext0.shape[0]
+        full = pl.BlockSpec((size, wide), lambda j, table: (0, 0))
+        part = lambda count: pl.BlockSpec((1, count, lanes), lambda j, table: (table[j], 0, 0))
+        keeps = CHUNK_STEPS - CHUNK_SENDS
+        return pl.pallas_call(
+            functools.partial(chunk_kernel, factor=factor, rows=shard_rows),
+            grid_spec=pltpu.PrefetchScalarGridSpec(
+                num_scalar_prefetch=1,
+                grid=(CHUNK_STEPS,),
+                in_specs=[full] * 4 + [part(2 * tok_dev), part(tok_dev), part(tok_dev)],
+                out_specs=[
+                    pl.BlockSpec((1, size, lanes), lambda j, table: (jnp.minimum(j, CHUNK_SENDS - 1), 0, 0)),
+                    pl.BlockSpec((1, size, lanes), lambda j, table: (jnp.maximum(j - CHUNK_SENDS, 0), 0, 0)),
+                ],
+            ),
+            out_shape=[
+                jax.ShapeDtypeStruct((CHUNK_SENDS, size, lanes), F32),
+                jax.ShapeDtypeStruct((keeps, size, lanes), F32),
+            ],
+            compiler_params=vmem_params(),
+            cost_estimate=pl.CostEstimate(
+                flops=2 * CHUNK_STEPS * size * (4 * tok_dev + 4 * HEAD) * lanes,
+                bytes_accessed=6 * 10**6,
+                transcendentals=0,
+            ),
+        )(table, ext0, ext1, ext2, ext3, own, near, far)
+
+    def along_z(value, pairs):
+        pairs = [(dp_index(p, b, a), dp_index(q, b, a)) for p, q in pairs for b in range(SIZE_Y) for a in range(SIZE_C)]
+        return lax.ppermute(value.astype(jnp.float16), "dp", pairs)
+
+    def only(condition, value):
+        return jnp.where(condition, value.astype(F32), jnp.zeros((), F32))
+
+    arrivals, mixed = [], []
+    for part in range(COL_PARTS):
+        send, keep = chunks_of(ext_keep[part], ext1[part], ext2[part], ext3[part])
+        pair = along_z(send[0], [(0, 1), (1, 0), (2, 3), (3, 2)])
+        inner = along_z(send[1], [(1, 2), (2, 1)])
+        outer = along_z(send[1], [(0, 2), (3, 1)])
+        arrivals.append((keep, pair, inner, outer))
+    middle = (z == 1) | (z == 2)
+    for keep, pair, inner, outer in arrivals:
+        merged = (keep[0] + only(middle, pair)).astype(jnp.float16)
+        last = along_z(merged, [(0, 1), (1, 3), (3, 2), (2, 0)])
+        base = keep[1] + only(~middle, after(pair, merged)) + (inner.astype(F32) + outer.astype(F32))
+        base, last = lax.optimization_barrier((base, last))
+        mixed.append(base + last.astype(F32))
+
+    owners = lax.axis_size("dp")
+    by_owner = (owners, 2 * depth, columns)
+    gram, gram_send = pl.pallas_call(
+        gram_kernel,
+        out_shape=[jax.ShapeDtypeStruct((2, HEAD, HEAD), kind) for kind in (F32, BF16)],
+        compiler_params=vmem_params(),
+    )(*mixed)
+    gram_far = swap_x(gram_send)
+    turned, mixed_send = pl.pallas_call(
+        turn_kernel,
+        out_shape=[jax.ShapeDtypeStruct((lanes, columns), F32), jax.ShapeDtypeStruct(by_owner, F32)],
+        compiler_params=vmem_params(),
+        cost_estimate=pl.CostEstimate(flops=10**10, bytes_accessed=2 * 10**6, transcendentals=0),
+    )(after(mixed[0], gram), *mixed[1:])
+    ortho_send = pl.pallas_call(
+        ortho_kernel,
+        out_shape=jax.ShapeDtypeStruct(by_owner, BF16),
+        compiler_params=vmem_params(),
+    )(gram, gram_far, turned)
+
+    def returned(value):
+        return lax.all_to_all(value, "dp", 0, 0).reshape(SIZE_Z, SIZE_Y, SIZE_C, 2 * depth, columns)
+
+    out = jax.ShapeDtypeStruct((layers, columns, shard_rows), F32)
+    mixed_back = returned(mixed_send.astype(jnp.float16)).astype(F32)
+    moment_new = pl.pallas_call(
+        momentum_kernel,
+        out_shape=out,
+        compiler_params=vmem_params(),
+        cost_estimate=pl.CostEstimate(flops=10**10, bytes_accessed=2 * 10**6, transcendentals=0),
+    )(mixed_back, momentum_t)
+    new_weights = pl.pallas_call(
+        functools.partial(weights_kernel, update_scale=0.2 * math.sqrt(max(HEAD, COLS))),
+        out_shape=out,
+        compiler_params=vmem_params(),
+    )(returned(ortho_send), weights_t)
+    return jnp.transpose(moment_new, (0, 2, 1)), jnp.transpose(new_weights, (0, 2, 1))
+
 
 def solution(mesh):
     in_specs = (
@@ -115,6 +493,7 @@
         P(None, "dp", "mp"),
     )
     out_specs = (P(None, "dp", "mp"), P(None, "dp", "mp"))
+    small = mesh.shape["dp"] == SIZE_Z * SIZE_Y * SIZE_C and mesh.shape["mp"] == 2
     return jax.shard_map(
-        per_device, mesh=mesh, in_specs=in_specs, out_specs=out_specs, check_vma=False
+        block_plan if small else row_plan, mesh=mesh, in_specs=in_specs, out_specs=out_specs, check_vma=False
     )

time: 562 us -> 120 us (0.21)
  waiting for transfers between devices: 411 us -> 52.8 us
  matrix products: 61.6 us -> 0 us
  local copies, waits for them, and re-layouts: 55.4 us -> 8.86 us
  starting transfers between devices: 0.39 us -> 26.6 us
  Pallas kernels: 0 us -> 23.4 us
  between operations: 15.3 us -> 1.56 us
  other arithmetic: 12.4 us -> 5.47 us
    unnamed x6 -> x0, waiting for transfers between devices: 231 us -> none
    psum x3 -> x0, waiting for transfers between devices: 115 us -> none  [per_device(): lax.psum(partial_value.astype(jnp.bfloat16), 'mp').astype(jnp.float32)]
    all_gather x1 -> x0, waiting for transfers between devices: 65.6 us -> none  [per_device(): gathered = lax.all_gather(nesterov, 'dp', axis=1, tiled=True)]
    dot_general x8 -> x0, matrix products: 61.6 us -> none  [the longest x3 34.8 us: quintic(): jnp.einsum('lshg,lsgc->lshc', poly_term, current, preferred_element_type=...]
    ppermute x0 -> x13, waiting for transfers between devices: none -> 37.7 us  [the longest x4 23 us: along_z(): return lax.ppermute(value.astype(jnp.float16), 'dp', pairs)]
    reshape x2 -> x0, local copies, waits for them, and re-layouts: 25.5 us -> none  [the longest x1 18.5 us: per_device(): orthogonal.reshape(layers, slots * HEAD, columns)]
    pallas_call x0 -> x11, Pallas kernels: none -> 23.4 us  [the longest x3 9.25 us: slots_of(): pl.pallas_call(slot_kernel, grid_spec=pltpu.PrefetchScalarGridSpec(num_sc...]
    gather x3 -> x0, local copies, waits for them, and re-layouts: 21.3 us -> none  [the longest x2 16.9 us: per_device(): slab_block = jnp.transpose(jnp.take(grid, head_ids, axis=2), (0, 2, 1, 3))]
  transfers between devices with their start and end apart: 5 -> 15, of which waited for: 5 -> 9; matrix products, arithmetic and copies ran while one was open for 0% -> 4% of each run, Pallas kernels for 0% -> 14%
where the time goes in v3:
time: 120 us; the launch traced here: 119 us
  waiting for transfers between devices  52.8 us (44%)
  starting transfers between devices  26.6 us (22%)
  Pallas kernels  23.4 us (20%)
  local copies, waits for them, and re-layouts  8.86 us (7%)
  other arithmetic  5.47 us (5%)
  between operations  1.56 us (1%)
    ppermute x4, waiting for transfers between devices, along_z(): return lax.ppermute(value.astype(jnp.float16), 'dp', pairs)  23 us
    all_to_all x2, waiting for transfers between devices, returned(): lax.all_to_all(value, 'dp', 0, 0)  15 us
    ppermute x2, waiting for transfers between devices, swap_x(): return lax.ppermute(value, 'mp', [(0, 1), (1, 0)])  11.8 us
    all_to_all x2, starting transfers between devices, returned(): lax.all_to_all(value, 'dp', 0, 0)  9.94 us
    pallas_call x3, Pallas kernels, slots_of(): pl.pallas_call(slot_kernel, grid_spec=pltpu.PrefetchScalarGridSpec(num_sc...  9.25 us
    ppermute x4, starting transfers between devices, along_z(): return lax.ppermute(value.astype(jnp.float16), 'dp', pairs)  7.53 us
    unnamed x24, local copies, waits for them, and re-layouts  5.92 us
    pallas_call x1, Pallas kernels, chunks_of(): pl.pallas_call(functools.partial(chunk_kernel, factor=factor, rows=shard_...  5.16 us
  transfers between devices with their start and end apart: 15, of which 9 were waited for; matrix products, arithmetic and copies ran while one was open for 4% of the time, Pallas kernels for 14%

profile of v3, /device:TPU:1, one launch (start us, length us, event | category | flops | bytes accessed | tf_op | source)
XLA Modules:
  0.0 118.6 jit_solution(10536860368259141449)
XLA Ops:
  0.7 1.5 %copy-done = bf16[2,256,1920]{2,1,0:T(8,128)(2,1)S(1)} copy-done((bf16[2,256,1920]{2,1,0:T(8,128)(2,1)S(1)}, bf16[2,256,1920]{2,1,0:T(8,128)(2,1)}, u32[]{:S(2)}) %copy-start) | copy-done | bytes 1966104
  2.2 0.8 dynamic-slice_bitcast_fusion.1
  3.1 0.1 collective-permute-start.3
  3.2 2.7 %collective-permute-start.2 = (bf16[128,1920]{1,0:T(8,128)(2,1)}, bf16[128,1920]{1,0:T(8,128)(2,1)S(1)}, u32[]{:S(2)}, u32[]{:S(2)}) collective-permute-start(bf16[128,1920]{1,0:T(8,128)(2,1)} %dynamic-slice_bitcast_fusion.1), channel_id=1, source_target_pairs={{0,4},{2,6},{4,0},{6,2},{8,12},{10,14},{12,8},{14,10},{16,20},{18,... | collective-permute-start | bytes 1474568 | tf_op jit(solution)/shard_map/ppermute | solution.py:137
  6.6 1.1 copy-done.5
  7.7 1.1 copy-done.7
  8.8 0.9 shard_map.77
  9.8 4.2 %shard_map.79.own = bf16[4,512,256]{2,1,0:T(8,128)(2,1)S(1)} custom-call(s32[1]{0:T(128)} %bitcast.4.core, bf16[256,1920]{1,0:T(8,128)(2,1)S(1)} %dynamic-slice_bitcast_fusion.refs_0_, bf16[256,1920]{1,0:T(8,128)(2,1)} %collective-permute-done.3.refs_1_), custom_call_target="tpu_custom_call" | custom-call | flops 1000000 | bytes 1000000 | tf_op jit(solution)/shard_map/pallas_call | solution.py:367
  14.0 1.0 copy-done.2
  15.0 2.6 %collective-permute-done.2.refs_0_ = bf16[128,1920]{1,0:T(8,128)(2,1)S(1)} collective-permute-done((bf16[128,1920]{1,0:T(8,128)(2,1)}, bf16[128,1920]{1,0:T(8,128)(2,1)S(1)}, u32[]{:S(2)}, u32[]{:S(2)}) %collective-permute-start.2) | collective-permute-done | bytes 491552 | tf_op jit(solution)/shard_map/ppermute | solution.py:137
  17.6 0.7 collective-permute-start.4
  18.3 1.5 %collective-permute-start.1 = (bf16[800,384]{1,0:T(8,128)(2,1)}, bf16[800,384]{1,0:T(8,128)(2,1)S(1)}, u32[]{:S(2)}, u32[]{:S(2)}) collective-permute-start(bf16[800,384]{1,0:T(8,128)(2,1)} %shard_map.77), channel_id=1, source_target_pairs={{0,4},{2,6},{4,0},{6,2},{8,12},{10,14},{12,8},{14,10},{16,20},{18,... | collective-permute-start | bytes 1843208 | tf_op jit(solution)/shard_map/ppermute | solution.py:137
  19.7 1.2 %collective-permute-start.6 = (bf16[128,1920]{1,0:T(8,128)(2,1)S(1)}, bf16[128,1920]{1,0:T(8,128)(2,1)}, u32[]{:S(2)}, u32[]{:S(2)}) collective-permute-start(bf16[128,1920]{1,0:T(8,128)(2,1)S(1)} %collective-permute-done.2.refs_0_), channel_id=1, source_target_pairs={{0,1},{1,0},{2,3},{3,2},{4,5},{5,4},{6,7},{7,6},{8,9},{9,8},{10,11... | collective-permute-start | bytes 1474568 | tf_op jit(solution)/shard_map/ppermute | solution.py:141
  21.0 1.9 %shard_map.80.near = bf16[4,256,256]{2,1,0:T(8,128)(2,1)S(1)} custom-call(s32[1]{0:T(128)} %bitcast.4.core, bf16[128,1920]{1,0:T(8,128)(2,1)S(1)} %collective-permute-done.2.refs_0_, bf16[128,1920]{1,0:T(8,128)(2,1)S(1)} %collective-permute-done.4.refs_1_), custom_call_target="tpu_custom_call" | custom-call | flops 10000000000 | bytes 1000000 | tf_op jit(solution)/shard_map/pallas_call | solution.py:367
  22.9 9.5 %collective-permute-done.6.refs_0_ = bf16[128,1920]{1,0:T(8,128)(2,1)} collective-permute-done((bf16[128,1920]{1,0:T(8,128)(2,1)S(1)}, bf16[128,1920]{1,0:T(8,128)(2,1)}, u32[]{:S(2)}, u32[]{:S(2)}) %collective-permute-start.6) | collective-permute-done | bytes 491552 | tf_op jit(solution)/shard_map/ppermute | solution.py:141
  32.4 1.1 collective-permute-start.7
  33.5 0.1 shard_map.78.ext0
  33.7 0.7 fusion.2
  34.4 0.1 concatenate.3.table
  34.5 0.5 collective-permute-start.5
  35.0 0.3 collective-permute-done.7.refs_1_
  35.3 3.1 %shard_map.81.far = bf16[4,256,256]{2,1,0:T(8,128)(2,1)S(1)} custom-call(s32[1]{0:T(128)} %bitcast.4.core, bf16[128,1920]{1,0:T(8,128)(2,1)} %collective-permute-done.6.refs_0_, bf16[128,1920]{1,0:T(8,128)(2,1)} %collective-permute-done.7.refs_1_), custom_call_target="tpu_custom_call" | custom-call | flops 10000000000 | bytes 1000000 | tf_op jit(solution)/shard_map/pallas_call | solution.py:367
  38.5 5.2 %shard_map.82 = (f32[2,800,256]{2,1,0:T(8,128)S(1)}, f32[2,800,256]{2,1,0:T(8,128)S(1)}) custom-call(s32[8]{0:T(128)S(1)} %concatenate.3.table, bf16[800,384]{1,0:T(8,128)(2,1)S(1)} %shard_map.78.ext0, bf16[800,384]{1,0:T(8,128)(2,1)} %collective-permute-done.ext1, bf16[800,384]{1,0:T(8,128)(2,1)S(1)} %collective-permute-done.1.ext2, ...), custom_call_target="tpu_custom_call" | custom-call | flops 2516582400 | bytes 6000000 | tf_op jit(solution)/shard_map/pallas_call | solution.py:403
  43.7 0.1 convert.5
  43.8 1.3 %slice_bitcast_fusion.1 = (f16[800,256]{1,0:T(8,128)(2,1)}, f16[800,256]{1,0:T(8,128)(2,1)}) fusion(f16[2,800,256]{2,1,0:T(8,128)(2,1)S(1)} %convert.5), kind=kLoop, calls=%fused_computation.8 | loop fusion | bytes 1638400 | tf_op jit(solution)/shard_map/convert_element_type | solution.py:428
  45.1 1.3 %collective-permute-start.8 = (f16[800,256]{1,0:T(8,128)(2,1)}, f16[800,256]{1,0:T(8,128)(2,1)S(1)}, u32[]{:S(2)}, u32[]{:S(2)}) collective-permute-start(f16[800,256]{1,0:T(8,128)(2,1)} %get-tuple-element.36), channel_id=1, source_target_pairs={{0,8},{2,10},{4,12},{6,14},{8,0},{10,2},{12,4},{14,6},{16,24},{18,... | collective-permute-start | bytes 1228808 | tf_op jit(solution)/shard_map/ppermute | solution.py:428
  46.4 4.2 %collective-permute-start.10 = (f16[800,256]{1,0:T(8,128)(2,1)}, f16[800,256]{1,0:T(8,128)(2,1)S(1)}, u32[]{:S(2)}, u32[]{:S(2)}) collective-permute-start(f16[800,256]{1,0:T(8,128)(2,1)} %get-tuple-element.37), channel_id=1, source_target_pairs={{0,16},{2,18},{4,20},{6,22},{24,8},{26,10},{28,12},{30,14},{1,17},... | collective-permute-start | bytes 1228808 | tf_op jit(solution)/shard_map/ppermute | solution.py:428
  50.6 0.7 collective-permute-start.9
  51.3 4.6 %collective-permute-done.8 = f16[800,256]{1,0:T(8,128)(2,1)S(1)} collective-permute-done((f16[800,256]{1,0:T(8,128)(2,1)}, f16[800,256]{1,0:T(8,128)(2,1)S(1)}, u32[]{:S(2)}, u32[]{:S(2)}) %collective-permute-start.8) | collective-permute-done | bytes 409632 | tf_op jit(solution)/shard_map/ppermute | solution.py:428
  56.0 2.0 %fusion = f16[800,256]{1,0:T(8,128)(2,1)} fusion(f16[800,256]{1,0:T(8,128)(2,1)S(1)} %collective-permute-done.8, f32[2,800,256]{2,1,0:T(8,128)} %copy-done.1, pred[]{:T(512)S(6)} %or.3), kind=kLoop, calls=%fused_computation.2 | loop fusion | flops 819200 | bytes 1638401 | tf_op jit(solution)/shard_map/convert_element_type | solution.py:442
  58.0 1.3 %collective-permute-start.11 = (f16[800,256]{1,0:T(8,128)(2,1)}, f16[800,256]{1,0:T(8,128)(2,1)}, u32[]{:S(2)}, u32[]{:S(2)}) collective-permute-start(f16[800,256]{1,0:T(8,128)(2,1)} %fusion), channel_id=1, source_target_pairs={{0,8},{2,10},{4,12},{6,14},{8,24},{10,26},{12,28},{14,30},{24,16},... | collective-permute-start | bytes 1228808 | tf_op jit(solution)/shard_map/ppermute | solution.py:428
  59.3 4.7 %collective-permute-done.10 = f16[800,256]{1,0:T(8,128)(2,1)S(1)} collective-permute-done((f16[800,256]{1,0:T(8,128)(2,1)}, f16[800,256]{1,0:T(8,128)(2,1)S(1)}, u32[]{:S(2)}, u32[]{:S(2)}) %collective-permute-start.10) | collective-permute-done | bytes 409632 | tf_op jit(solution)/shard_map/ppermute | solution.py:428
  64.0 1.3 %fusion.1 = f32[800,256]{1,0:T(8,128)S(1)} fusion(f16[800,256]{1,0:T(8,128)(2,1)S(1)} %collective-permute-done.10, f16[800,256]{1,0:T(8,128)(2,1)S(1)} %collective-permute-done.9, f16[800,256]{1,0:T(8,128)(2,1)S(1)} %collective-permute-done.8, f32[2,800,256]{2,1,0:T(8,128)} %copy-done.1, pred[]{:T(512)S(6)} %not.3), kind=kLoop, calls=%fused_computation.4 | loop fusion | flops 1433600 | bytes 2867201 | tf_op jit(solution)/shard_map/add | solution.py:444
  65.3 13.6 %collective-permute-done.11 = f16[800,256]{1,0:T(8,128)(2,1)} collective-permute-done((f16[800,256]{1,0:T(8,128)(2,1)}, f16[800,256]{1,0:T(8,128)(2,1)}, u32[]{:S(2)}, u32[]{:S(2)}) %collective-permute-start.11) | collective-permute-done | bytes 409632 | tf_op jit(solution)/shard_map/ppermute | solution.py:428
  79.0 1.1 convert_add_fusion.refs_0_
  80.1 0.3 shard_map.83
  80.4 0.3 shard_map.84
  80.7 0.8 convert_element_type.43
  81.5 5.7 %all-to-all-start = ((f16[16,16,800]{2,1,0:T(8,128)(2,1)}), f16[16,16,800]{2,1,0:T(8,128)(2,1)S(1)}, u32[]{:S(2)}, u32[]{:S(2)}) async-start(f16[16,16,800]{2,1,0:T(8,128)(2,1)} %convert_element_type.43), calls=%async_computation | async-start | bytes 917504 | tf_op jit(solution)/shard_map/all_to_all | solution.py:469
  87.3 1.2 %collective-permute-start.12 = (bf16[2,128,128]{2,1,0:T(8,128)(2,1)S(1)}, bf16[2,128,128]{2,1,0:T(8,128)(2,1)S(1)}, u32[]{:S(2)}, u32[]{:S(2)}) collective-permute-start(bf16[2,128,128]{2,1,0:T(8,128)(2,1)S(1)} %get-tuple-element.34), channel_id=1, source_target_pairs={{0,1},{1,0},{2,3},{3,2},{4,5},{5,4},{6,7},{7,6},{8,9},{9,8},{10,11... | collective-permute-start | bytes 196616 | tf_op jit(solution)/shard_map/ppermute | solution.py:141
  88.5 2.3 %collective-permute-done.12.far = bf16[2,128,128]{2,1,0:T(8,128)(2,1)S(1)} collective-permute-done((bf16[2,128,128]{2,1,0:T(8,128)(2,1)S(1)}, bf16[2,128,128]{2,1,0:T(8,128)(2,1)S(1)}, u32[]{:S(2)}, u32[]{:S(2)}) %collective-permute-start.12) | collective-permute-done | bytes 65568 | tf_op jit(solution)/shard_map/ppermute | solution.py:141
  90.8 4.7 %shard_map.86 = bf16[16,16,800]{2,1,0:T(8,128)(2,1)} custom-call(f32[2,128,128]{2,1,0:T(8,128)S(1)} %get-tuple-element.31.near, bf16[2,128,128]{2,1,0:T(8,128)(2,1)S(1)} %collective-permute-done.12.far, f32[256,800]{1,0:T(8,128)S(1)} %get-tuple-element.35.turned), custom_call_target="tpu_custom_call" | custom-call | tf_op jit(solution)/shard_map/pallas_call | solution.py:462
  95.5 4.7 %all-to-all-done = f16[16,16,800]{2,1,0:T(8,128)(2,1)S(1)} async-done(((f16[16,16,800]{2,1,0:T(8,128)(2,1)}), f16[16,16,800]{2,1,0:T(8,128)(2,1)S(1)}, u32[]{:S(2)}, u32[]{:S(2)}) %all-to-all-start) | async-done | bytes 409632 | tf_op jit(solution)/shard_map/all_to_all | solution.py:469
  100.2 4.2 %all-to-all-start.1 = ((bf16[16,16,800]{2,1,0:T(8,128)(2,1)}), bf16[16,16,800]{2,1,0:T(8,128)(2,1)S(1)}, u32[]{:S(2)}, u32[]{:S(2)}) async-start(bf16[16,16,800]{2,1,0:T(8,128)(2,1)} %shard_map.86), calls=%async_computation.1 | async-start | bytes 917504 | tf_op jit(solution)/shard_map/all_to_all | solution.py:469
  104.5 1.1 copy-done.9
  105.7 1.4 %shard_map.85 = f32[2,800,120]{2,1,0:T(8,128)} custom-call(f32[4,2,2,16,800]{4,3,2,1,0:T(8,128)S(1)} %convert.6.mixed_back, f32[2,800,120]{2,1,0:T(8,128)S(1)} %bitcast.38), custom_call_target="tpu_custom_call" | custom-call | flops 10000000000 | bytes 2000000 | tf_op jit(solution)/shard_map/pallas_call | solution.py:473
  107.0 10.4 %all-to-all-done.1 = bf16[16,16,800]{2,1,0:T(8,128)(2,1)S(1)} async-done(((bf16[16,16,800]{2,1,0:T(8,128)(2,1)}), bf16[16,16,800]{2,1,0:T(8,128)(2,1)S(1)}, u32[]{:S(2)}, u32[]{:S(2)}) %all-to-all-start.1) | async-done | bytes 409632 | tf_op jit(solution)/shard_map/all_to_all | solution.py:469
  117.4 1.2 %shard_map.87 = f32[2,800,120]{2,1,0:T(8,128)} custom-call(bf16[4,2,2,16,800]{4,3,2,1,0:T(8,128)(2,1)S(1)} %bitcast.32, f32[2,800,120]{2,1,0:T(8,128)S(1)} %bitcast.33), custom_call_target="tpu_custom_call" | custom-call | tf_op jit(solution)/shard_map/pallas_call | solution.py:479
  (28 shorter events, 0.3 us)
Async XLA Ops:
  0.6 1.6 %copy-start = (bf16[2,256,1920]{2,1,0:T(8,128)(2,1)S(1)}, bf16[2,256,1920]{2,1,0:T(8,128)(2,1)}, u32[]{:S(2)}) copy-start(bf16[2,256,1920]{2,1,0:T(8,128)(2,1)} %param.6) | copy-start | bytes 5898244
  3.1 6.7 %collective-permute-start.3 = (bf16[256,1920]{1,0:T(8,128)(2,1)S(1)}, bf16[256,1920]{1,0:T(8,128)(2,1)}, u32[]{:S(2)}, u32[]{:S(2)}) collective-permute-start(bf16[256,1920]{1,0:T(8,128)(2,1)S(1)} %dynamic-slice_bitcast_fusion.refs_0_), channel_id=1, source_target_pairs={{0,2},{2,0},{4,6},{6,4},{8,10},{10,8},{12,14},{14,12},{16,18},{18,... | collective-permute-start | bytes 2949128 | tf_op jit(solution)/shard_map/ppermute | solution.py:133
  3.2 14.4 %collective-permute-start.2 = (bf16[128,1920]{1,0:T(8,128)(2,1)}, bf16[128,1920]{1,0:T(8,128)(2,1)S(1)}, u32[]{:S(2)}, u32[]{:S(2)}) collective-permute-start(bf16[128,1920]{1,0:T(8,128)(2,1)} %dynamic-slice_bitcast_fusion.1), channel_id=1, source_target_pairs={{0,4},{2,6},{4,0},{6,2},{8,12},{10,14},{12,8},{14,10},{16,20},{18,... | collective-permute-start | bytes 1474568 | tf_op jit(solution)/shard_map/ppermute | solution.py:137
  6.5 1.1 copy-start.5
  7.7 1.1 copy-start.7
  14.0 1.0 copy-start.2
  15.0 18.5 %copy-start.6 = (bf16[2,256,800]{1,2,0:T(8,128)(2,1)S(1)}, bf16[2,256,800]{1,2,0:T(8,128)(2,1)}, u32[]{:S(2)}) copy-start(bf16[2,256,800]{1,2,0:T(8,128)(2,1)} %param.7) | copy-start | bytes 2457604
  15.0 18.5 %copy-start.8 = (f32[2,120,800]{1,2,0:T(8,128)S(1)}, f32[2,120,800]{1,2,0:T(8,128)}, u32[]{:S(2)}) copy-start(f32[2,120,800]{1,2,0:T(8,128)} %param.9) | copy-start | bytes 2304004
  17.6 3.4 %collective-permute-start.4 = (bf16[128,1920]{1,0:T(8,128)(2,1)S(1)}, bf16[128,1920]{1,0:T(8,128)(2,1)S(1)}, u32[]{:S(2)}, u32[]{:S(2)}) collective-permute-start(bf16[128,1920]{1,0:T(8,128)(2,1)S(1)} %collective-permute-done.2.refs_0_), channel_id=1, source_target_pairs={{0,2},{2,0},{4,6},{6,4},{8,10},{10,8},{12,14},{14,12},{16,18},{18,... | collective-permute-start | bytes 1474568 | tf_op jit(solution)/shard_map/ppermute | solution.py:133
  18.3 16.2 %collective-permute-start.1 = (bf16[800,384]{1,0:T(8,128)(2,1)}, bf16[800,384]{1,0:T(8,128)(2,1)S(1)}, u32[]{:S(2)}, u32[]{:S(2)}) collective-permute-start(bf16[800,384]{1,0:T(8,128)(2,1)} %shard_map.77), channel_id=1, source_target_pairs={{0,4},{2,6},{4,0},{6,2},{8,12},{10,14},{12,8},{14,10},{16,20},{18,... | collective-permute-start | bytes 1843208 | tf_op jit(solution)/shard_map/ppermute | solution.py:137
  19.7 12.6 %collective-permute-start.6 = (bf16[128,1920]{1,0:T(8,128)(2,1)S(1)}, bf16[128,1920]{1,0:T(8,128)(2,1)}, u32[]{:S(2)}, u32[]{:S(2)}) collective-permute-start(bf16[128,1920]{1,0:T(8,128)(2,1)S(1)} %collective-permute-done.2.refs_0_), channel_id=1, source_target_pairs={{0,1},{1,0},{2,3},{3,2},{4,5},{5,4},{6,7},{7,6},{8,9},{9,8},{10,11... | collective-permute-start | bytes 1474568 | tf_op jit(solution)/shard_map/ppermute | solution.py:141
  22.9 10.7 %copy-start.10 = (bf16[4,256,256]{2,1,0:T(8,128)(2,1)}, bf16[4,256,256]{2,1,0:T(8,128)(2,1)S(1)}, u32[]{:S(2)}) copy-start(bf16[4,256,256]{2,1,0:T(8,128)(2,1)S(1)} %shard_map.80.near) | copy-start | bytes 1572868
  32.4 2.9 %collective-permute-start.7 = (bf16[128,1920]{1,0:T(8,128)(2,1)}, bf16[128,1920]{1,0:T(8,128)(2,1)}, u32[]{:S(2)}, u32[]{:S(2)}) collective-permute-start(bf16[128,1920]{1,0:T(8,128)(2,1)} %collective-permute-done.6.refs_0_), channel_id=1, source_target_pairs={{0,2},{2,0},{4,6},{6,4},{8,10},{10,8},{12,14},{14,12},{16,18},{18,... | collective-permute-start | bytes 1474568 | tf_op jit(solution)/shard_map/ppermute | solution.py:133
  33.6 4.8 %collective-permute-start = (bf16[800,384]{1,0:T(8,128)(2,1)S(1)}, bf16[800,384]{1,0:T(8,128)(2,1)}, u32[]{:S(2)}, u32[]{:S(2)}) collective-permute-start(bf16[800,384]{1,0:T(8,128)(2,1)S(1)} %shard_map.78.ext0), channel_id=1, source_target_pairs={{0,2},{2,0},{4,6},{6,4},{8,10},{10,8},{12,14},{14,12},{16,18},{18,... | collective-permute-start | bytes 1843208 | tf_op jit(solution)/shard_map/ppermute | solution.py:133
  34.5 4.0 %copy-start.3 = (bf16[4,512,256]{2,1,0:T(8,128)(2,1)S(1)}, bf16[4,512,256]{2,1,0:T(8,128)(2,1)}, u32[]{:S(2)}) copy-start(bf16[4,512,256]{2,1,0:T(8,128)(2,1)} %copy-done.2) | copy-start | bytes 3145732
  34.5 4.0 %copy-start.11 = (bf16[4,256,256]{2,1,0:T(8,128)(2,1)S(1)}, bf16[4,256,256]{2,1,0:T(8,128)(2,1)}, u32[]{:S(2)}) copy-start(bf16[4,256,256]{2,1,0:T(8,128)(2,1)} %copy-done.10) | copy-start | bytes 1572868
  34.5 4.0 %collective-permute-start.5 = (bf16[800,384]{1,0:T(8,128)(2,1)S(1)}, bf16[800,384]{1,0:T(8,128)(2,1)S(1)}, u32[]{:S(2)}, u32[]{:S(2)}) collective-permute-start(bf16[800,384]{1,0:T(8,128)(2,1)S(1)} %collective-permute-done.1.ext2), channel_id=1, source_target_pairs={{0,2},{2,0},{4,6},{6,4},{8,10},{10,8},{12,14},{14,12},{16,18},{18,... | collective-permute-start | bytes 1843208 | tf_op jit(solution)/shard_map/ppermute | solution.py:133
  43.7 1.4 %copy-start.1 = (f32[2,800,256]{2,1,0:T(8,128)}, f32[2,800,256]{2,1,0:T(8,128)S(1)}, u32[]{:S(2)}) copy-start(f32[2,800,256]{2,1,0:T(8,128)S(1)} %get-tuple-element.26) | copy-start | bytes 4915204
  45.1 10.9 %collective-permute-start.8 = (f16[800,256]{1,0:T(8,128)(2,1)}, f16[800,256]{1,0:T(8,128)(2,1)S(1)}, u32[]{:S(2)}, u32[]{:S(2)}) collective-permute-start(f16[800,256]{1,0:T(8,128)(2,1)} %get-tuple-element.36), channel_id=1, source_target_pairs={{0,8},{2,10},{4,12},{6,14},{8,0},{10,2},{12,4},{14,6},{16,24},{18,... | collective-permute-start | bytes 1228808 | tf_op jit(solution)/shard_map/ppermute | solution.py:428
  46.4 17.6 %collective-permute-start.10 = (f16[800,256]{1,0:T(8,128)(2,1)}, f16[800,256]{1,0:T(8,128)(2,1)S(1)}, u32[]{:S(2)}, u32[]{:S(2)}) collective-permute-start(f16[800,256]{1,0:T(8,128)(2,1)} %get-tuple-element.37), channel_id=1, source_target_pairs={{0,16},{2,18},{4,20},{6,22},{24,8},{26,10},{28,12},{30,14},{1,17},... | collective-permute-start | bytes 1228808 | tf_op jit(solution)/shard_map/ppermute | solution.py:428
  50.6 13.4 %collective-permute-start.9 = (f16[800,256]{1,0:T(8,128)(2,1)}, f16[800,256]{1,0:T(8,128)(2,1)S(1)}, u32[]{:S(2)}, u32[]{:S(2)}) collective-permute-start(f16[800,256]{1,0:T(8,128)(2,1)} %get-tuple-element.37), channel_id=1, source_target_pairs={{8,16},{10,18},{12,20},{14,22},{16,8},{18,10},{20,12},{22,14},{9,1... | collective-permute-start | bytes 1228808 | tf_op jit(solution)/shard_map/ppermute | solution.py:428
  58.0 21.0 %collective-permute-start.11 = (f16[800,256]{1,0:T(8,128)(2,1)}, f16[800,256]{1,0:T(8,128)(2,1)}, u32[]{:S(2)}, u32[]{:S(2)}) collective-permute-start(f16[800,256]{1,0:T(8,128)(2,1)} %fusion), channel_id=1, source_target_pairs={{0,8},{2,10},{4,12},{6,14},{8,24},{10,26},{12,28},{14,30},{24,16},... | collective-permute-start | bytes 1228808 | tf_op jit(solution)/shard_map/ppermute | solution.py:428
  81.5 18.7 %all-to-all-start = ((f16[16,16,800]{2,1,0:T(8,128)(2,1)}), f16[16,16,800]{2,1,0:T(8,128)(2,1)S(1)}, u32[]{:S(2)}, u32[]{:S(2)}) async-start(f16[16,16,800]{2,1,0:T(8,128)(2,1)} %convert_element_type.43), calls=%async_computation | async-start | bytes 917504 | tf_op jit(solution)/shard_map/all_to_all | solution.py:469
  87.3 3.5 %collective-permute-start.12 = (bf16[2,128,128]{2,1,0:T(8,128)(2,1)S(1)}, bf16[2,128,128]{2,1,0:T(8,128)(2,1)S(1)}, u32[]{:S(2)}, u32[]{:S(2)}) collective-permute-start(bf16[2,128,128]{2,1,0:T(8,128)(2,1)S(1)} %get-tuple-element.34), channel_id=1, source_target_pairs={{0,1},{1,0},{2,3},{3,2},{4,5},{5,4},{6,7},{7,6},{8,9},{9,8},{10,11... | collective-permute-start | bytes 196616 | tf_op jit(solution)/shard_map/ppermute | solution.py:141
  100.2 17.2 %all-to-all-start.1 = ((bf16[16,16,800]{2,1,0:T(8,128)(2,1)}), bf16[16,16,800]{2,1,0:T(8,128)(2,1)S(1)}, u32[]{:S(2)}, u32[]{:S(2)}) async-start(bf16[16,16,800]{2,1,0:T(8,128)(2,1)} %shard_map.86), calls=%async_computation.1 | async-start | bytes 917504 | tf_op jit(solution)/shard_map/all_to_all | solution.py:469
  104.5 1.1 copy-start.9
  105.7 11.7 %copy-start.4 = (f32[2,120,800]{1,2,0:T(8,128)S(1)}, f32[2,120,800]{1,2,0:T(8,128)}, u32[]{:S(2)}) copy-start(f32[2,120,800]{1,2,0:T(8,128)} %param.10) | copy-start | bytes 2304004

commit v4 on v0

--- a/solution.py
+++ b/solution.py
@@ -1,8 +1,11 @@
+import functools
 import math
 
 import jax
 import jax.numpy as jnp
 from jax import lax
+from jax.experimental import pallas as pl
+from jax.experimental.pallas import tpu as pltpu
 from jax.sharding import PartitionSpec as P
 
 HEAD = 128
@@ -20,6 +23,18 @@
 weight_decay = 0.1
 norm_floor = 1e-07
 
+SIZE_Z, SIZE_Y, SIZE_C = 4, 2, 2
+GAIN = 1.0 + momentum_rate
+MIX = momentum_rate * momentum_rate / GAIN
+BF16 = jnp.bfloat16
+F32 = jnp.float32
+F16 = jnp.float16
+VMEM_BYTES = 20 * 1024 * 1024
+CHUNK_ORDERS = ((3, 2, 1, 0), (0, 2, 3, 1), (3, 1, 0, 2), (0, 1, 2, 3))
+CHUNK_STEPS = len(CHUNK_ORDERS[0])
+CHUNK_SENDS = 2
+NO_HEAD = -(1 << 20)
+
 
 def quintic(current, reduce_gram):
     for step_index in range(ITERS):
@@ -40,7 +55,7 @@
     return current
 
 
-def per_device(context, cotangent, tile_counts, momentum, weights):
+def row_plan(context, cotangent, tile_counts, momentum, weights):
     layers, tok_dev, all_rows = context.shape
     columns = cotangent.shape[2]
     shard_rows = momentum.shape[1]
@@ -105,6 +120,354 @@
     new_weights = weights - learn_rate * (weight_decay * weights + update_scale * update_rows)
     return (moment_new, new_weights)
 
+def dp_index(z, y, c):
+    return (z * SIZE_Y + y) * SIZE_C + c
+
+
+def all_chips():
+    return [(z, y, c) for z in range(SIZE_Z) for y in range(SIZE_Y) for c in range(SIZE_C)]
+
+
+def swap_core(value):
+    return lax.ppermute(value, "dp", [(dp_index(z, y, c), dp_index(z, y, 1 - c)) for z, y, c in all_chips()])
+
+
+def swap_y(value):
+    return lax.ppermute(value, "dp", [(dp_index(z, y, c), dp_index(z, 1 - y, c)) for z, y, c in all_chips()])
+
+
+def swap_x(value):
+    return lax.ppermute(value, "mp", [(0, 1), (1, 0)])
+
+
+def after(value, *earlier):
+    return lax.optimization_barrier((value, *earlier))[0]
+
+
+def contract(left, right, dims):
+    return lax.dot_general(left, right, (dims, ((), ())), preferred_element_type=F32)
+
+
+def ext_kernel(table, counts, cotangent, momentum, send_ref, keep_ref):
+    y = table[CHUNK_STEPS + 2]
+    tokens, rows = cotangent.shape[2], momentum.shape[2]
+    position = lax.broadcasted_iota(jnp.int32, (1, tokens), 1)
+    live = (position // TILE_TOK < counts[0]).astype(F32)
+    pad = jnp.zeros((send_ref.shape[0], HEAD - rows), BF16)
+    for layer, out_ref in ((1 - y, send_ref), (y, keep_ref)):
+        out_ref[:, :tokens] = (cotangent[layer].astype(F32) * live).astype(BF16)
+        out_ref[:, tokens:] = jnp.concatenate([mixed_part(momentum[layer]), pad], axis=1)
+
+
+def mixed_part(momentum):
+    return (momentum * (2.0 * MIX)).astype(BF16)
+
+
+def head_of(step, c, index):
+    head = step * 4 + c * 2 + index
+    return jnp.where(head < HEADS_WIN, head, NO_HEAD)
+
+
+def fill_lead(lead):
+    row = lax.broadcasted_iota(jnp.int32, lead.shape, 0)
+    lead[...] = row - HEADS_WIN * lax.broadcasted_iota(jnp.int32, lead.shape, 1)
+
+
+def slots(pieces, lead, chunk, c):
+    places = [(lead[...] == head_of(chunk, c, index)).astype(F32).astype(BF16) for index in range(2)]
+    tokens = jnp.concatenate([piece[...] for piece in pieces], axis=0)
+    return contract(tokens, jnp.concatenate(places, axis=1), ((1,), (0,))).astype(BF16)
+
+
+def momentum_places(table, chunk, sender_y, rows, value):
+    z, y, c = (table[CHUNK_STEPS + index] for index in range(1, 4))
+    local = lax.broadcasted_iota(jnp.int32, (HEAD, HEAD), 0)
+    lead = jnp.where(local < rows, local - HEADS_WIN * lax.broadcasted_iota(jnp.int32, (HEAD, HEAD), 1), 2 * NO_HEAD)
+    places = []
+    for sender_c in (c, 1 - c):
+        first_row = dp_index(z, sender_y, sender_c) * rows
+        hits = [lead + first_row == head_of(chunk, c, index) for index in range(2)]
+        hits = jnp.concatenate([jnp.where(hit, value, 0.0) for hit in hits], axis=1)
+        places.append(hits.astype(BF16))
+    return jnp.concatenate(places, axis=0)
+
+
+def near_kernel(table, first, second, out_ref, lead):
+    fill_lead(lead)
+    for chunk in range(SIZE_Z):
+        out_ref[chunk] = slots((first, second), lead, chunk, table[CHUNK_STEPS + 3])
+
+
+def own_kernel(table, ctx0, ctx1, ext0, ext1, out_ref, lead, *, factor, rows):
+    y, c = table[CHUNK_STEPS + 2], table[CHUNK_STEPS + 3]
+    tokens = ctx0.shape[0]
+    fill_lead(lead)
+    for step in range(CHUNK_STEPS):
+        chunk = table[step]
+        own = slots((ctx0, ctx1), lead, chunk, c)
+        total = contract(ext0[:, :tokens], own[:tokens], ((1,), (0,)))
+        total += contract(ext1[:, :tokens], own[tokens:], ((1,), (0,)))
+        mixed_in = jnp.concatenate([ext0[:, tokens:], ext1[:, tokens:]], axis=1)
+        total += contract(mixed_in, momentum_places(table, chunk, y, rows, 0.5 / factor), ((1,), (0,)))
+        out_ref[step] = total
+
+
+def chunk_kernel(table, ext2, ext3, near, far0, far1, own, send_ref, keep_ref, lead, *, factor, rows):
+    x, y, c = table[CHUNK_STEPS], table[CHUNK_STEPS + 2], table[CHUNK_STEPS + 3]
+    half = far0.shape[0]
+    tokens = 2 * half
+    fill_lead(lead)
+    for step in range(CHUNK_STEPS):
+        chunk = table[step]
+        far = slots((far0, far1), lead, chunk, c)
+        total = own[step]
+        for source, ext in enumerate((ext2, ext3)):
+            here = near[chunk, source * half : (source + 1) * half]
+            there = far[source * half : (source + 1) * half]
+            low = jnp.where(x == 0, here, there)
+            high = jnp.where(x == 0, there, here)
+            total += contract(ext[:, :tokens], jnp.concatenate([low, high], axis=0), ((1,), (0,)))
+        mixed_in = jnp.concatenate([ext2[:, tokens:], ext3[:, tokens:]], axis=1)
+        total += contract(mixed_in, momentum_places(table, chunk, 1 - y, rows, 0.5 / factor), ((1,), (0,)))
+        if step < CHUNK_SENDS:
+            send_ref[step] = total * factor
+        else:
+            keep_ref[step - CHUNK_SENDS] = total * factor
+
+
+def gram_kernel(mixed, near_ref, far_ref):
+    for head in range(2):
+        block = (GAIN * mixed[:, head * HEAD : (head + 1) * HEAD]).astype(BF16)
+        total = contract(block, block, ((0,), (0,)))
+        near_ref[head] = total
+        far_ref[head] = total.astype(BF16)
+
+
+def turn_kernel(mixed, turned_ref, owner_ref):
+    value = mixed[...].T
+    turned_ref[...] = value
+    store_by_owner(owner_ref, [value[:HEAD], value[HEAD:]])
+
+
+def store_by_owner(owner_ref, blocks):
+    owners = owner_ref.shape[0]
+    depth = HEAD // owners
+    for owner in range(owners):
+        rows = [block[owner * depth : (owner + 1) * depth] for block in blocks]
+        owner_ref[owner] = jnp.concatenate(rows, axis=0).astype(owner_ref.dtype)
+
+
+def square_dot(left, right):
+    return jnp.dot(left, right, precision=lax.Precision.HIGHEST, preferred_element_type=F32)
+
+
+def ortho_kernel(near, far, turned, out_ref):
+    row = lax.broadcasted_iota(jnp.int32, (HEAD, HEAD), 0)
+    column = lax.broadcasted_iota(jnp.int32, (HEAD, HEAD), 1)
+    eye = (row == column).astype(F32)
+    heads = range(2)
+    raws = [near[head] + far[head].astype(F32) for head in heads]
+    scales = [1.0 / (jnp.sqrt(jnp.sum(raw * eye, axis=(0, 1), keepdims=True)) + norm_floor) for raw in raws]
+    grams = [raw * (scale * scale) for raw, scale in zip(raws, scales)]
+    totals = None
+    for step in range(ITERS):
+        squares = [square_dot(gram, gram) for gram in grams]
+        factors = [quintic_a * eye + quintic_b * gram + quintic_c * square for gram, square in zip(grams, squares)]
+        totals = [square_dot(f, t) for f, t in zip(factors, totals)] if totals else factors
+        if step + 1 < ITERS:
+            grams = [square_dot(f, gram) for f, gram in zip(factors, grams)]
+            grams = [square_dot(gram, f) for f, gram in zip(factors, grams)]
+    blocks = []
+    for head in heads:
+        total = totals[head] * scales[head]
+        high = total.astype(BF16)
+        low = (total - high.astype(F32)).astype(BF16)
+        block = (GAIN * turned[head * HEAD : (head + 1) * HEAD]).astype(BF16)
+        blocks.append(contract(high, block, ((1,), (0,))) + contract(low, block, ((1,), (0,))))
+    store_by_owner(out_ref, blocks)
+
+
+def to_rows(pieces):
+    depth = pieces[0].shape[0] // 2
+    value = jnp.concatenate(pieces, axis=0)
+    row = lax.broadcasted_iota(jnp.int32, (value.shape[0], HEAD), 0)
+    col = lax.broadcasted_iota(jnp.int32, (value.shape[0], HEAD), 1)
+    order = (col == row % depth * HEADS_WIN + row // depth) & (row // depth < HEADS_WIN)
+    order = order.astype(F32).astype(BF16)
+    high = value.astype(BF16)
+    result = contract(high, order, ((0,), (0,)))
+    if value.dtype == F32:
+        result += contract((value - high.astype(F32)).astype(BF16), order, ((0,), (0,)))
+    return result
+
+
+def momentum_kernel(here, mixed_back, momentum, out_ref):
+    z, y, c = (here[index] for index in range(3))
+    for layer in range(2):
+        old = momentum[layer]
+        pieces = [
+            mixed_back[(y ^ layer) * SIZE_C + (c ^ core), z ^ chip] for chip in range(SIZE_Z) for core in range(SIZE_C)
+        ]
+        gradient = to_rows(pieces)[:, : old.shape[1]] - 0.5 * mixed_part(old).astype(F32)
+        out_ref[layer] = momentum_rate * old + gradient
+
+
+def weights_kernel(ortho_back, weights, out_ref, *, update_scale):
+    for layer in range(2):
+        old = weights[layer]
+        pieces = [ortho_back[chip, layer, core] for chip in range(SIZE_Z) for core in range(SIZE_C)]
+        update = to_rows(pieces)[:, : old.shape[1]]
+        out_ref[layer] = old - learn_rate * (weight_decay * old + update_scale * update)
+
+
+def vmem_params(**kwargs):
+    return pltpu.CompilerParams(vmem_limit_bytes=VMEM_BYTES, **kwargs)
+
+
+def block_plan(context, cotangent, tile_counts, momentum, weights):
+    layers, tok_dev, all_rows = context.shape
+    columns = cotangent.shape[2]
+    shard_rows = momentum.shape[1]
+    depth = shard_rows // HEADS_WIN
+    half = tok_dev // 2
+    where = lax.axis_index("dp")
+    z, y, c = where // (SIZE_Y * SIZE_C), where // SIZE_C % SIZE_Y, where % SIZE_C
+    x = lax.axis_index("mp")
+    factor = 1.0 / math.sqrt(tok_dev * lax.axis_size("dp"))
+
+    half_send = lax.dynamic_slice(context, (1 - y, x * half, 0), (1, half, all_rows))[0]
+    first0 = swap_y(half_send)
+
+    cotangent_t = jnp.transpose(cotangent, (0, 2, 1))
+    momentum_t = jnp.transpose(momentum, (0, 2, 1))
+    weights_t = jnp.transpose(weights, (0, 2, 1))
+    wide = tok_dev + HEAD
+
+    table = lax.dynamic_index_in_dim(jnp.array(CHUNK_ORDERS, jnp.int32), z, 0, False)
+    table = jnp.concatenate([table, jnp.stack([x, z, y, c])])
+    smem, vmem = pl.BlockSpec(memory_space=pltpu.SMEM), pl.BlockSpec(memory_space=pltpu.VMEM)
+    ext_send, ext_keep = pl.pallas_call(
+        ext_kernel,
+        in_specs=[smem, smem, vmem, vmem],
+        out_shape=[jax.ShapeDtypeStruct((columns, wide), BF16)] * 2,
+        compiler_params=vmem_params(),
+        cost_estimate=pl.CostEstimate(flops=10**10, bytes_accessed=2 * 10**6, transcendentals=0),
+    )(after(table, half_send), tile_counts, cotangent_t, momentum_t)
+    ext2 = swap_y(ext_send)
+    ctx_keep = lax.dynamic_index_in_dim(context, after(y, half_send), 0, False)
+    ctx1 = swap_core(ctx_keep)
+    ext1 = swap_core(ext_keep)
+
+    lanes = 2 * HEAD
+
+    def planned(kernel, out_shape, *args):
+        return pl.pallas_call(
+            kernel,
+            in_specs=[smem] + [vmem] * len(args),
+            out_shape=out_shape,
+            scratch_shapes=[pltpu.VMEM((all_rows, HEAD), jnp.int32)],
+            compiler_params=vmem_params(),
+            cost_estimate=pl.CostEstimate(flops=10**3, bytes_accessed=10**3, transcendentals=0),
+        )(table, *args)
+
+    def chunks(count):
+        return jax.ShapeDtypeStruct((count, columns, lanes), F32)
+
+    first0 = after(first0, ext_keep, table)
+    second0 = swap_x(first0)
+    first1 = swap_core(first0)
+    own = planned(
+        functools.partial(own_kernel, factor=factor, rows=shard_rows),
+        chunks(CHUNK_STEPS),
+        after(ctx_keep, first0),
+        ctx1,
+        ext_keep,
+        ext1,
+    )
+    near = planned(near_kernel, jax.ShapeDtypeStruct((SIZE_Z, tok_dev, lanes), BF16), first0, first1)
+    second0 = after(second0, near, own)
+    second1 = swap_core(second0)
+    ext2 = after(ext2, near, own)
+    ext3 = swap_core(ext2)
+    send, keep = planned(
+        functools.partial(chunk_kernel, factor=factor, rows=shard_rows),
+        [chunks(CHUNK_SENDS), chunks(CHUNK_STEPS - CHUNK_SENDS)],
+        ext2,
+        ext3,
+        near,
+        second0,
+        second1,
+        own,
+    )
+
+    def along_z(value, pairs):
+        pairs = [(dp_index(p, b, a), dp_index(q, b, a)) for p, q in pairs for b in range(SIZE_Y) for a in range(SIZE_C)]
+        return lax.ppermute(value, "dp", pairs)
+
+    def only(condition, value):
+        return jnp.where(condition, value.astype(F32), jnp.zeros((), F32))
+
+    sent = send.astype(F16)
+    pair = along_z(sent[0], [(0, 1), (1, 0), (2, 3), (3, 2)])
+    inner = along_z(sent[1], [(1, 2), (2, 1)])
+    outer = along_z(sent[1], [(0, 2), (3, 1)])
+    middle = (z == 1) | (z == 2)
+    merged = (keep[0] + only(middle, pair)).astype(F16)
+    last = along_z(merged, [(0, 1), (1, 3), (3, 2), (2, 0)])
+    base = keep[1] + only(~middle, after(pair, merged)) + (outer.astype(F32) + inner.astype(F32))
+    base, last = lax.optimization_barrier((base, last))
+    mixed = base + last.astype(F32)
+
+    owners = lax.axis_size("dp")
+    by_owner = (owners, 2 * depth, columns)
+    gram, gram_send = pl.pallas_call(
+        gram_kernel,
+        out_shape=[jax.ShapeDtypeStruct((2, HEAD, HEAD), kind) for kind in (F32, BF16)],
+        compiler_params=vmem_params(),
+    )(mixed)
+    gram_far = swap_x(gram_send)
+    turned, mixed_send = pl.pallas_call(
+        turn_kernel,
+        out_shape=[jax.ShapeDtypeStruct((lanes, columns), F32), jax.ShapeDtypeStruct(by_owner, F32)],
+        compiler_params=vmem_params(),
+        cost_estimate=pl.CostEstimate(flops=10**10, bytes_accessed=2 * 10**6, transcendentals=0),
+    )(after(mixed, gram))
+    ortho_send = pl.pallas_call(
+        ortho_kernel,
+        out_shape=jax.ShapeDtypeStruct(by_owner, BF16),
+        compiler_params=vmem_params(),
+    )(gram, gram_far, turned)
+
+    mixed_send = mixed_send.astype(F16).reshape(SIZE_Z, SIZE_Y * SIZE_C, 2 * depth, columns)
+    arrived = []
+    for apart in range(SIZE_Z):
+        piece = lax.dynamic_index_in_dim(mixed_send, z ^ apart, 0, False)
+        arrived.append(along_z(piece, [(k, k ^ apart) for k in range(SIZE_Z)]) if apart else piece)
+    mixed_back = []
+    for apart in range(SIZE_Y * SIZE_C):
+        mine = (y * SIZE_C + c) ^ apart
+        piece = jnp.stack([lax.dynamic_index_in_dim(value, mine, 0, False) for value in arrived])
+        if apart:
+            piece = lax.ppermute(piece, "dp", [(k, k ^ apart) for k in range(owners)])
+        mixed_back.append(piece)
+    mixed_back = jnp.stack(mixed_back).astype(F32)
+
+    out = jax.ShapeDtypeStruct((layers, columns, shard_rows), F32)
+    moment_new = pl.pallas_call(
+        momentum_kernel,
+        in_specs=[smem, vmem, vmem],
+        out_shape=out,
+        compiler_params=vmem_params(),
+        cost_estimate=pl.CostEstimate(flops=10**10, bytes_accessed=2 * 10**6, transcendentals=0),
+    )(jnp.stack([z, y, c]), mixed_back, momentum_t)
+    ortho_back = lax.all_to_all(ortho_send, "dp", 0, 0).reshape(SIZE_Z, SIZE_Y, SIZE_C, 2 * depth, columns)
+    new_weights = pl.pallas_call(
+        functools.partial(weights_kernel, update_scale=0.2 * math.sqrt(max(HEAD, COLS))),
+        out_shape=out,
+        compiler_params=vmem_params(),
+    )(ortho_back, weights_t)
+    return jnp.transpose(moment_new, (0, 2, 1)), jnp.transpose(new_weights, (0, 2, 1))
+
 
 def solution(mesh):
     in_specs = (
@@ -115,6 +478,7 @@
         P(None, "dp", "mp"),
     )
     out_specs = (P(None, "dp", "mp"), P(None, "dp", "mp"))
+    small = mesh.shape["dp"] == SIZE_Z * SIZE_Y * SIZE_C and mesh.shape["mp"] == 2
     return jax.shard_map(
-        per_device, mesh=mesh, in_specs=in_specs, out_specs=out_specs, check_vma=False
-    )
+        block_plan if small else row_plan, mesh=mesh, in_specs=in_specs, out_specs=out_specs, check_vma=False
+    )

time: 562 us -> 105 us (0.19)
  waiting for transfers between devices: 411 us -> 37 us
  matrix products: 61.6 us -> 0 us
  local copies, waits for them, and re-layouts: 55.4 us -> 6.93 us
  starting transfers between devices: 0.39 us -> 31.5 us
  Pallas kernels: 0 us -> 22.1 us
  between operations: 15.3 us -> 1.64 us
  other arithmetic: 12.4 us -> 4.97 us
    unnamed x6 -> x0, waiting for transfers between devices: 231 us -> none
    psum x3 -> x0, waiting for transfers between devices: 115 us -> none  [per_device(): lax.psum(partial_value.astype(jnp.bfloat16), 'mp').astype(jnp.float32)]
    all_gather x1 -> x0, waiting for transfers between devices: 65.6 us -> none  [per_device(): gathered = lax.all_gather(nesterov, 'dp', axis=1, tiled=True)]
    dot_general x8 -> x0, matrix products: 61.6 us -> none  [the longest x3 34.8 us: quintic(): jnp.einsum('lshg,lsgc->lshc', poly_term, current, preferred_element_type=...]
    ppermute x0 -> x19, waiting for transfers between devices: none -> 37 us  [the longest x7 20.3 us: along_z(): return lax.ppermute(value, 'dp', pairs)]
    reshape x2 -> x0, local copies, waits for them, and re-layouts: 25.5 us -> none  [the longest x1 18.5 us: per_device(): orthogonal.reshape(layers, slots * HEAD, columns)]
    ppermute x0 -> x19, starting transfers between devices: none -> 24.3 us  [the longest x7 12.7 us: along_z(): return lax.ppermute(value, 'dp', pairs)]
    pallas_call x0 -> x9, Pallas kernels: none -> 22.1 us  [the longest x3 14.3 us: planned(): pl.pallas_call(kernel, in_specs=[smem] + [vmem] * len(args), out_shape=ou...]
  transfers between devices with their start and end apart: 5 -> 20, of which waited for: 5 -> 8; matrix products, arithmetic and copies ran while one was open for 0% -> 5% of each run, Pallas kernels for 0% -> 16%
where the time goes in v4:
time: 105 us; the launch traced here: 104 us
  waiting for transfers between devices  37 us (35%)
  starting transfers between devices  31.5 us (30%)
  Pallas kernels  22.1 us (21%)
  local copies, waits for them, and re-layouts  6.93 us (7%)
  other arithmetic  4.97 us (5%)
  between operations  1.64 us (2%)
    ppermute x7, waiting for transfers between devices, along_z(): return lax.ppermute(value, 'dp', pairs)  20.3 us
    pallas_call x3, Pallas kernels, planned(): pl.pallas_call(kernel, in_specs=[smem] + [vmem] * len(args), out_shape=ou...  14.3 us
    ppermute x7, starting transfers between devices, along_z(): return lax.ppermute(value, 'dp', pairs)  12.7 us
    ppermute x3, waiting for transfers between devices, block_plan(): piece = lax.ppermute(piece, 'dp', [(k, k ^ apart) for k in range(owners)])  9.04 us
    all_to_all x1, starting transfers between devices, block_plan(): lax.all_to_all(ortho_send, 'dp', 0, 0)  7.19 us
    ppermute x2, waiting for transfers between devices, swap_y(): lax.ppermute(value, 'dp', [(dp_index(z, y, c), dp_index(z, 1 - y, c)) for...  5.4 us
    ppermute x5, starting transfers between devices, swap_core(): lax.ppermute(value, 'dp', [(dp_index(z, y, c), dp_index(z, y, 1 - c)) for...  4.12 us
    unnamed x12, local copies, waits for them, and re-layouts  3.8 us
  transfers between devices with their start and end apart: 20, of which 8 were waited for; matrix products, arithmetic and copies ran while one was open for 5% of the time, Pallas kernels for 16%

profile of v4, /device:TPU:1, one launch (start us, length us, event | category | flops | bytes accessed | tf_op | source)
XLA Modules:
  0.0 104.1 jit_solution(8927214286250541131)
XLA Ops:
  0.7 1.5 %copy-done = bf16[2,256,1920]{2,1,0:T(8,128)(2,1)S(1)} copy-done((bf16[2,256,1920]{2,1,0:T(8,128)(2,1)S(1)}, bf16[2,256,1920]{2,1,0:T(8,128)(2,1)}, u32[]{:S(2)}) %copy-start) | copy-done | bytes 1966104
  2.2 0.8 dynamic-slice_bitcast_fusion.1
  3.0 2.1 %collective-permute-start.1 = (bf16[128,1920]{1,0:T(8,128)(2,1)}, bf16[128,1920]{1,0:T(8,128)(2,1)S(1)}, u32[]{:S(2)}, u32[]{:S(2)}) collective-permute-start(bf16[128,1920]{1,0:T(8,128)(2,1)} %dynamic-slice_bitcast_fusion.1), channel_id=1, source_target_pairs={{0,4},{2,6},{4,0},{6,2},{8,12},{10,14},{12,8},{14,10},{16,20},{18,... | collective-permute-start | bytes 1474568 | tf_op jit(solution)/shard_map/ppermute | solution.py:136
  5.1 1.0 collective-permute-start.3
  6.2 0.7 fusion.2
  6.8 0.1 concatenate.3.table
  7.6 1.1 %copy-done.3 = bf16[2,256,800]{1,2,0:T(8,128)(2,1)S(1)} copy-done((bf16[2,256,800]{1,2,0:T(8,128)(2,1)S(1)}, bf16[2,256,800]{1,2,0:T(8,128)(2,1)}, u32[]{:S(2)}) %copy-start.3) | copy-done | bytes 819224
  8.7 1.1 %copy-done.4 = f32[2,120,800]{1,2,0:T(8,128)S(1)} copy-done((f32[2,120,800]{1,2,0:T(8,128)S(1)}, f32[2,120,800]{1,2,0:T(8,128)}, u32[]{:S(2)}) %copy-start.4) | copy-done | bytes 768024
  9.9 0.8 shard_map.77
  10.7 0.1 collective-permute-start.4
  10.8 5.4 %collective-permute-done.1.first = bf16[128,1920]{1,0:T(8,128)(2,1)S(1)} collective-permute-done((bf16[128,1920]{1,0:T(8,128)(2,1)}, bf16[128,1920]{1,0:T(8,128)(2,1)S(1)}, u32[]{:S(2)}, u32[]{:S(2)}) %collective-permute-start.1) | collective-permute-done | bytes 491552 | tf_op jit(solution)/shard_map/ppermute | solution.py:136
  16.2 2.1 %collective-permute-start.2 = (bf16[128,1920]{1,0:T(8,128)(2,1)S(1)}, bf16[128,1920]{1,0:T(8,128)(2,1)S(1)}, u32[]{:S(2)}, u32[]{:S(2)}) collective-permute-start(bf16[128,1920]{1,0:T(8,128)(2,1)S(1)} %collective-permute-done.1.first), channel_id=1, source_target_pairs={{0,2},{2,0},{4,6},{6,4},{8,10},{10,8},{12,14},{14,12},{16,18},{18,... | collective-permute-start | bytes 1474568 | tf_op jit(solution)/shard_map/ppermute | solution.py:132
  18.3 1.8 %collective-permute-start.6 = (bf16[128,1920]{1,0:T(8,128)(2,1)S(1)}, bf16[128,1920]{1,0:T(8,128)(2,1)S(1)}, u32[]{:S(2)}, u32[]{:S(2)}) collective-permute-start(bf16[128,1920]{1,0:T(8,128)(2,1)S(1)} %collective-permute-done.1.first), channel_id=1, source_target_pairs={{0,1},{1,0},{2,3},{3,2},{4,5},{5,4},{6,7},{7,6},{8,9},{9,8},{10,11... | collective-permute-start | bytes 1474568 | tf_op jit(solution)/shard_map/ppermute | solution.py:140
  20.0 1.8 %shard_map.78.near = bf16[4,256,256]{2,1,0:T(8,128)(2,1)S(1)} custom-call(s32[8]{0:T(128)S(1)} %concatenate.3.table, bf16[128,1920]{1,0:T(8,128)(2,1)S(1)} %collective-permute-done.1.first, bf16[128,1920]{1,0:T(8,128)(2,1)S(1)} %collective-permute-done.2.second), custom_call_target="tpu_custom_call" | custom-call | flops 1000 | bytes 1000 | tf_op jit(solution)/shard_map/pallas_call | solution.py:364
  21.8 8.7 %shard_map.79.own = f32[4,800,256]{2,1,0:T(8,128)S(1)} custom-call(s32[8]{0:T(128)S(1)} %concatenate.3.table, bf16[256,1920]{1,0:T(8,128)(2,1)S(1)} %dynamic-slice_bitcast_fusion.ctx0, bf16[256,1920]{1,0:T(8,128)(2,1)} %collective-permute-done.3.ctx1, bf16[800,384]{1,0:T(8,128)(2,1)S(1)} %get-tuple-element.22.ext0, ...), custom_call_target="tpu_custom_call" | custom-call | flops 1000 | bytes 1000 | tf_op jit(solution)/shard_map/pallas_call | solution.py:364
  30.5 0.4 collective-permute-start.5
  30.9 0.7 collective-permute-done.6.far0
  31.6 0.6 collective-permute-start.7
  32.2 1.5 %collective-permute-done.7.far1 = bf16[128,1920]{1,0:T(8,128)(2,1)S(1)} collective-permute-done((bf16[128,1920]{1,0:T(8,128)(2,1)S(1)}, bf16[128,1920]{1,0:T(8,128)(2,1)S(1)}, u32[]{:S(2)}, u32[]{:S(2)}) %collective-permute-start.7) | collective-permute-done | bytes 491552 | tf_op jit(solution)/shard_map/ppermute | solution.py:132
  33.7 3.8 %shard_map.80 = (f32[2,800,256]{2,1,0:T(8,128)S(1)}, f32[2,800,256]{2,1,0:T(8,128)S(1)}) custom-call(s32[8]{0:T(128)S(1)} %concatenate.3.table, bf16[800,384]{1,0:T(8,128)(2,1)S(1)} %collective-permute-done.ext2, bf16[800,384]{1,0:T(8,128)(2,1)S(1)} %collective-permute-done.5.ext3, bf16[4,256,256]{2,1,0:T(8,128)(2,1)S(1)} %shard_map.78.near, ...), custom_call_target="tpu_custom_call" | custom-call | flops 1000 | bytes 1000 | tf_op jit(solution)/shard_map/pallas_call | solution.py:364
  37.6 0.1 convert_element_type.27
  37.7 1.3 %slice_bitcast_fusion.1 = (f16[800,256]{1,0:T(8,128)(2,1)}, f16[800,256]{1,0:T(8,128)(2,1)}) fusion(f16[2,800,256]{2,1,0:T(8,128)(2,1)S(1)} %convert_element_type.27), kind=kLoop, calls=%fused_computation.9 | loop fusion | bytes 1638400 | tf_op jit(solution)/shard_map/squeeze | solution.py:411
  39.0 1.5 %collective-permute-start.8 = (f16[800,256]{1,0:T(8,128)(2,1)}, f16[800,256]{1,0:T(8,128)(2,1)S(1)}, u32[]{:S(2)}, u32[]{:S(2)}) collective-permute-start(f16[800,256]{1,0:T(8,128)(2,1)} %get-tuple-element.38), channel_id=1, source_target_pairs={{0,8},{2,10},{4,12},{6,14},{8,0},{10,2},{12,4},{14,6},{16,24},{18,... | collective-permute-start | bytes 1228808 | tf_op jit(solution)/shard_map/ppermute | solution.py:405
  40.5 0.7 collective-permute-start.10
  41.2 5.5 %collective-permute-start.9 = (f16[800,256]{1,0:T(8,128)(2,1)}, f16[800,256]{1,0:T(8,128)(2,1)S(1)}, u32[]{:S(2)}, u32[]{:S(2)}) collective-permute-start(f16[800,256]{1,0:T(8,128)(2,1)} %get-tuple-element.39), channel_id=1, source_target_pairs={{0,16},{2,18},{4,20},{6,22},{24,8},{26,10},{28,12},{30,14},{1,17},... | collective-permute-start | bytes 1228808 | tf_op jit(solution)/shard_map/ppermute | solution.py:405
  46.7 3.3 %collective-permute-done.8 = f16[800,256]{1,0:T(8,128)(2,1)S(1)} collective-permute-done((f16[800,256]{1,0:T(8,128)(2,1)}, f16[800,256]{1,0:T(8,128)(2,1)S(1)}, u32[]{:S(2)}, u32[]{:S(2)}) %collective-permute-start.8) | collective-permute-done | bytes 409632 | tf_op jit(solution)/shard_map/ppermute | solution.py:405
  50.0 2.0 %fusion = f16[800,256]{1,0:T(8,128)(2,1)} fusion(f16[800,256]{1,0:T(8,128)(2,1)S(1)} %collective-permute-done.8, f32[2,800,256]{2,1,0:T(8,128)} %copy-done.1, pred[]{:T(512)S(6)} %or.3), kind=kLoop, calls=%fused_computation.2 | loop fusion | flops 819200 | bytes 1638401 | tf_op jit(solution)/shard_map/convert_element_type | solution.py:415
  52.1 1.4 %collective-permute-start.11 = (f16[800,256]{1,0:T(8,128)(2,1)}, f16[800,256]{1,0:T(8,128)(2,1)}, u32[]{:S(2)}, u32[]{:S(2)}) collective-permute-start(f16[800,256]{1,0:T(8,128)(2,1)} %fusion), channel_id=1, source_target_pairs={{0,8},{2,10},{4,12},{6,14},{8,24},{10,26},{12,28},{14,30},{24,16},... | collective-permute-start | bytes 1228808 | tf_op jit(solution)/shard_map/ppermute | solution.py:405
  53.4 0.1 pad_add_fusion.here
  53.5 4.6 %collective-permute-done.9 = f16[800,256]{1,0:T(8,128)(2,1)S(1)} collective-permute-done((f16[800,256]{1,0:T(8,128)(2,1)}, f16[800,256]{1,0:T(8,128)(2,1)S(1)}, u32[]{:S(2)}, u32[]{:S(2)}) %collective-permute-start.9) | collective-permute-done | bytes 409632 | tf_op jit(solution)/shard_map/ppermute | solution.py:405
  58.1 1.3 %fusion.1 = f32[800,256]{1,0:T(8,128)S(1)} fusion(f16[800,256]{1,0:T(8,128)(2,1)S(1)} %collective-permute-done.10, f16[800,256]{1,0:T(8,128)(2,1)S(1)} %collective-permute-done.9, f16[800,256]{1,0:T(8,128)(2,1)S(1)} %collective-permute-done.8, f32[2,800,256]{2,1,0:T(8,128)} %copy-done.1, pred[]{:T(512)S(6)} %not.3), kind=kLoop, calls=%fused_computation.4 | loop fusion | flops 1433600 | bytes 2867201 | tf_op jit(solution)/shard_map/add | solution.py:417
  59.5 12.3 %collective-permute-done.11 = f16[800,256]{1,0:T(8,128)(2,1)} collective-permute-done((f16[800,256]{1,0:T(8,128)(2,1)}, f16[800,256]{1,0:T(8,128)(2,1)}, u32[]{:S(2)}, u32[]{:S(2)}) %collective-permute-start.11) | collective-permute-done | bytes 409632 | tf_op jit(solution)/shard_map/ppermute | solution.py:405
  71.8 1.1 %convert_add_fusion.mixed = f32[800,256]{1,0:T(8,128)S(1)} fusion(f32[800,256]{1,0:T(8,128)S(1)} %fusion.1, f16[800,256]{1,0:T(8,128)(2,1)} %collective-permute-done.11), kind=kLoop, calls=%fused_computation.5 | loop fusion | flops 409600 | bytes 2048000 | tf_op jit(solution)/shard_map/add | solution.py:419
  72.9 0.3 shard_map.81
  73.2 0.3 shard_map.82
  73.5 1.3 %collective-permute-start.18 = (bf16[2,128,128]{2,1,0:T(8,128)(2,1)S(1)}, bf16[2,128,128]{2,1,0:T(8,128)(2,1)S(1)}, u32[]{:S(2)}, u32[]{:S(2)}) collective-permute-start(bf16[2,128,128]{2,1,0:T(8,128)(2,1)S(1)} %get-tuple-element.36), channel_id=1, source_target_pairs={{0,1},{1,0},{2,3},{3,2},{4,5},{5,4},{6,7},{7,6},{8,9},{9,8},{10,11... | collective-permute-start | bytes 196616 | tf_op jit(solution)/shard_map/ppermute | solution.py:140
  75.0 2.3 %collective-permute-start.13 = (f16[4,16,800]{2,1,0:T(8,128)(2,1)S(1)}, f16[4,16,800]{2,1,0:T(8,128)(2,1)S(1)}, u32[]{:S(2)}, u32[]{:S(2)}) collective-permute-start(f16[4,16,800]{2,1,0:T(8,128)(2,1)S(1)} %get-tuple-element.46), channel_id=1, source_target_pairs={{0,16},{2,18},{4,20},{6,22},{8,24},{10,26},{12,28},{14,30},{16,0},... | collective-permute-start | bytes 307208 | tf_op jit(solution)/shard_map/ppermute | solution.py:405
  77.3 1.2 %collective-permute-start.14 = (f16[4,16,800]{2,1,0:T(8,128)(2,1)S(1)}, f16[4,16,800]{2,1,0:T(8,128)(2,1)S(1)}, u32[]{:S(2)}, u32[]{:S(2)}) collective-permute-start(f16[4,16,800]{2,1,0:T(8,128)(2,1)S(1)} %get-tuple-element.45), channel_id=1, source_target_pairs={{0,24},{2,26},{4,28},{6,30},{8,16},{10,18},{12,20},{14,22},{16,8},... | collective-permute-start | bytes 307208 | tf_op jit(solution)/shard_map/ppermute | solution.py:405
  78.6 3.3 %shard_map.84 = bf16[16,16,800]{2,1,0:T(8,128)(2,1)} custom-call(f32[2,128,128]{2,1,0:T(8,128)S(1)} %get-tuple-element.33.near, bf16[2,128,128]{2,1,0:T(8,128)(2,1)S(1)} %collective-permute-done.18.far, f32[256,800]{1,0:T(8,128)S(1)} %get-tuple-element.37.turned), custom_call_target="tpu_custom_call" | custom-call | tf_op jit(solution)/shard_map/pallas_call | solution.py:435
  81.9 7.2 %all-to-all-start = ((bf16[16,16,800]{2,1,0:T(8,128)(2,1)}), bf16[16,16,800]{2,1,0:T(8,128)(2,1)S(1)}, u32[]{:S(2)}, u32[]{:S(2)}) async-start(bf16[16,16,800]{2,1,0:T(8,128)(2,1)} %shard_map.84), calls=%async_computation | async-start | bytes 917504 | tf_op jit(solution)/shard_map/all_to_all | solution.py:463
  89.3 0.2 collective-permute-start.15
  89.5 1.7 %collective-permute-start.16 = (f16[4,16,800]{2,1,0:T(8,128)(2,1)S(1)}, f16[4,16,800]{2,1,0:T(8,128)(2,1)S(1)}, u32[]{:S(2)}, u32[]{:S(2)}) collective-permute-start(f16[4,16,800]{2,1,0:T(8,128)(2,1)S(1)} %pad_maximum_fusion.1), channel_id=1, source_target_pairs={{0,4},{2,6},{4,0},{6,2},{8,12},{10,14},{12,8},{14,10},{16,20},{18,... | collective-permute-start | bytes 307208 | tf_op jit(solution)/shard_map/ppermute | solution.py:451
  91.3 0.5 collective-permute-start.17
  91.8 5.2 %collective-permute-done.16 = f16[4,16,800]{2,1,0:T(8,128)(2,1)S(1)} collective-permute-done((f16[4,16,800]{2,1,0:T(8,128)(2,1)S(1)}, f16[4,16,800]{2,1,0:T(8,128)(2,1)S(1)}, u32[]{:S(2)}, u32[]{:S(2)}) %collective-permute-start.16) | collective-permute-done | bytes 102432 | tf_op jit(solution)/shard_map/ppermute | solution.py:451
  97.0 3.9 %collective-permute-done.17 = f16[4,16,800]{2,1,0:T(8,128)(2,1)S(1)} collective-permute-done((f16[4,16,800]{2,1,0:T(8,128)(2,1)S(1)}, f16[4,16,800]{2,1,0:T(8,128)(2,1)S(1)}, u32[]{:S(2)}, u32[]{:S(2)}) %collective-permute-start.17) | collective-permute-done | bytes 102432 | tf_op jit(solution)/shard_map/ppermute | solution.py:451
  100.8 0.1 maximum_convert_fusion.mixed_back
  101.0 1.9 %shard_map.83 = f32[2,800,120]{2,1,0:T(8,128)} custom-call(s32[3]{0:T(128)S(1)} %pad_add_fusion.here, f32[4,4,16,800]{3,2,1,0:T(8,128)S(1)} %maximum_convert_fusion.mixed_back, f32[2,800,120]{2,1,0:T(8,128)S(1)} %bitcast.52), custom_call_target="tpu_custom_call" | custom-call | flops 10000000000 | bytes 2000000 | tf_op jit(solution)/shard_map/pallas_call | solution.py:456
  102.9 1.2 %shard_map.85 = f32[2,800,120]{2,1,0:T(8,128)} custom-call(bf16[4,2,2,16,800]{4,3,2,1,0:T(8,128)(2,1)S(1)} %bitcast.48, f32[2,800,120]{2,1,0:T(8,128)S(1)} %bitcast.49), custom_call_target="tpu_custom_call" | custom-call | tf_op jit(solution)/shard_map/pallas_call | solution.py:464
  (34 shorter events, 0.7 us)
Async XLA Ops:
  0.6 1.6 %copy-start = (bf16[2,256,1920]{2,1,0:T(8,128)(2,1)S(1)}, bf16[2,256,1920]{2,1,0:T(8,128)(2,1)}, u32[]{:S(2)}) copy-start(bf16[2,256,1920]{2,1,0:T(8,128)(2,1)} %param.6) | copy-start | bytes 5898244
  3.0 13.2 %collective-permute-start.1 = (bf16[128,1920]{1,0:T(8,128)(2,1)}, bf16[128,1920]{1,0:T(8,128)(2,1)S(1)}, u32[]{:S(2)}, u32[]{:S(2)}) collective-permute-start(bf16[128,1920]{1,0:T(8,128)(2,1)} %dynamic-slice_bitcast_fusion.1), channel_id=1, source_target_pairs={{0,4},{2,6},{4,0},{6,2},{8,12},{10,14},{12,8},{14,10},{16,20},{18,... | collective-permute-start | bytes 1474568 | tf_op jit(solution)/shard_map/ppermute | solution.py:136
  5.1 16.7 %collective-permute-start.3 = (bf16[256,1920]{1,0:T(8,128)(2,1)S(1)}, bf16[256,1920]{1,0:T(8,128)(2,1)}, u32[]{:S(2)}, u32[]{:S(2)}) collective-permute-start(bf16[256,1920]{1,0:T(8,128)(2,1)S(1)} %dynamic-slice_bitcast_fusion.ctx0), channel_id=1, source_target_pairs={{0,2},{2,0},{4,6},{6,4},{8,10},{10,8},{12,14},{14,12},{16,18},{18,... | collective-permute-start | bytes 2949128 | tf_op jit(solution)/shard_map/ppermute | solution.py:132
  7.6 1.1 %copy-start.3 = (bf16[2,256,800]{1,2,0:T(8,128)(2,1)S(1)}, bf16[2,256,800]{1,2,0:T(8,128)(2,1)}, u32[]{:S(2)}) copy-start(bf16[2,256,800]{1,2,0:T(8,128)(2,1)} %param.7) | copy-start | bytes 2457604
  8.7 1.1 %copy-start.4 = (f32[2,120,800]{1,2,0:T(8,128)S(1)}, f32[2,120,800]{1,2,0:T(8,128)}, u32[]{:S(2)}) copy-start(f32[2,120,800]{1,2,0:T(8,128)} %param.9) | copy-start | bytes 2304004
  10.7 11.2 %collective-permute-start.4 = (bf16[800,384]{1,0:T(8,128)(2,1)S(1)}, bf16[800,384]{1,0:T(8,128)(2,1)S(1)}, u32[]{:S(2)}, u32[]{:S(2)}) collective-permute-start(bf16[800,384]{1,0:T(8,128)(2,1)S(1)} %get-tuple-element.22.ext0), channel_id=1, source_target_pairs={{0,2},{2,0},{4,6},{6,4},{8,10},{10,8},{12,14},{14,12},{16,18},{18,... | collective-permute-start | bytes 1843208 | tf_op jit(solution)/shard_map/ppermute | solution.py:132
  10.8 19.8 %collective-permute-start = (bf16[800,384]{1,0:T(8,128)(2,1)S(1)}, bf16[800,384]{1,0:T(8,128)(2,1)S(1)}, u32[]{:S(2)}, u32[]{:S(2)}) collective-permute-start(bf16[800,384]{1,0:T(8,128)(2,1)S(1)} %get-tuple-element.21), channel_id=1, source_target_pairs={{0,4},{2,6},{4,0},{6,2},{8,12},{10,14},{12,8},{14,10},{16,20},{18,... | collective-permute-start | bytes 1843208 | tf_op jit(solution)/shard_map/ppermute | solution.py:136
  16.2 3.8 %collective-permute-start.2 = (bf16[128,1920]{1,0:T(8,128)(2,1)S(1)}, bf16[128,1920]{1,0:T(8,128)(2,1)S(1)}, u32[]{:S(2)}, u32[]{:S(2)}) collective-permute-start(bf16[128,1920]{1,0:T(8,128)(2,1)S(1)} %collective-permute-done.1.first), channel_id=1, source_target_pairs={{0,2},{2,0},{4,6},{6,4},{8,10},{10,8},{12,14},{14,12},{16,18},{18,... | collective-permute-start | bytes 1474568 | tf_op jit(solution)/shard_map/ppermute | solution.py:132
  18.3 13.3 %collective-permute-start.6 = (bf16[128,1920]{1,0:T(8,128)(2,1)S(1)}, bf16[128,1920]{1,0:T(8,128)(2,1)S(1)}, u32[]{:S(2)}, u32[]{:S(2)}) collective-permute-start(bf16[128,1920]{1,0:T(8,128)(2,1)S(1)} %collective-permute-done.1.first), channel_id=1, source_target_pairs={{0,1},{1,0},{2,3},{3,2},{4,5},{5,4},{6,7},{7,6},{8,9},{9,8},{10,11... | collective-permute-start | bytes 1474568 | tf_op jit(solution)/shard_map/ppermute | solution.py:140
  30.5 3.1 %collective-permute-start.5 = (bf16[800,384]{1,0:T(8,128)(2,1)S(1)}, bf16[800,384]{1,0:T(8,128)(2,1)S(1)}, u32[]{:S(2)}, u32[]{:S(2)}) collective-permute-start(bf16[800,384]{1,0:T(8,128)(2,1)S(1)} %collective-permute-done.ext2), channel_id=1, source_target_pairs={{0,2},{2,0},{4,6},{6,4},{8,10},{10,8},{12,14},{14,12},{16,18},{18,... | collective-permute-start | bytes 1843208 | tf_op jit(solution)/shard_map/ppermute | solution.py:132
  31.6 2.1 %collective-permute-start.7 = (bf16[128,1920]{1,0:T(8,128)(2,1)S(1)}, bf16[128,1920]{1,0:T(8,128)(2,1)S(1)}, u32[]{:S(2)}, u32[]{:S(2)}) collective-permute-start(bf16[128,1920]{1,0:T(8,128)(2,1)S(1)} %collective-permute-done.6.far0), channel_id=1, source_target_pairs={{0,2},{2,0},{4,6},{6,4},{8,10},{10,8},{12,14},{14,12},{16,18},{18,... | collective-permute-start | bytes 1474568 | tf_op jit(solution)/shard_map/ppermute | solution.py:132
  37.5 1.4 %copy-start.1 = (f32[2,800,256]{2,1,0:T(8,128)}, f32[2,800,256]{2,1,0:T(8,128)S(1)}, u32[]{:S(2)}) copy-start(f32[2,800,256]{2,1,0:T(8,128)S(1)} %get-tuple-element.28) | copy-start | bytes 4915204
  39.0 11.1 %collective-permute-start.8 = (f16[800,256]{1,0:T(8,128)(2,1)}, f16[800,256]{1,0:T(8,128)(2,1)S(1)}, u32[]{:S(2)}, u32[]{:S(2)}) collective-permute-start(f16[800,256]{1,0:T(8,128)(2,1)} %get-tuple-element.38), channel_id=1, source_target_pairs={{0,8},{2,10},{4,12},{6,14},{8,0},{10,2},{12,4},{14,6},{16,24},{18,... | collective-permute-start | bytes 1228808 | tf_op jit(solution)/shard_map/ppermute | solution.py:405
  40.5 13.0 %collective-permute-start.10 = (f16[800,256]{1,0:T(8,128)(2,1)}, f16[800,256]{1,0:T(8,128)(2,1)S(1)}, u32[]{:S(2)}, u32[]{:S(2)}) collective-permute-start(f16[800,256]{1,0:T(8,128)(2,1)} %get-tuple-element.39), channel_id=1, source_target_pairs={{8,16},{10,18},{12,20},{14,22},{16,8},{18,10},{20,12},{22,14},{9,1... | collective-permute-start | bytes 1228808 | tf_op jit(solution)/shard_map/ppermute | solution.py:405
  41.2 16.9 %collective-permute-start.9 = (f16[800,256]{1,0:T(8,128)(2,1)}, f16[800,256]{1,0:T(8,128)(2,1)S(1)}, u32[]{:S(2)}, u32[]{:S(2)}) collective-permute-start(f16[800,256]{1,0:T(8,128)(2,1)} %get-tuple-element.39), channel_id=1, source_target_pairs={{0,16},{2,18},{4,20},{6,22},{24,8},{26,10},{28,12},{30,14},{1,17},... | collective-permute-start | bytes 1228808 | tf_op jit(solution)/shard_map/ppermute | solution.py:405
  52.1 19.7 %collective-permute-start.11 = (f16[800,256]{1,0:T(8,128)(2,1)}, f16[800,256]{1,0:T(8,128)(2,1)}, u32[]{:S(2)}, u32[]{:S(2)}) collective-permute-start(f16[800,256]{1,0:T(8,128)(2,1)} %fusion), channel_id=1, source_target_pairs={{0,8},{2,10},{4,12},{6,14},{8,24},{10,26},{12,28},{14,30},{24,16},... | collective-permute-start | bytes 1228808 | tf_op jit(solution)/shard_map/ppermute | solution.py:405
  73.5 5.1 %collective-permute-start.18 = (bf16[2,128,128]{2,1,0:T(8,128)(2,1)S(1)}, bf16[2,128,128]{2,1,0:T(8,128)(2,1)S(1)}, u32[]{:S(2)}, u32[]{:S(2)}) collective-permute-start(bf16[2,128,128]{2,1,0:T(8,128)(2,1)S(1)} %get-tuple-element.36), channel_id=1, source_target_pairs={{0,1},{1,0},{2,3},{3,2},{4,5},{5,4},{6,7},{7,6},{8,9},{9,8},{10,11... | collective-permute-start | bytes 196616 | tf_op jit(solution)/shard_map/ppermute | solution.py:140
  74.9 14.1 %collective-permute-start.12 = (f16[4,16,800]{2,1,0:T(8,128)(2,1)S(1)}, f16[4,16,800]{2,1,0:T(8,128)(2,1)S(1)}, u32[]{:S(2)}, u32[]{:S(2)}) collective-permute-start(f16[4,16,800]{2,1,0:T(8,128)(2,1)S(1)} %get-tuple-element.44), channel_id=1, source_target_pairs={{0,8},{2,10},{4,12},{6,14},{8,0},{10,2},{12,4},{14,6},{16,24},{18,... | collective-permute-start | bytes 307208 | tf_op jit(solution)/shard_map/ppermute | solution.py:405
  75.0 14.1 %collective-permute-start.13 = (f16[4,16,800]{2,1,0:T(8,128)(2,1)S(1)}, f16[4,16,800]{2,1,0:T(8,128)(2,1)S(1)}, u32[]{:S(2)}, u32[]{:S(2)}) collective-permute-start(f16[4,16,800]{2,1,0:T(8,128)(2,1)S(1)} %get-tuple-element.46), channel_id=1, source_target_pairs={{0,16},{2,18},{4,20},{6,22},{8,24},{10,26},{12,28},{14,30},{16,0},... | collective-permute-start | bytes 307208 | tf_op jit(solution)/shard_map/ppermute | solution.py:405
  77.3 11.9 %collective-permute-start.14 = (f16[4,16,800]{2,1,0:T(8,128)(2,1)S(1)}, f16[4,16,800]{2,1,0:T(8,128)(2,1)S(1)}, u32[]{:S(2)}, u32[]{:S(2)}) collective-permute-start(f16[4,16,800]{2,1,0:T(8,128)(2,1)S(1)} %get-tuple-element.45), channel_id=1, source_target_pairs={{0,24},{2,26},{4,28},{6,30},{8,16},{10,18},{12,20},{14,22},{16,8},... | collective-permute-start | bytes 307208 | tf_op jit(solution)/shard_map/ppermute | solution.py:405
  81.9 21.0 %all-to-all-start = ((bf16[16,16,800]{2,1,0:T(8,128)(2,1)}), bf16[16,16,800]{2,1,0:T(8,128)(2,1)S(1)}, u32[]{:S(2)}, u32[]{:S(2)}) async-start(bf16[16,16,800]{2,1,0:T(8,128)(2,1)} %shard_map.84), calls=%async_computation | async-start | bytes 917504 | tf_op jit(solution)/shard_map/all_to_all | solution.py:463
  89.1 11.9 %copy-start.5 = (f32[2,120,800]{1,2,0:T(8,128)S(1)}, f32[2,120,800]{1,2,0:T(8,128)}, u32[]{:S(2)}) copy-start(f32[2,120,800]{1,2,0:T(8,128)} %param.9) | copy-start | bytes 2304004
  89.3 2.5 %collective-permute-start.15 = (f16[4,16,800]{2,1,0:T(8,128)(2,1)S(1)}, f16[4,16,800]{2,1,0:T(8,128)(2,1)S(1)}, u32[]{:S(2)}, u32[]{:S(2)}) collective-permute-start(f16[4,16,800]{2,1,0:T(8,128)(2,1)S(1)} %pad_maximum_fusion), channel_id=1, source_target_pairs={{0,2},{2,0},{4,6},{6,4},{8,10},{10,8},{12,14},{14,12},{16,18},{18,... | collective-permute-start | bytes 307208 | tf_op jit(solution)/shard_map/ppermute | solution.py:451
  89.5 7.5 %collective-permute-start.16 = (f16[4,16,800]{2,1,0:T(8,128)(2,1)S(1)}, f16[4,16,800]{2,1,0:T(8,128)(2,1)S(1)}, u32[]{:S(2)}, u32[]{:S(2)}) collective-permute-start(f16[4,16,800]{2,1,0:T(8,128)(2,1)S(1)} %pad_maximum_fusion.1), channel_id=1, source_target_pairs={{0,4},{2,6},{4,0},{6,2},{8,12},{10,14},{12,8},{14,10},{16,20},{18,... | collective-permute-start | bytes 307208 | tf_op jit(solution)/shard_map/ppermute | solution.py:451
  91.3 9.6 %collective-permute-start.17 = (f16[4,16,800]{2,1,0:T(8,128)(2,1)S(1)}, f16[4,16,800]{2,1,0:T(8,128)(2,1)S(1)}, u32[]{:S(2)}, u32[]{:S(2)}) collective-permute-start(f16[4,16,800]{2,1,0:T(8,128)(2,1)S(1)} %pad_maximum_fusion.2), channel_id=1, source_target_pairs={{0,6},{2,4},{4,2},{6,0},{8,14},{10,12},{12,10},{14,8},{16,22},{18,... | collective-permute-start | bytes 307208 | tf_op jit(solution)/shard_map/ppermute | solution.py:451
  100.9 1.9 %copy-start.2 = (f32[2,120,800]{1,2,0:T(8,128)S(1)}, f32[2,120,800]{1,2,0:T(8,128)}, u32[]{:S(2)}) copy-start(f32[2,120,800]{1,2,0:T(8,128)} %param.10) | copy-start | bytes 2304004

commit v5 on v4

--- a/solution.py
+++ b/solution.py
@@ -34,6 +34,7 @@
 CHUNK_STEPS = len(CHUNK_ORDERS[0])
 CHUNK_SENDS = 2
 NO_HEAD = -(1 << 20)
+HALF_HEAD = HEAD // 2
 
 
 def quintic(current, reduce_gram):
@@ -163,90 +164,113 @@
     return (momentum * (2.0 * MIX)).astype(BF16)
 
 
-def head_of(step, c, index):
-    head = step * 4 + c * 2 + index
-    return jnp.where(head < HEADS_WIN, head, NO_HEAD)
-
-
-def fill_lead(lead):
-    row = lax.broadcasted_iota(jnp.int32, lead.shape, 0)
-    lead[...] = row - HEADS_WIN * lax.broadcasted_iota(jnp.int32, lead.shape, 1)
-
-
-def slots(pieces, lead, chunk, c):
-    places = [(lead[...] == head_of(chunk, c, index)).astype(F32).astype(BF16) for index in range(2)]
+def lane_lead(rows):
+    row = lax.broadcasted_iota(jnp.int32, (rows, HEAD), 0)
+    lane = lax.broadcasted_iota(jnp.int32, (rows, HEAD), 1)
+    return row - HEADS_WIN * (lane % HALF_HEAD) - lane // HALF_HEAD
+
+
+def slot_hits(lead, shift, chunk, c):
+    first = chunk * 4 + c * 2
+    lane = lax.broadcasted_iota(jnp.int32, lead.shape, 1)
+    return (lead == first + shift) & (lane < jnp.where(first + 1 < HEADS_WIN, HEAD, HALF_HEAD))
+
+
+def fill_slots(pieces, lead, table, refs, steps=range(CHUNK_STEPS)):
+    lead[...] = lane_lead(lead.shape[0])
+    window, columns = lead.shape[0], pieces[0].shape[-1]
     tokens = jnp.concatenate([piece[...] for piece in pieces], axis=0)
-    return contract(tokens, jnp.concatenate(places, axis=1), ((1,), (0,))).astype(BF16)
+    for pair in steps[::2]:
+        for half in range(2):
+            first = half * (columns - window)
+            shift = half * (columns // 2) - first
+            places = [
+                slot_hits(lead[...], shift, table[pair + index], table[CHUNK_STEPS + 3]).astype(F32).astype(BF16)
+                for index in range(2)
+            ]
+            moved = contract(tokens[:, first : first + window], jnp.concatenate(places, axis=1), ((1,), (0,)))
+            moved = moved.astype(BF16)
+            for index in range(2):
+                row = 0
+                for ref in refs:
+                    count = ref.shape[1]
+                    ref[pair - steps[0] + index, :, half * HEAD : (half + 1) * HEAD] = moved[
+                        row : row + count, index * HEAD : (index + 1) * HEAD
+                    ]
+                    row += count
 
 
 def momentum_places(table, chunk, sender_y, rows, value):
     z, y, c = (table[CHUNK_STEPS + index] for index in range(1, 4))
     local = lax.broadcasted_iota(jnp.int32, (HEAD, HEAD), 0)
-    lead = jnp.where(local < rows, local - HEADS_WIN * lax.broadcasted_iota(jnp.int32, (HEAD, HEAD), 1), 2 * NO_HEAD)
+    lead = jnp.where(local < rows, lane_lead(HEAD), NO_HEAD)
     places = []
     for sender_c in (c, 1 - c):
         first_row = dp_index(z, sender_y, sender_c) * rows
-        hits = [lead + first_row == head_of(chunk, c, index) for index in range(2)]
+        hits = [slot_hits(lead + first_row, half * HALF_HEAD * HEADS_WIN, chunk, c) for half in range(2)]
         hits = jnp.concatenate([jnp.where(hit, value, 0.0) for hit in hits], axis=1)
         places.append(hits.astype(BF16))
     return jnp.concatenate(places, axis=0)
 
 
 def near_kernel(table, first, second, out_ref, lead):
-    fill_lead(lead)
-    for chunk in range(SIZE_Z):
-        out_ref[chunk] = slots((first, second), lead, chunk, table[CHUNK_STEPS + 3])
-
-
-def own_kernel(table, ctx0, ctx1, ext0, ext1, out_ref, lead, *, factor, rows):
-    y, c = table[CHUNK_STEPS + 2], table[CHUNK_STEPS + 3]
-    tokens = ctx0.shape[0]
-    fill_lead(lead)
+    fill_slots((first, second), lead, table, (out_ref,))
+
+
+def chip_part(ext0, ext1, tokens, places):
+    count = tokens.shape[0] // 2
+    total = contract(ext0[:, :count], tokens[:count], ((1,), (0,)))
+    total += contract(ext1[:, :count], tokens[count:], ((1,), (0,)))
+    mixed_in = jnp.concatenate([ext0[:, count:], ext1[:, count:]], axis=1)
+    return total + contract(mixed_in, places, ((1,), (0,)))
+
+
+def own_kernel(table, ctx0, ctx1, ext0, ext1, out_ref, lead, own, *, factor, rows):
+    fill_slots((ctx0, ctx1), lead, table, (own,))
     for step in range(CHUNK_STEPS):
-        chunk = table[step]
-        own = slots((ctx0, ctx1), lead, chunk, c)
-        total = contract(ext0[:, :tokens], own[:tokens], ((1,), (0,)))
-        total += contract(ext1[:, :tokens], own[tokens:], ((1,), (0,)))
-        mixed_in = jnp.concatenate([ext0[:, tokens:], ext1[:, tokens:]], axis=1)
-        total += contract(mixed_in, momentum_places(table, chunk, y, rows, 0.5 / factor), ((1,), (0,)))
-        out_ref[step] = total
-
-
-def chunk_kernel(table, ext2, ext3, near, far0, far1, own, send_ref, keep_ref, lead, *, factor, rows):
-    x, y, c = table[CHUNK_STEPS], table[CHUNK_STEPS + 2], table[CHUNK_STEPS + 3]
+        places = momentum_places(table, table[step], table[CHUNK_STEPS + 2], rows, 0.5 / factor)
+        out_ref[step] = chip_part(ext0[...], ext1[...], own[step], places)
+
+
+def chunk_kernel(table, ext2, ext3, near, far0, far1, own, *refs, factor, rows, steps):
+    *out_refs, lead, far = refs
+    x, y = table[CHUNK_STEPS], table[CHUNK_STEPS + 2]
     half = far0.shape[0]
     tokens = 2 * half
-    fill_lead(lead)
-    for step in range(CHUNK_STEPS):
-        chunk = table[step]
-        far = slots((far0, far1), lead, chunk, c)
+    fill_slots((far0, far1), lead, table, (far,), steps)
+    for step, out_ref in zip(steps, out_refs):
         total = own[step]
         for source, ext in enumerate((ext2, ext3)):
-            here = near[chunk, source * half : (source + 1) * half]
-            there = far[source * half : (source + 1) * half]
+            here = near[step, source * half : (source + 1) * half]
+            there = far[step - steps[0], source * half : (source + 1) * half]
             low = jnp.where(x == 0, here, there)
             high = jnp.where(x == 0, there, here)
             total += contract(ext[:, :tokens], jnp.concatenate([low, high], axis=0), ((1,), (0,)))
         mixed_in = jnp.concatenate([ext2[:, tokens:], ext3[:, tokens:]], axis=1)
-        total += contract(mixed_in, momentum_places(table, chunk, 1 - y, rows, 0.5 / factor), ((1,), (0,)))
-        if step < CHUNK_SENDS:
-            send_ref[step] = total * factor
-        else:
-            keep_ref[step - CHUNK_SENDS] = total * factor
+        total += contract(mixed_in, momentum_places(table, table[step], 1 - y, rows, 0.5 / factor), ((1,), (0,)))
+        out_ref[...] = total * factor
+
+
+def head_rows(value, head):
+    first, second = (value[start : start + HALF_HEAD] for start in (head * HALF_HEAD, HEAD + head * HALF_HEAD))
+    return jnp.concatenate([first, second], axis=0)
 
 
 def gram_kernel(mixed, near_ref, far_ref):
+    block = (GAIN * mixed[...]).astype(BF16)
+    total = contract(block, block, ((0,), (0,)))
     for head in range(2):
-        block = (GAIN * mixed[:, head * HEAD : (head + 1) * HEAD]).astype(BF16)
-        total = contract(block, block, ((0,), (0,)))
-        near_ref[head] = total
-        far_ref[head] = total.astype(BF16)
+        gram = head_rows(head_rows(total, head).T, head)
+        near_ref[head] = gram
+        far_ref[head] = gram.astype(BF16)
 
 
 def turn_kernel(mixed, turned_ref, owner_ref):
     value = mixed[...].T
-    turned_ref[...] = value
-    store_by_owner(owner_ref, [value[:HEAD], value[HEAD:]])
+    blocks = [head_rows(value, head) for head in range(2)]
+    for head in range(2):
+        turned_ref[head * HEAD : (head + 1) * HEAD] = blocks[head]
+    store_by_owner(owner_ref, blocks)
 
 
 def store_by_owner(owner_ref, blocks):
@@ -360,12 +384,17 @@
 
     lanes = 2 * HEAD
 
-    def planned(kernel, out_shape, *args):
+    window = -(-all_rows // 2 // HEAD) * HEAD
+
+    def planned(kernel, out_shape, *args, tokens):
+        scratch = [pltpu.VMEM((window, HEAD), jnp.int32)]
+        if tokens:
+            scratch.append(pltpu.VMEM((CHUNK_STEPS, tokens, lanes), BF16))
         return pl.pallas_call(
             kernel,
             in_specs=[smem] + [vmem] * len(args),
             out_shape=out_shape,
-            scratch_shapes=[pltpu.VMEM((all_rows, HEAD), jnp.int32)],
+            scratch_shapes=scratch,
             compiler_params=vmem_params(),
             cost_estimate=pl.CostEstimate(flops=10**3, bytes_accessed=10**3, transcendentals=0),
         )(table, *args)
@@ -383,22 +412,29 @@
         ctx1,
         ext_keep,
         ext1,
+        tokens=2 * tok_dev,
     )
-    near = planned(near_kernel, jax.ShapeDtypeStruct((SIZE_Z, tok_dev, lanes), BF16), first0, first1)
+    near = planned(near_kernel, jax.ShapeDtypeStruct((CHUNK_STEPS, tok_dev, lanes), BF16), first0, first1, tokens=0)
     second0 = after(second0, near, own)
     second1 = swap_core(second0)
     ext2 = after(ext2, near, own)
     ext3 = swap_core(ext2)
-    send, keep = planned(
-        functools.partial(chunk_kernel, factor=factor, rows=shard_rows),
-        [chunks(CHUNK_SENDS), chunks(CHUNK_STEPS - CHUNK_SENDS)],
-        ext2,
-        ext3,
-        near,
-        second0,
-        second1,
-        own,
-    )
+    one = jax.ShapeDtypeStruct((columns, lanes), F32)
+    chunk = [
+        planned(
+            functools.partial(chunk_kernel, factor=factor, rows=shard_rows, steps=steps),
+            [one] * len(steps),
+            ext2,
+            ext3,
+            near,
+            second0,
+            second1,
+            own,
+            tokens=tok_dev,
+        )
+        for steps in (range(CHUNK_SENDS), range(CHUNK_SENDS, CHUNK_STEPS))
+    ]
+    chunk = [*chunk[0], *chunk[1]]
 
     def along_z(value, pairs):
         pairs = [(dp_index(p, b, a), dp_index(q, b, a)) for p, q in pairs for b in range(SIZE_Y) for a in range(SIZE_C)]
@@ -407,14 +443,14 @@
     def only(condition, value):
         return jnp.where(condition, value.astype(F32), jnp.zeros((), F32))
 
-    sent = send.astype(F16)
+    sent = [value.astype(F16) for value in chunk[:CHUNK_SENDS]]
     pair = along_z(sent[0], [(0, 1), (1, 0), (2, 3), (3, 2)])
     inner = along_z(sent[1], [(1, 2), (2, 1)])
     outer = along_z(sent[1], [(0, 2), (3, 1)])
     middle = (z == 1) | (z == 2)
-    merged = (keep[0] + only(middle, pair)).astype(F16)
+    merged = (chunk[2] + only(middle, pair)).astype(F16)
     last = along_z(merged, [(0, 1), (1, 3), (3, 2), (2, 0)])
-    base = keep[1] + only(~middle, after(pair, merged)) + (outer.astype(F32) + inner.astype(F32))
+    base = chunk[3] + only(~middle, after(pair, merged)) + (outer.astype(F32) + inner.astype(F32))
     base, last = lax.optimization_barrier((base, last))
     mixed = base + last.astype(F32)
 

time: 105 us -> 103 us (0.981)
  Pallas kernels: 22.1 us -> 17 us
  local copies, waits for them, and re-layouts: 6.93 us -> 10.8 us
  waiting for transfers between devices: 37 us -> 34.6 us
    ppermute x7, waiting for transfers between devices: 20.3 us -> 13.8 us  [along_z(): return lax.ppermute(value, 'dp', pairs)]
    unnamed x12 -> x34, local copies, waits for them, and re-layouts: 3.8 us -> 9.77 us
    pallas_call x3 -> x4, Pallas kernels: 14.3 us -> 9.1 us  [planned(): pl.pallas_call(kernel, in_specs=[smem] + [vmem] * len(args), out_shape=ou...]
    ppermute x2, waiting for transfers between devices: 5.4 us -> 8.95 us  [swap_y(): lax.ppermute(value, 'dp', [(dp_index(z, y, c), dp_index(z, 1 - y, c)) for...]
    squeeze x1 -> x0, local copies, waits for them, and re-layouts: 1.28 us -> none  [block_plan(): pair = along_z(sent[0], [(0, 1), (1, 0), (2, 3), (3, 2)])]
    convert_element_type x2 -> x3, other arithmetic: 2.15 us -> 2.92 us  [the longest x2 1.69 us: block_plan(): sent = [value.astype(F16) for value in chunk[:CHUNK_SENDS]]]
  transfers between devices with their start and end apart: 20 -> 20, of which waited for: 8 -> 8; matrix products, arithmetic and copies ran while one was open for 5% -> 5% of each run, Pallas kernels for 16% -> 13%
where the time goes in v5:
time: 103 us; the launch traced here: 102 us
  waiting for transfers between devices  34.6 us (34%)
  starting transfers between devices  31.8 us (31%)
  Pallas kernels  17 us (17%)
  local copies, waits for them, and re-layouts  10.8 us (10%)
  other arithmetic  5.84 us (6%)
  between operations  1.71 us (2%)
    ppermute x7, waiting for transfers between devices, along_z(): return lax.ppermute(value, 'dp', pairs)  13.8 us
    ppermute x7, starting transfers between devices, along_z(): return lax.ppermute(value, 'dp', pairs)  12.1 us
    unnamed x34, local copies, waits for them, and re-layouts  9.77 us
    pallas_call x4, Pallas kernels, planned(): pl.pallas_call(kernel, in_specs=[smem] + [vmem] * len(args), out_shape=ou...  9.1 us
    ppermute x3, waiting for transfers between devices, block_plan(): piece = lax.ppermute(piece, 'dp', [(k, k ^ apart) for k in range(owners)])  9.04 us
    ppermute x2, waiting for transfers between devices, swap_y(): lax.ppermute(value, 'dp', [(dp_index(z, y, c), dp_index(z, 1 - y, c)) for...  8.95 us
    all_to_all x1, starting transfers between devices, block_plan(): lax.all_to_all(ortho_send, 'dp', 0, 0)  7.2 us
    ppermute x5, starting transfers between devices, swap_core(): lax.ppermute(value, 'dp', [(dp_index(z, y, c), dp_index(z, y, 1 - c)) for...  5 us
  transfers between devices with their start and end apart: 20, of which 8 were waited for; matrix products, arithmetic and copies ran while one was open for 5% of the time, Pallas kernels for 13%

profile of v5, /device:TPU:1, one launch (start us, length us, event | category | flops | bytes accessed | tf_op | source)
XLA Modules:
  0.0 101.9 jit_solution(6077177013726989966)
XLA Ops:
  0.7 1.5 %copy-done = bf16[2,256,1920]{2,1,0:T(8,128)(2,1)S(1)} copy-done((bf16[2,256,1920]{2,1,0:T(8,128)(2,1)S(1)}, bf16[2,256,1920]{2,1,0:T(8,128)(2,1)}, u32[]{:S(2)}) %copy-start) | copy-done | bytes 1966104
  2.2 2.1 %collective-permute-start.1 = (bf16[128,1920]{1,0:T(8,128)(2,1)S(1)}, bf16[128,1920]{1,0:T(8,128)(2,1)}, u32[]{:S(2)}, u32[]{:S(2)}) collective-permute-start(bf16[128,1920]{1,0:T(8,128)(2,1)S(1)} %dynamic-slice_bitcast_fusion.1), channel_id=1, source_target_pairs={{0,4},{2,6},{4,0},{6,2},{8,12},{10,14},{12,8},{14,10},{16,20},{18,... | collective-permute-start | bytes 1474568 | tf_op jit(solution)/shard_map/ppermute | solution.py:137
  4.4 1.0 %collective-permute-start.3 = (bf16[256,1920]{1,0:T(8,128)(2,1)S(1)}, bf16[256,1920]{1,0:T(8,128)(2,1)}, u32[]{:S(2)}, u32[]{:S(2)}) collective-permute-start(bf16[256,1920]{1,0:T(8,128)(2,1)S(1)} %dynamic-slice_bitcast_fusion.ctx0), channel_id=1, source_target_pairs={{0,2},{2,0},{4,6},{6,4},{8,10},{10,8},{12,14},{14,12},{16,18},{18,... | collective-permute-start | bytes 2949128 | tf_op jit(solution)/shard_map/ppermute | solution.py:133
  5.4 0.7 fusion
  6.9 1.1 %copy-done.14 = bf16[2,256,800]{1,2,0:T(8,128)(2,1)S(1)} copy-done((bf16[2,256,800]{1,2,0:T(8,128)(2,1)S(1)}, bf16[2,256,800]{1,2,0:T(8,128)(2,1)}, u32[]{:S(2)}) %copy-start.14) | copy-done | bytes 819224
  8.0 1.1 %copy-done.15 = f32[2,120,800]{1,2,0:T(8,128)S(1)} copy-done((f32[2,120,800]{1,2,0:T(8,128)S(1)}, f32[2,120,800]{1,2,0:T(8,128)}, u32[]{:S(2)}) %copy-start.15) | copy-done | bytes 768024
  9.2 0.8 shard_map.77
  10.1 5.3 %collective-permute-done.1.first = bf16[128,1920]{1,0:T(8,128)(2,1)} collective-permute-done((bf16[128,1920]{1,0:T(8,128)(2,1)S(1)}, bf16[128,1920]{1,0:T(8,128)(2,1)}, u32[]{:S(2)}, u32[]{:S(2)}) %collective-permute-start.1) | collective-permute-done | bytes 491552 | tf_op jit(solution)/shard_map/ppermute | solution.py:137
  15.4 2.1 %collective-permute-start.2 = (bf16[128,1920]{1,0:T(8,128)(2,1)}, bf16[128,1920]{1,0:T(8,128)(2,1)S(1)}, u32[]{:S(2)}, u32[]{:S(2)}) collective-permute-start(bf16[128,1920]{1,0:T(8,128)(2,1)} %collective-permute-done.1.first), channel_id=1, source_target_pairs={{0,2},{2,0},{4,6},{6,4},{8,10},{10,8},{12,14},{14,12},{16,18},{18,... | collective-permute-start | bytes 1474568 | tf_op jit(solution)/shard_map/ppermute | solution.py:133
  17.5 1.7 %collective-permute-start.6 = (bf16[128,1920]{1,0:T(8,128)(2,1)}, bf16[128,1920]{1,0:T(8,128)(2,1)S(1)}, u32[]{:S(2)}, u32[]{:S(2)}) collective-permute-start(bf16[128,1920]{1,0:T(8,128)(2,1)} %collective-permute-done.1.first), channel_id=1, source_target_pairs={{0,1},{1,0},{2,3},{3,2},{4,5},{5,4},{6,7},{7,6},{8,9},{9,8},{10,11... | collective-permute-start | bytes 1474568 | tf_op jit(solution)/shard_map/ppermute | solution.py:141
  19.2 1.8 %shard_map.78.near = bf16[4,256,256]{2,1,0:T(8,128)(2,1)S(1)} custom-call(s32[8]{0:T(128)S(1)} %concatenate.3.table, bf16[128,1920]{1,0:T(8,128)(2,1)} %collective-permute-done.1.first, bf16[128,1920]{1,0:T(8,128)(2,1)S(1)} %collective-permute-done.2.second), custom_call_target="tpu_custom_call" | custom-call | flops 1000 | bytes 1000 | tf_op jit(solution)/shard_map/pallas_call | solution.py:393
  21.1 3.7 %shard_map.79.own = f32[4,800,256]{2,1,0:T(8,128)S(1)} custom-call(s32[8]{0:T(128)S(1)} %concatenate.3.table, bf16[256,1920]{1,0:T(8,128)(2,1)S(1)} %dynamic-slice_bitcast_fusion.ctx0, bf16[256,1920]{1,0:T(8,128)(2,1)} %collective-permute-done.3.ctx1, bf16[800,384]{1,0:T(8,128)(2,1)S(1)} %get-tuple-element.24.ext0, ...), custom_call_target="tpu_custom_call" | custom-call | flops 1000 | bytes 1000 | tf_op jit(solution)/shard_map/pallas_call | solution.py:393
  24.8 3.7 %collective-permute-done.ext2 = bf16[800,384]{1,0:T(8,128)(2,1)S(1)} collective-permute-done((bf16[800,384]{1,0:T(8,128)(2,1)S(1)}, bf16[800,384]{1,0:T(8,128)(2,1)S(1)}, u32[]{:S(2)}, u32[]{:S(2)}) %collective-permute-start) | collective-permute-done | bytes 614432 | tf_op jit(solution)/shard_map/ppermute | solution.py:137
  28.5 1.2 %collective-permute-start.5 = (bf16[800,384]{1,0:T(8,128)(2,1)S(1)}, bf16[800,384]{1,0:T(8,128)(2,1)S(1)}, u32[]{:S(2)}, u32[]{:S(2)}) collective-permute-start(bf16[800,384]{1,0:T(8,128)(2,1)S(1)} %collective-permute-done.ext2), channel_id=1, source_target_pairs={{0,2},{2,0},{4,6},{6,4},{8,10},{10,8},{12,14},{14,12},{16,18},{18,... | collective-permute-start | bytes 1843208 | tf_op jit(solution)/shard_map/ppermute | solution.py:133
  29.7 1.3 %collective-permute-done.6.far0 = bf16[128,1920]{1,0:T(8,128)(2,1)S(1)} collective-permute-done((bf16[128,1920]{1,0:T(8,128)(2,1)}, bf16[128,1920]{1,0:T(8,128)(2,1)S(1)}, u32[]{:S(2)}, u32[]{:S(2)}) %collective-permute-start.6) | collective-permute-done | bytes 491552 | tf_op jit(solution)/shard_map/ppermute | solution.py:141
  31.0 0.6 collective-permute-start.7
  31.6 1.5 %collective-permute-done.7.far1 = bf16[128,1920]{1,0:T(8,128)(2,1)S(1)} collective-permute-done((bf16[128,1920]{1,0:T(8,128)(2,1)S(1)}, bf16[128,1920]{1,0:T(8,128)(2,1)S(1)}, u32[]{:S(2)}, u32[]{:S(2)}) %collective-permute-start.7) | collective-permute-done | bytes 491552 | tf_op jit(solution)/shard_map/ppermute | solution.py:133
  33.1 1.8 %shard_map.81 = (f32[800,256]{1,0:T(8,128)S(1)}, f32[800,256]{1,0:T(8,128)S(1)}) custom-call(s32[8]{0:T(128)S(1)} %concatenate.3.table, bf16[800,384]{1,0:T(8,128)(2,1)S(1)} %collective-permute-done.ext2, bf16[800,384]{1,0:T(8,128)(2,1)S(1)} %collective-permute-done.5.ext3, bf16[4,256,256]{2,1,0:T(8,128)(2,1)S(1)} %shard_map.78.near, ...), custom_call_target="tpu_custom_call" | custom-call | flops 1000 | bytes 1000 | tf_op jit(solution)/shard_map/pallas_call | solution.py:393
  34.9 0.8 convert_element_type.30
  35.8 1.6 %collective-permute-start.8 = (f16[800,256]{1,0:T(8,128)(2,1)}, f16[800,256]{1,0:T(8,128)(2,1)}, u32[]{:S(2)}, u32[]{:S(2)}) collective-permute-start(f16[800,256]{1,0:T(8,128)(2,1)} %convert_element_type.30), channel_id=1, source_target_pairs={{0,8},{2,10},{4,12},{6,14},{8,0},{10,2},{12,4},{14,6},{16,24},{18,... | collective-permute-start | bytes 1228808 | tf_op jit(solution)/shard_map/ppermute | solution.py:441
  37.3 0.8 convert_element_type.34
  38.2 1.4 %collective-permute-start.10 = (f16[800,256]{1,0:T(8,128)(2,1)}, f16[800,256]{1,0:T(8,128)(2,1)}, u32[]{:S(2)}, u32[]{:S(2)}) collective-permute-start(f16[800,256]{1,0:T(8,128)(2,1)} %convert_element_type.34), channel_id=1, source_target_pairs={{8,16},{10,18},{12,20},{14,22},{16,8},{18,10},{20,12},{22,14},{9,1... | collective-permute-start | bytes 1228808 | tf_op jit(solution)/shard_map/ppermute | solution.py:441
  39.6 5.5 %collective-permute-start.9 = (f16[800,256]{1,0:T(8,128)(2,1)}, f16[800,256]{1,0:T(8,128)(2,1)}, u32[]{:S(2)}, u32[]{:S(2)}) collective-permute-start(f16[800,256]{1,0:T(8,128)(2,1)} %convert_element_type.34), channel_id=1, source_target_pairs={{0,16},{2,18},{4,20},{6,22},{24,8},{26,10},{28,12},{30,14},{1,17},... | collective-permute-start | bytes 1228808 | tf_op jit(solution)/shard_map/ppermute | solution.py:441
  45.1 1.9 %copy-done.2 = f32[4,800,256]{2,1,0:T(8,128)S(1)} copy-done((f32[4,800,256]{2,1,0:T(8,128)S(1)}, f32[4,800,256]{2,1,0:T(8,128)}, u32[]{:S(2)}) %copy-start.2) | copy-done | bytes 3276824
  47.0 1.1 %copy-done.6 = bf16[800,384]{1,0:T(8,128)(2,1)S(1)} copy-done((bf16[800,384]{1,0:T(8,128)(2,1)S(1)}, bf16[800,384]{1,0:T(8,128)(2,1)}, u32[]{:S(2)}) %copy-start.6) | copy-done | bytes 614424
  48.1 1.0 %copy-done.8 = bf16[128,1920]{1,0:T(8,128)(2,1)S(1)} copy-done((bf16[128,1920]{1,0:T(8,128)(2,1)S(1)}, bf16[128,1920]{1,0:T(8,128)(2,1)}, u32[]{:S(2)}) %copy-start.8) | copy-done | bytes 491544
  49.1 1.0 %copy-done.10 = bf16[128,1920]{1,0:T(8,128)(2,1)S(1)} copy-done((bf16[128,1920]{1,0:T(8,128)(2,1)S(1)}, bf16[128,1920]{1,0:T(8,128)(2,1)}, u32[]{:S(2)}) %copy-start.10) | copy-done | bytes 491544
  50.1 1.8 %shard_map.80 = (f32[800,256]{1,0:T(8,128)S(1)}, f32[800,256]{1,0:T(8,128)S(1)}) custom-call(s32[8]{0:T(128)S(1)} %concatenate.3.table, bf16[800,384]{1,0:T(8,128)(2,1)S(1)} %copy-done.4, bf16[800,384]{1,0:T(8,128)(2,1)S(1)} %copy-done.6, bf16[4,256,256]{2,1,0:T(8,128)(2,1)S(1)} %shard_map.78.near, bf16[128,1920]{1,0:T(8,128)(2,1)S(1)} %copy-done.8, ...), custom_call_target="tpu_custom_call" | custom-call | flops 1000 | bytes 1000 | tf_op jit(solution)/shard_map/pallas_call | solution.py:393
  51.9 0.9 copy-done.11
  52.8 1.2 %add_convert_fusion = f16[800,256]{1,0:T(8,128)(2,1)S(1)} fusion(f32[800,256]{1,0:T(8,128)S(1)} %get-tuple-element.32, f16[800,256]{1,0:T(8,128)(2,1)} %collective-permute-done.8, pred[]{:T(512)S(6)} %or.3), kind=kLoop, calls=%fused_computation.3 | loop fusion | flops 819200 | bytes 1638401 | tf_op jit(solution)/shard_map/convert_element_type | solution.py:451
  54.3 0.7 collective-permute-done.9
  55.0 1.4 %add_add_fusion = f32[800,256]{1,0:T(8,128)S(1)} fusion(f16[800,256]{1,0:T(8,128)(2,1)} %collective-permute-done.10, f16[800,256]{1,0:T(8,128)(2,1)} %collective-permute-done.9, f32[800,256]{1,0:T(8,128)S(1)} %copy-done.12, f16[800,256]{1,0:T(8,128)(2,1)} %collective-permute-done.8, pred[]{:T(512)S(6)} %not.3), kind=kLoop, calls=%fused_computation.2 | loop fusion | flops 1433600 | bytes 2867201 | tf_op jit(solution)/shard_map/add | solution.py:453
  56.4 13.1 %collective-permute-done.11 = f16[800,256]{1,0:T(8,128)(2,1)} collective-permute-done((f16[800,256]{1,0:T(8,128)(2,1)S(1)}, f16[800,256]{1,0:T(8,128)(2,1)}, u32[]{:S(2)}, u32[]{:S(2)}) %collective-permute-start.11) | collective-permute-done | bytes 409632 | tf_op jit(solution)/shard_map/ppermute | solution.py:441
  69.5 1.1 %convert_add_fusion.mixed = f32[800,256]{1,0:T(8,128)S(1)} fusion(f32[800,256]{1,0:T(8,128)S(1)} %add_add_fusion, f16[800,256]{1,0:T(8,128)(2,1)} %collective-permute-done.11), kind=kLoop, calls=%fused_computation.1 | loop fusion | flops 409600 | bytes 2048000 | tf_op jit(solution)/shard_map/add | solution.py:455
  70.5 0.4 shard_map.82
  71.0 0.3 shard_map.83
  71.3 1.3 %collective-permute-start.18 = (bf16[2,128,128]{2,1,0:T(8,128)(2,1)S(1)}, bf16[2,128,128]{2,1,0:T(8,128)(2,1)S(1)}, u32[]{:S(2)}, u32[]{:S(2)}) collective-permute-start(bf16[2,128,128]{2,1,0:T(8,128)(2,1)S(1)} %get-tuple-element.40), channel_id=1, source_target_pairs={{0,1},{1,0},{2,3},{3,2},{4,5},{5,4},{6,7},{7,6},{8,9},{9,8},{10,11... | collective-permute-start | bytes 196616 | tf_op jit(solution)/shard_map/ppermute | solution.py:141
  72.8 2.3 %collective-permute-start.13 = (f16[4,16,800]{2,1,0:T(8,128)(2,1)S(1)}, f16[4,16,800]{2,1,0:T(8,128)(2,1)S(1)}, u32[]{:S(2)}, u32[]{:S(2)}) collective-permute-start(f16[4,16,800]{2,1,0:T(8,128)(2,1)S(1)} %get-tuple-element.48), channel_id=1, source_target_pairs={{0,16},{2,18},{4,20},{6,22},{8,24},{10,26},{12,28},{14,30},{16,0},... | collective-permute-start | bytes 307208 | tf_op jit(solution)/shard_map/ppermute | solution.py:441
  75.1 1.2 %collective-permute-start.14 = (f16[4,16,800]{2,1,0:T(8,128)(2,1)S(1)}, f16[4,16,800]{2,1,0:T(8,128)(2,1)S(1)}, u32[]{:S(2)}, u32[]{:S(2)}) collective-permute-start(f16[4,16,800]{2,1,0:T(8,128)(2,1)S(1)} %get-tuple-element.47), channel_id=1, source_target_pairs={{0,24},{2,26},{4,28},{6,30},{8,16},{10,18},{12,20},{14,22},{16,8},... | collective-permute-start | bytes 307208 | tf_op jit(solution)/shard_map/ppermute | solution.py:441
  76.4 3.3 %shard_map.85 = bf16[16,16,800]{2,1,0:T(8,128)(2,1)} custom-call(f32[2,128,128]{2,1,0:T(8,128)S(1)} %get-tuple-element.37.near, bf16[2,128,128]{2,1,0:T(8,128)(2,1)S(1)} %collective-permute-done.18.far, f32[256,800]{1,0:T(8,128)S(1)} %get-tuple-element.41.turned), custom_call_target="tpu_custom_call" | custom-call | tf_op jit(solution)/shard_map/pallas_call | solution.py:471
  79.6 7.2 %all-to-all-start = ((bf16[16,16,800]{2,1,0:T(8,128)(2,1)}), bf16[16,16,800]{2,1,0:T(8,128)(2,1)S(1)}, u32[]{:S(2)}, u32[]{:S(2)}) async-start(bf16[16,16,800]{2,1,0:T(8,128)(2,1)} %shard_map.85), calls=%async_computation | async-start | bytes 917504 | tf_op jit(solution)/shard_map/all_to_all | solution.py:499
  87.1 0.2 collective-permute-start.15
  87.3 1.7 %collective-permute-start.16 = (f16[4,16,800]{2,1,0:T(8,128)(2,1)S(1)}, f16[4,16,800]{2,1,0:T(8,128)(2,1)S(1)}, u32[]{:S(2)}, u32[]{:S(2)}) collective-permute-start(f16[4,16,800]{2,1,0:T(8,128)(2,1)S(1)} %pad_maximum_fusion.1), channel_id=1, source_target_pairs={{0,4},{2,6},{4,0},{6,2},{8,12},{10,14},{12,8},{14,10},{16,20},{18,... | collective-permute-start | bytes 307208 | tf_op jit(solution)/shard_map/ppermute | solution.py:487
  89.0 0.5 collective-permute-start.17
  89.5 5.2 %collective-permute-done.16 = f16[4,16,800]{2,1,0:T(8,128)(2,1)S(1)} collective-permute-done((f16[4,16,800]{2,1,0:T(8,128)(2,1)S(1)}, f16[4,16,800]{2,1,0:T(8,128)(2,1)S(1)}, u32[]{:S(2)}, u32[]{:S(2)}) %collective-permute-start.16) | collective-permute-done | bytes 102432 | tf_op jit(solution)/shard_map/ppermute | solution.py:487
  94.7 3.9 %collective-permute-done.17 = f16[4,16,800]{2,1,0:T(8,128)(2,1)S(1)} collective-permute-done((f16[4,16,800]{2,1,0:T(8,128)(2,1)S(1)}, f16[4,16,800]{2,1,0:T(8,128)(2,1)S(1)}, u32[]{:S(2)}, u32[]{:S(2)}) %collective-permute-start.17) | collective-permute-done | bytes 102432 | tf_op jit(solution)/shard_map/ppermute | solution.py:487
  98.7 1.9 %shard_map.84 = f32[2,800,120]{2,1,0:T(8,128)} custom-call(s32[3]{0:T(128)S(1)} %pad_add_fusion.here, f32[4,4,16,800]{3,2,1,0:T(8,128)S(1)} %maximum_convert_fusion.mixed_back, f32[2,800,120]{2,1,0:T(8,128)S(1)} %bitcast.40), custom_call_target="tpu_custom_call" | custom-call | flops 10000000000 | bytes 2000000 | tf_op jit(solution)/shard_map/pallas_call | solution.py:492
  100.6 1.2 %shard_map.86 = f32[2,800,120]{2,1,0:T(8,128)} custom-call(bf16[4,2,2,16,800]{4,3,2,1,0:T(8,128)(2,1)S(1)} %bitcast.36, f32[2,800,120]{2,1,0:T(8,128)S(1)} %bitcast.37), custom_call_target="tpu_custom_call" | custom-call | tf_op jit(solution)/shard_map/pallas_call | solution.py:500
  (57 shorter events, 1.2 us)
Async XLA Ops:
  0.6 1.6 %copy-start = (bf16[2,256,1920]{2,1,0:T(8,128)(2,1)S(1)}, bf16[2,256,1920]{2,1,0:T(8,128)(2,1)}, u32[]{:S(2)}) copy-start(bf16[2,256,1920]{2,1,0:T(8,128)(2,1)} %param.6) | copy-start | bytes 5898244
  2.2 13.2 %collective-permute-start.1 = (bf16[128,1920]{1,0:T(8,128)(2,1)S(1)}, bf16[128,1920]{1,0:T(8,128)(2,1)}, u32[]{:S(2)}, u32[]{:S(2)}) collective-permute-start(bf16[128,1920]{1,0:T(8,128)(2,1)S(1)} %dynamic-slice_bitcast_fusion.1), channel_id=1, source_target_pairs={{0,4},{2,6},{4,0},{6,2},{8,12},{10,14},{12,8},{14,10},{16,20},{18,... | collective-permute-start | bytes 1474568 | tf_op jit(solution)/shard_map/ppermute | solution.py:137
  4.4 16.6 %collective-permute-start.3 = (bf16[256,1920]{1,0:T(8,128)(2,1)S(1)}, bf16[256,1920]{1,0:T(8,128)(2,1)}, u32[]{:S(2)}, u32[]{:S(2)}) collective-permute-start(bf16[256,1920]{1,0:T(8,128)(2,1)S(1)} %dynamic-slice_bitcast_fusion.ctx0), channel_id=1, source_target_pairs={{0,2},{2,0},{4,6},{6,4},{8,10},{10,8},{12,14},{14,12},{16,18},{18,... | collective-permute-start | bytes 2949128 | tf_op jit(solution)/shard_map/ppermute | solution.py:133
  6.9 1.1 %copy-start.14 = (bf16[2,256,800]{1,2,0:T(8,128)(2,1)S(1)}, bf16[2,256,800]{1,2,0:T(8,128)(2,1)}, u32[]{:S(2)}) copy-start(bf16[2,256,800]{1,2,0:T(8,128)(2,1)} %param.7) | copy-start | bytes 2457604
  8.0 1.1 %copy-start.15 = (f32[2,120,800]{1,2,0:T(8,128)S(1)}, f32[2,120,800]{1,2,0:T(8,128)}, u32[]{:S(2)}) copy-start(f32[2,120,800]{1,2,0:T(8,128)} %param.9) | copy-start | bytes 2304004
  9.9 11.1 %collective-permute-start.4 = (bf16[800,384]{1,0:T(8,128)(2,1)S(1)}, bf16[800,384]{1,0:T(8,128)(2,1)S(1)}, u32[]{:S(2)}, u32[]{:S(2)}) collective-permute-start(bf16[800,384]{1,0:T(8,128)(2,1)S(1)} %get-tuple-element.24.ext0), channel_id=1, source_target_pairs={{0,2},{2,0},{4,6},{6,4},{8,10},{10,8},{12,14},{14,12},{16,18},{18,... | collective-permute-start | bytes 1843208 | tf_op jit(solution)/shard_map/ppermute | solution.py:133
  10.1 18.4 %collective-permute-start = (bf16[800,384]{1,0:T(8,128)(2,1)S(1)}, bf16[800,384]{1,0:T(8,128)(2,1)S(1)}, u32[]{:S(2)}, u32[]{:S(2)}) collective-permute-start(bf16[800,384]{1,0:T(8,128)(2,1)S(1)} %get-tuple-element.23), channel_id=1, source_target_pairs={{0,4},{2,6},{4,0},{6,2},{8,12},{10,14},{12,8},{14,10},{16,20},{18,... | collective-permute-start | bytes 1843208 | tf_op jit(solution)/shard_map/ppermute | solution.py:137
  15.4 3.8 %collective-permute-start.2 = (bf16[128,1920]{1,0:T(8,128)(2,1)}, bf16[128,1920]{1,0:T(8,128)(2,1)S(1)}, u32[]{:S(2)}, u32[]{:S(2)}) collective-permute-start(bf16[128,1920]{1,0:T(8,128)(2,1)} %collective-permute-done.1.first), channel_id=1, source_target_pairs={{0,2},{2,0},{4,6},{6,4},{8,10},{10,8},{12,14},{14,12},{16,18},{18,... | collective-permute-start | bytes 1474568 | tf_op jit(solution)/shard_map/ppermute | solution.py:133
  17.5 13.6 %collective-permute-start.6 = (bf16[128,1920]{1,0:T(8,128)(2,1)}, bf16[128,1920]{1,0:T(8,128)(2,1)S(1)}, u32[]{:S(2)}, u32[]{:S(2)}) collective-permute-start(bf16[128,1920]{1,0:T(8,128)(2,1)} %collective-permute-done.1.first), channel_id=1, source_target_pairs={{0,1},{1,0},{2,3},{3,2},{4,5},{5,4},{6,7},{7,6},{8,9},{9,8},{10,11... | collective-permute-start | bytes 1474568 | tf_op jit(solution)/shard_map/ppermute | solution.py:141
  24.8 10.1 %copy-start.1 = (f32[4,800,256]{2,1,0:T(8,128)}, f32[4,800,256]{2,1,0:T(8,128)S(1)}, u32[]{:S(2)}) copy-start(f32[4,800,256]{2,1,0:T(8,128)S(1)} %shard_map.79.own) | copy-start | bytes 9830404
  28.5 6.4 %copy-start.3 = (bf16[800,384]{1,0:T(8,128)(2,1)}, bf16[800,384]{1,0:T(8,128)(2,1)S(1)}, u32[]{:S(2)}) copy-start(bf16[800,384]{1,0:T(8,128)(2,1)S(1)} %collective-permute-done.ext2) | copy-start | bytes 1843204
  28.5 4.6 %collective-permute-start.5 = (bf16[800,384]{1,0:T(8,128)(2,1)S(1)}, bf16[800,384]{1,0:T(8,128)(2,1)S(1)}, u32[]{:S(2)}, u32[]{:S(2)}) collective-permute-start(bf16[800,384]{1,0:T(8,128)(2,1)S(1)} %collective-permute-done.ext2), channel_id=1, source_target_pairs={{0,2},{2,0},{4,6},{6,4},{8,10},{10,8},{12,14},{14,12},{16,18},{18,... | collective-permute-start | bytes 1843208 | tf_op jit(solution)/shard_map/ppermute | solution.py:133
  31.0 3.9 %copy-start.7 = (bf16[128,1920]{1,0:T(8,128)(2,1)}, bf16[128,1920]{1,0:T(8,128)(2,1)S(1)}, u32[]{:S(2)}) copy-start(bf16[128,1920]{1,0:T(8,128)(2,1)S(1)} %collective-permute-done.6.far0) | copy-start | bytes 1474564
  31.0 2.1 %collective-permute-start.7 = (bf16[128,1920]{1,0:T(8,128)(2,1)S(1)}, bf16[128,1920]{1,0:T(8,128)(2,1)S(1)}, u32[]{:S(2)}, u32[]{:S(2)}) collective-permute-start(bf16[128,1920]{1,0:T(8,128)(2,1)S(1)} %collective-permute-done.6.far0), channel_id=1, source_target_pairs={{0,2},{2,0},{4,6},{6,4},{8,10},{10,8},{12,14},{14,12},{16,18},{18,... | collective-permute-start | bytes 1474568 | tf_op jit(solution)/shard_map/ppermute | solution.py:133
  33.1 1.8 %copy-start.9 = (bf16[128,1920]{1,0:T(8,128)(2,1)}, bf16[128,1920]{1,0:T(8,128)(2,1)S(1)}, u32[]{:S(2)}) copy-start(bf16[128,1920]{1,0:T(8,128)(2,1)S(1)} %collective-permute-done.7.far1) | copy-start | bytes 1474564
  33.1 1.8 %copy-start.5 = (bf16[800,384]{1,0:T(8,128)(2,1)}, bf16[800,384]{1,0:T(8,128)(2,1)S(1)}, u32[]{:S(2)}) copy-start(bf16[800,384]{1,0:T(8,128)(2,1)S(1)} %collective-permute-done.5.ext3) | copy-start | bytes 1843204
  34.9 10.1 %copy-start.4 = (bf16[800,384]{1,0:T(8,128)(2,1)S(1)}, bf16[800,384]{1,0:T(8,128)(2,1)}, u32[]{:S(2)}) copy-start(bf16[800,384]{1,0:T(8,128)(2,1)} %copy-done.3) | copy-start | bytes 1843204
  35.8 17.0 %collective-permute-start.8 = (f16[800,256]{1,0:T(8,128)(2,1)}, f16[800,256]{1,0:T(8,128)(2,1)}, u32[]{:S(2)}, u32[]{:S(2)}) collective-permute-start(f16[800,256]{1,0:T(8,128)(2,1)} %convert_element_type.30), channel_id=1, source_target_pairs={{0,8},{2,10},{4,12},{6,14},{8,0},{10,2},{12,4},{14,6},{16,24},{18,... | collective-permute-start | bytes 1228808 | tf_op jit(solution)/shard_map/ppermute | solution.py:441
  38.2 16.1 %collective-permute-start.10 = (f16[800,256]{1,0:T(8,128)(2,1)}, f16[800,256]{1,0:T(8,128)(2,1)}, u32[]{:S(2)}, u32[]{:S(2)}) collective-permute-start(f16[800,256]{1,0:T(8,128)(2,1)} %convert_element_type.34), channel_id=1, source_target_pairs={{8,16},{10,18},{12,20},{14,22},{16,8},{18,10},{20,12},{22,14},{9,1... | collective-permute-start | bytes 1228808 | tf_op jit(solution)/shard_map/ppermute | solution.py:441
  39.6 15.3 %collective-permute-start.9 = (f16[800,256]{1,0:T(8,128)(2,1)}, f16[800,256]{1,0:T(8,128)(2,1)}, u32[]{:S(2)}, u32[]{:S(2)}) collective-permute-start(f16[800,256]{1,0:T(8,128)(2,1)} %convert_element_type.34), channel_id=1, source_target_pairs={{0,16},{2,18},{4,20},{6,22},{24,8},{26,10},{28,12},{30,14},{1,17},... | collective-permute-start | bytes 1228808 | tf_op jit(solution)/shard_map/ppermute | solution.py:441
  45.1 1.9 %copy-start.2 = (f32[4,800,256]{2,1,0:T(8,128)S(1)}, f32[4,800,256]{2,1,0:T(8,128)}, u32[]{:S(2)}) copy-start(f32[4,800,256]{2,1,0:T(8,128)} %copy-done.1) | copy-start | bytes 9830404
  47.0 1.1 %copy-start.6 = (bf16[800,384]{1,0:T(8,128)(2,1)S(1)}, bf16[800,384]{1,0:T(8,128)(2,1)}, u32[]{:S(2)}) copy-start(bf16[800,384]{1,0:T(8,128)(2,1)} %copy-done.5) | copy-start | bytes 1843204
  48.1 1.0 %copy-start.8 = (bf16[128,1920]{1,0:T(8,128)(2,1)S(1)}, bf16[128,1920]{1,0:T(8,128)(2,1)}, u32[]{:S(2)}) copy-start(bf16[128,1920]{1,0:T(8,128)(2,1)} %copy-done.7) | copy-start | bytes 1474564
  49.1 1.0 %copy-start.10 = (bf16[128,1920]{1,0:T(8,128)(2,1)S(1)}, bf16[128,1920]{1,0:T(8,128)(2,1)}, u32[]{:S(2)}) copy-start(bf16[128,1920]{1,0:T(8,128)(2,1)} %copy-done.9) | copy-start | bytes 1474564
  51.9 0.9 copy-start.11
  52.8 2.1 %copy-start.12 = (f32[800,256]{1,0:T(8,128)S(1)}, f32[800,256]{1,0:T(8,128)}, u32[]{:S(2)}) copy-start(f32[800,256]{1,0:T(8,128)} %copy-done.11) | copy-start | bytes 2457604
  54.1 15.4 %collective-permute-start.11 = (f16[800,256]{1,0:T(8,128)(2,1)S(1)}, f16[800,256]{1,0:T(8,128)(2,1)}, u32[]{:S(2)}, u32[]{:S(2)}) collective-permute-start(f16[800,256]{1,0:T(8,128)(2,1)S(1)} %add_convert_fusion), channel_id=1, source_target_pairs={{0,8},{2,10},{4,12},{6,14},{8,24},{10,26},{12,28},{14,30},{24,16},... | collective-permute-start | bytes 1228808 | tf_op jit(solution)/shard_map/ppermute | solution.py:441
  71.3 5.1 %collective-permute-start.18 = (bf16[2,128,128]{2,1,0:T(8,128)(2,1)S(1)}, bf16[2,128,128]{2,1,0:T(8,128)(2,1)S(1)}, u32[]{:S(2)}, u32[]{:S(2)}) collective-permute-start(bf16[2,128,128]{2,1,0:T(8,128)(2,1)S(1)} %get-tuple-element.40), channel_id=1, source_target_pairs={{0,1},{1,0},{2,3},{3,2},{4,5},{5,4},{6,7},{7,6},{8,9},{9,8},{10,11... | collective-permute-start | bytes 196616 | tf_op jit(solution)/shard_map/ppermute | solution.py:141
  72.7 14.1 %collective-permute-start.12 = (f16[4,16,800]{2,1,0:T(8,128)(2,1)S(1)}, f16[4,16,800]{2,1,0:T(8,128)(2,1)S(1)}, u32[]{:S(2)}, u32[]{:S(2)}) collective-permute-start(f16[4,16,800]{2,1,0:T(8,128)(2,1)S(1)} %get-tuple-element.46), channel_id=1, source_target_pairs={{0,8},{2,10},{4,12},{6,14},{8,0},{10,2},{12,4},{14,6},{16,24},{18,... | collective-permute-start | bytes 307208 | tf_op jit(solution)/shard_map/ppermute | solution.py:441
  72.8 14.1 %collective-permute-start.13 = (f16[4,16,800]{2,1,0:T(8,128)(2,1)S(1)}, f16[4,16,800]{2,1,0:T(8,128)(2,1)S(1)}, u32[]{:S(2)}, u32[]{:S(2)}) collective-permute-start(f16[4,16,800]{2,1,0:T(8,128)(2,1)S(1)} %get-tuple-element.48), channel_id=1, source_target_pairs={{0,16},{2,18},{4,20},{6,22},{8,24},{10,26},{12,28},{14,30},{16,0},... | collective-permute-start | bytes 307208 | tf_op jit(solution)/shard_map/ppermute | solution.py:441
  75.1 11.9 %collective-permute-start.14 = (f16[4,16,800]{2,1,0:T(8,128)(2,1)S(1)}, f16[4,16,800]{2,1,0:T(8,128)(2,1)S(1)}, u32[]{:S(2)}, u32[]{:S(2)}) collective-permute-start(f16[4,16,800]{2,1,0:T(8,128)(2,1)S(1)} %get-tuple-element.47), channel_id=1, source_target_pairs={{0,24},{2,26},{4,28},{6,30},{8,16},{10,18},{12,20},{14,22},{16,8},... | collective-permute-start | bytes 307208 | tf_op jit(solution)/shard_map/ppermute | solution.py:441
  79.6 21.0 %all-to-all-start = ((bf16[16,16,800]{2,1,0:T(8,128)(2,1)}), bf16[16,16,800]{2,1,0:T(8,128)(2,1)S(1)}, u32[]{:S(2)}, u32[]{:S(2)}) async-start(bf16[16,16,800]{2,1,0:T(8,128)(2,1)} %shard_map.85), calls=%async_computation | async-start | bytes 917504 | tf_op jit(solution)/shard_map/all_to_all | solution.py:499
  86.8 11.9 %copy-start.16 = (f32[2,120,800]{1,2,0:T(8,128)S(1)}, f32[2,120,800]{1,2,0:T(8,128)}, u32[]{:S(2)}) copy-start(f32[2,120,800]{1,2,0:T(8,128)} %param.9) | copy-start | bytes 2304004
  87.1 2.5 %collective-permute-start.15 = (f16[4,16,800]{2,1,0:T(8,128)(2,1)S(1)}, f16[4,16,800]{2,1,0:T(8,128)(2,1)S(1)}, u32[]{:S(2)}, u32[]{:S(2)}) collective-permute-start(f16[4,16,800]{2,1,0:T(8,128)(2,1)S(1)} %pad_maximum_fusion), channel_id=1, source_target_pairs={{0,2},{2,0},{4,6},{6,4},{8,10},{10,8},{12,14},{14,12},{16,18},{18,... | collective-permute-start | bytes 307208 | tf_op jit(solution)/shard_map/ppermute | solution.py:487
  87.3 7.5 %collective-permute-start.16 = (f16[4,16,800]{2,1,0:T(8,128)(2,1)S(1)}, f16[4,16,800]{2,1,0:T(8,128)(2,1)S(1)}, u32[]{:S(2)}, u32[]{:S(2)}) collective-permute-start(f16[4,16,800]{2,1,0:T(8,128)(2,1)S(1)} %pad_maximum_fusion.1), channel_id=1, source_target_pairs={{0,4},{2,6},{4,0},{6,2},{8,12},{10,14},{12,8},{14,10},{16,20},{18,... | collective-permute-start | bytes 307208 | tf_op jit(solution)/shard_map/ppermute | solution.py:487
  89.0 9.6 %collective-permute-start.17 = (f16[4,16,800]{2,1,0:T(8,128)(2,1)S(1)}, f16[4,16,800]{2,1,0:T(8,128)(2,1)S(1)}, u32[]{:S(2)}, u32[]{:S(2)}) collective-permute-start(f16[4,16,800]{2,1,0:T(8,128)(2,1)S(1)} %pad_maximum_fusion.2), channel_id=1, source_target_pairs={{0,6},{2,4},{4,2},{6,0},{8,14},{10,12},{12,10},{14,8},{16,22},{18,... | collective-permute-start | bytes 307208 | tf_op jit(solution)/shard_map/ppermute | solution.py:487
  98.7 1.9 %copy-start.13 = (f32[2,120,800]{1,2,0:T(8,128)S(1)}, f32[2,120,800]{1,2,0:T(8,128)}, u32[]{:S(2)}) copy-start(f32[2,120,800]{1,2,0:T(8,128)} %param.10) | copy-start | bytes 2304004

commit v6 on v5

--- a/solution.py
+++ b/solution.py
@@ -34,6 +34,8 @@
 CHUNK_STEPS = len(CHUNK_ORDERS[0])
 CHUNK_SENDS = 2
 NO_HEAD = -(1 << 20)
+VALUE_MOST = 6.0
+F16_MOST = 65504.0
 HALF_HEAD = HEAD // 2
 
 
@@ -232,7 +234,7 @@
         out_ref[step] = chip_part(ext0[...], ext1[...], own[step], places)
 
 
-def chunk_kernel(table, ext2, ext3, near, far0, far1, own, *refs, factor, rows, steps):
+def chunk_kernel(table, ext2, ext3, near, far0, far1, own, *refs, factor, rows, steps, spread):
     *out_refs, lead, far = refs
     x, y = table[CHUNK_STEPS], table[CHUNK_STEPS + 2]
     half = far0.shape[0]
@@ -248,7 +250,7 @@
             total += contract(ext[:, :tokens], jnp.concatenate([low, high], axis=0), ((1,), (0,)))
         mixed_in = jnp.concatenate([ext2[:, tokens:], ext3[:, tokens:]], axis=1)
         total += contract(mixed_in, momentum_places(table, table[step], 1 - y, rows, 0.5 / factor), ((1,), (0,)))
-        out_ref[...] = total * factor
+        out_ref[...] = total * (factor * spread)
 
 
 def head_rows(value, head):
@@ -256,8 +258,8 @@
     return jnp.concatenate([first, second], axis=0)
 
 
-def gram_kernel(mixed, near_ref, far_ref):
-    block = (GAIN * mixed[...]).astype(BF16)
+def gram_kernel(mixed, near_ref, far_ref, *, spread):
+    block = (GAIN / spread * mixed[...]).astype(BF16)
     total = contract(block, block, ((0,), (0,)))
     for head in range(2):
         gram = head_rows(head_rows(total, head).T, head)
@@ -285,7 +287,7 @@
     return jnp.dot(left, right, precision=lax.Precision.HIGHEST, preferred_element_type=F32)
 
 
-def ortho_kernel(near, far, turned, out_ref):
+def ortho_kernel(near, far, turned, out_ref, *, spread):
     row = lax.broadcasted_iota(jnp.int32, (HEAD, HEAD), 0)
     column = lax.broadcasted_iota(jnp.int32, (HEAD, HEAD), 1)
     eye = (row == column).astype(F32)
@@ -306,7 +308,7 @@
         total = totals[head] * scales[head]
         high = total.astype(BF16)
         low = (total - high.astype(F32)).astype(BF16)
-        block = (GAIN * turned[head * HEAD : (head + 1) * HEAD]).astype(BF16)
+        block = (GAIN / spread * turned[head * HEAD : (head + 1) * HEAD]).astype(BF16)
         blocks.append(contract(high, block, ((1,), (0,))) + contract(low, block, ((1,), (0,))))
     store_by_owner(out_ref, blocks)
 
@@ -325,14 +327,14 @@
     return result
 
 
-def momentum_kernel(here, mixed_back, momentum, out_ref):
+def momentum_kernel(here, mixed_back, momentum, out_ref, *, spread):
     z, y, c = (here[index] for index in range(3))
     for layer in range(2):
         old = momentum[layer]
         pieces = [
             mixed_back[(y ^ layer) * SIZE_C + (c ^ core), z ^ chip] for chip in range(SIZE_Z) for core in range(SIZE_C)
         ]
-        gradient = to_rows(pieces)[:, : old.shape[1]] - 0.5 * mixed_part(old).astype(F32)
+        gradient = to_rows(pieces)[:, : old.shape[1]] * (1.0 / spread) - 0.5 * mixed_part(old).astype(F32)
         out_ref[layer] = momentum_rate * old + gradient
 
 
@@ -358,6 +360,7 @@
     z, y, c = where // (SIZE_Y * SIZE_C), where // SIZE_C % SIZE_Y, where % SIZE_C
     x = lax.axis_index("mp")
     factor = 1.0 / math.sqrt(tok_dev * lax.axis_size("dp"))
+    spread = 2.0 ** math.floor(math.log2(F16_MOST / (VALUE_MOST**2 / factor + VALUE_MOST)))
 
     half_send = lax.dynamic_slice(context, (1 - y, x * half, 0), (1, half, all_rows))[0]
     first0 = swap_y(half_send)
@@ -422,7 +425,7 @@
     one = jax.ShapeDtypeStruct((columns, lanes), F32)
     chunk = [
         planned(
-            functools.partial(chunk_kernel, factor=factor, rows=shard_rows, steps=steps),
+            functools.partial(chunk_kernel, factor=factor, rows=shard_rows, steps=steps, spread=spread),
             [one] * len(steps),
             ext2,
             ext3,
@@ -457,7 +460,7 @@
     owners = lax.axis_size("dp")
     by_owner = (owners, 2 * depth, columns)
     gram, gram_send = pl.pallas_call(
-        gram_kernel,
+        functools.partial(gram_kernel, spread=spread),
         out_shape=[jax.ShapeDtypeStruct((2, HEAD, HEAD), kind) for kind in (F32, BF16)],
         compiler_params=vmem_params(),
     )(mixed)
@@ -469,7 +472,7 @@
         cost_estimate=pl.CostEstimate(flops=10**10, bytes_accessed=2 * 10**6, transcendentals=0),
     )(after(mixed, gram))
     ortho_send = pl.pallas_call(
-        ortho_kernel,
+        functools.partial(ortho_kernel, spread=spread),
         out_shape=jax.ShapeDtypeStruct(by_owner, BF16),
         compiler_params=vmem_params(),
     )(gram, gram_far, turned)
@@ -490,7 +493,7 @@
 
     out = jax.ShapeDtypeStruct((layers, columns, shard_rows), F32)
     moment_new = pl.pallas_call(
-        momentum_kernel,
+        functools.partial(momentum_kernel, spread=spread),
         in_specs=[smem, vmem, vmem],
         out_shape=out,
         compiler_params=vmem_params(),

time: 103 us -> 103 us (level)
  no operation moved by 1% of the time
where the time goes in v6:
time: 103 us; the launch traced here: 102 us
  waiting for transfers between devices  34.6 us (34%)
  starting transfers between devices  31.8 us (31%)
  Pallas kernels  17.1 us (17%)
  local copies, waits for them, and re-layouts  10.8 us (10%)
  other arithmetic  5.84 us (6%)
  between operations  1.71 us (2%)
    ppermute x7, waiting for transfers between devices, along_z(): return lax.ppermute(value, 'dp', pairs)  13.8 us
    ppermute x7, starting transfers between devices, along_z(): return lax.ppermute(value, 'dp', pairs)  12.1 us
    unnamed x34, local copies, waits for them, and re-layouts  9.77 us
    pallas_call x4, Pallas kernels, planned(): pl.pallas_call(kernel, in_specs=[smem] + [vmem] * len(args), out_shape=ou...  9.1 us
    ppermute x3, waiting for transfers between devices, block_plan(): piece = lax.ppermute(piece, 'dp', [(k, k ^ apart) for k in range(owners)])  9.04 us
    ppermute x2, waiting for transfers between devices, swap_y(): lax.ppermute(value, 'dp', [(dp_index(z, y, c), dp_index(z, 1 - y, c)) for...  8.95 us
    all_to_all x1, starting transfers between devices, block_plan(): lax.all_to_all(ortho_send, 'dp', 0, 0)  7.2 us
    ppermute x5, starting transfers between devices, swap_core(): lax.ppermute(value, 'dp', [(dp_index(z, y, c), dp_index(z, y, 1 - c)) for...  5 us
  transfers between devices with their start and end apart: 20, of which 8 were waited for; matrix products, arithmetic and copies ran while one was open for 5% of the time, Pallas kernels for 13%

profile of v6, /device:TPU:1, one launch (start us, length us, event | category | flops | bytes accessed | tf_op | source)
XLA Modules:
  0.0 101.9 jit_solution(1367239437644504890)
XLA Ops:
  0.7 1.5 %copy-done = bf16[2,256,1920]{2,1,0:T(8,128)(2,1)S(1)} copy-done((bf16[2,256,1920]{2,1,0:T(8,128)(2,1)S(1)}, bf16[2,256,1920]{2,1,0:T(8,128)(2,1)}, u32[]{:S(2)}) %copy-start) | copy-done | bytes 1966104
  2.2 2.1 %collective-permute-start.1 = (bf16[128,1920]{1,0:T(8,128)(2,1)S(1)}, bf16[128,1920]{1,0:T(8,128)(2,1)}, u32[]{:S(2)}, u32[]{:S(2)}) collective-permute-start(bf16[128,1920]{1,0:T(8,128)(2,1)S(1)} %dynamic-slice_bitcast_fusion.1), channel_id=1, source_target_pairs={{0,4},{2,6},{4,0},{6,2},{8,12},{10,14},{12,8},{14,10},{16,20},{18,... | collective-permute-start | bytes 1474568 | tf_op jit(solution)/shard_map/ppermute | solution.py:139
  4.4 1.0 %collective-permute-start.3 = (bf16[256,1920]{1,0:T(8,128)(2,1)S(1)}, bf16[256,1920]{1,0:T(8,128)(2,1)}, u32[]{:S(2)}, u32[]{:S(2)}) collective-permute-start(bf16[256,1920]{1,0:T(8,128)(2,1)S(1)} %dynamic-slice_bitcast_fusion.ctx0), channel_id=1, source_target_pairs={{0,2},{2,0},{4,6},{6,4},{8,10},{10,8},{12,14},{14,12},{16,18},{18,... | collective-permute-start | bytes 2949128 | tf_op jit(solution)/shard_map/ppermute | solution.py:135
  5.4 0.7 fusion
  6.9 1.1 %copy-done.14 = bf16[2,256,800]{1,2,0:T(8,128)(2,1)S(1)} copy-done((bf16[2,256,800]{1,2,0:T(8,128)(2,1)S(1)}, bf16[2,256,800]{1,2,0:T(8,128)(2,1)}, u32[]{:S(2)}) %copy-start.14) | copy-done | bytes 819224
  8.0 1.1 %copy-done.15 = f32[2,120,800]{1,2,0:T(8,128)S(1)} copy-done((f32[2,120,800]{1,2,0:T(8,128)S(1)}, f32[2,120,800]{1,2,0:T(8,128)}, u32[]{:S(2)}) %copy-start.15) | copy-done | bytes 768024
  9.2 0.8 shard_map.77
  10.1 5.3 %collective-permute-done.1.first = bf16[128,1920]{1,0:T(8,128)(2,1)} collective-permute-done((bf16[128,1920]{1,0:T(8,128)(2,1)S(1)}, bf16[128,1920]{1,0:T(8,128)(2,1)}, u32[]{:S(2)}, u32[]{:S(2)}) %collective-permute-start.1) | collective-permute-done | bytes 491552 | tf_op jit(solution)/shard_map/ppermute | solution.py:139
  15.4 2.1 %collective-permute-start.2 = (bf16[128,1920]{1,0:T(8,128)(2,1)}, bf16[128,1920]{1,0:T(8,128)(2,1)S(1)}, u32[]{:S(2)}, u32[]{:S(2)}) collective-permute-start(bf16[128,1920]{1,0:T(8,128)(2,1)} %collective-permute-done.1.first), channel_id=1, source_target_pairs={{0,2},{2,0},{4,6},{6,4},{8,10},{10,8},{12,14},{14,12},{16,18},{18,... | collective-permute-start | bytes 1474568 | tf_op jit(solution)/shard_map/ppermute | solution.py:135
  17.5 1.7 %collective-permute-start.6 = (bf16[128,1920]{1,0:T(8,128)(2,1)}, bf16[128,1920]{1,0:T(8,128)(2,1)S(1)}, u32[]{:S(2)}, u32[]{:S(2)}) collective-permute-start(bf16[128,1920]{1,0:T(8,128)(2,1)} %collective-permute-done.1.first), channel_id=1, source_target_pairs={{0,1},{1,0},{2,3},{3,2},{4,5},{5,4},{6,7},{7,6},{8,9},{9,8},{10,11... | collective-permute-start | bytes 1474568 | tf_op jit(solution)/shard_map/ppermute | solution.py:143
  19.2 1.8 %shard_map.78.near = bf16[4,256,256]{2,1,0:T(8,128)(2,1)S(1)} custom-call(s32[8]{0:T(128)S(1)} %concatenate.3.table, bf16[128,1920]{1,0:T(8,128)(2,1)} %collective-permute-done.1.first, bf16[128,1920]{1,0:T(8,128)(2,1)S(1)} %collective-permute-done.2.second), custom_call_target="tpu_custom_call" | custom-call | flops 1000 | bytes 1000 | tf_op jit(solution)/shard_map/pallas_call | solution.py:396
  21.1 3.7 %shard_map.79.own = f32[4,800,256]{2,1,0:T(8,128)S(1)} custom-call(s32[8]{0:T(128)S(1)} %concatenate.3.table, bf16[256,1920]{1,0:T(8,128)(2,1)S(1)} %dynamic-slice_bitcast_fusion.ctx0, bf16[256,1920]{1,0:T(8,128)(2,1)} %collective-permute-done.3.ctx1, bf16[800,384]{1,0:T(8,128)(2,1)S(1)} %get-tuple-element.24.ext0, ...), custom_call_target="tpu_custom_call" | custom-call | flops 1000 | bytes 1000 | tf_op jit(solution)/shard_map/pallas_call | solution.py:396
  24.8 3.7 %collective-permute-done.ext2 = bf16[800,384]{1,0:T(8,128)(2,1)S(1)} collective-permute-done((bf16[800,384]{1,0:T(8,128)(2,1)S(1)}, bf16[800,384]{1,0:T(8,128)(2,1)S(1)}, u32[]{:S(2)}, u32[]{:S(2)}) %collective-permute-start) | collective-permute-done | bytes 614432 | tf_op jit(solution)/shard_map/ppermute | solution.py:139
  28.5 1.2 %collective-permute-start.5 = (bf16[800,384]{1,0:T(8,128)(2,1)S(1)}, bf16[800,384]{1,0:T(8,128)(2,1)S(1)}, u32[]{:S(2)}, u32[]{:S(2)}) collective-permute-start(bf16[800,384]{1,0:T(8,128)(2,1)S(1)} %collective-permute-done.ext2), channel_id=1, source_target_pairs={{0,2},{2,0},{4,6},{6,4},{8,10},{10,8},{12,14},{14,12},{16,18},{18,... | collective-permute-start | bytes 1843208 | tf_op jit(solution)/shard_map/ppermute | solution.py:135
  29.7 1.3 %collective-permute-done.6.far0 = bf16[128,1920]{1,0:T(8,128)(2,1)S(1)} collective-permute-done((bf16[128,1920]{1,0:T(8,128)(2,1)}, bf16[128,1920]{1,0:T(8,128)(2,1)S(1)}, u32[]{:S(2)}, u32[]{:S(2)}) %collective-permute-start.6) | collective-permute-done | bytes 491552 | tf_op jit(solution)/shard_map/ppermute | solution.py:143
  31.0 0.6 collective-permute-start.7
  31.6 1.5 %collective-permute-done.7.far1 = bf16[128,1920]{1,0:T(8,128)(2,1)S(1)} collective-permute-done((bf16[128,1920]{1,0:T(8,128)(2,1)S(1)}, bf16[128,1920]{1,0:T(8,128)(2,1)S(1)}, u32[]{:S(2)}, u32[]{:S(2)}) %collective-permute-start.7) | collective-permute-done | bytes 491552 | tf_op jit(solution)/shard_map/ppermute | solution.py:135
  33.1 1.8 %shard_map.81 = (f32[800,256]{1,0:T(8,128)S(1)}, f32[800,256]{1,0:T(8,128)S(1)}) custom-call(s32[8]{0:T(128)S(1)} %concatenate.3.table, bf16[800,384]{1,0:T(8,128)(2,1)S(1)} %collective-permute-done.ext2, bf16[800,384]{1,0:T(8,128)(2,1)S(1)} %collective-permute-done.5.ext3, bf16[4,256,256]{2,1,0:T(8,128)(2,1)S(1)} %shard_map.78.near, ...), custom_call_target="tpu_custom_call" | custom-call | flops 1000 | bytes 1000 | tf_op jit(solution)/shard_map/pallas_call | solution.py:396
  34.9 0.8 convert_element_type.30
  35.8 1.6 %collective-permute-start.8 = (f16[800,256]{1,0:T(8,128)(2,1)}, f16[800,256]{1,0:T(8,128)(2,1)}, u32[]{:S(2)}, u32[]{:S(2)}) collective-permute-start(f16[800,256]{1,0:T(8,128)(2,1)} %convert_element_type.30), channel_id=1, source_target_pairs={{0,8},{2,10},{4,12},{6,14},{8,0},{10,2},{12,4},{14,6},{16,24},{18,... | collective-permute-start | bytes 1228808 | tf_op jit(solution)/shard_map/ppermute | solution.py:444
  37.3 0.8 convert_element_type.34
  38.2 1.4 %collective-permute-start.10 = (f16[800,256]{1,0:T(8,128)(2,1)}, f16[800,256]{1,0:T(8,128)(2,1)}, u32[]{:S(2)}, u32[]{:S(2)}) collective-permute-start(f16[800,256]{1,0:T(8,128)(2,1)} %convert_element_type.34), channel_id=1, source_target_pairs={{8,16},{10,18},{12,20},{14,22},{16,8},{18,10},{20,12},{22,14},{9,1... | collective-permute-start | bytes 1228808 | tf_op jit(solution)/shard_map/ppermute | solution.py:444
  39.6 5.5 %collective-permute-start.9 = (f16[800,256]{1,0:T(8,128)(2,1)}, f16[800,256]{1,0:T(8,128)(2,1)}, u32[]{:S(2)}, u32[]{:S(2)}) collective-permute-start(f16[800,256]{1,0:T(8,128)(2,1)} %convert_element_type.34), channel_id=1, source_target_pairs={{0,16},{2,18},{4,20},{6,22},{24,8},{26,10},{28,12},{30,14},{1,17},... | collective-permute-start | bytes 1228808 | tf_op jit(solution)/shard_map/ppermute | solution.py:444
  45.1 1.9 %copy-done.2 = f32[4,800,256]{2,1,0:T(8,128)S(1)} copy-done((f32[4,800,256]{2,1,0:T(8,128)S(1)}, f32[4,800,256]{2,1,0:T(8,128)}, u32[]{:S(2)}) %copy-start.2) | copy-done | bytes 3276824
  47.0 1.1 %copy-done.6 = bf16[800,384]{1,0:T(8,128)(2,1)S(1)} copy-done((bf16[800,384]{1,0:T(8,128)(2,1)S(1)}, bf16[800,384]{1,0:T(8,128)(2,1)}, u32[]{:S(2)}) %copy-start.6) | copy-done | bytes 614424
  48.1 1.0 %copy-done.8 = bf16[128,1920]{1,0:T(8,128)(2,1)S(1)} copy-done((bf16[128,1920]{1,0:T(8,128)(2,1)S(1)}, bf16[128,1920]{1,0:T(8,128)(2,1)}, u32[]{:S(2)}) %copy-start.8) | copy-done | bytes 491544
  49.1 1.0 %copy-done.10 = bf16[128,1920]{1,0:T(8,128)(2,1)S(1)} copy-done((bf16[128,1920]{1,0:T(8,128)(2,1)S(1)}, bf16[128,1920]{1,0:T(8,128)(2,1)}, u32[]{:S(2)}) %copy-start.10) | copy-done | bytes 491544
  50.1 1.8 %shard_map.80 = (f32[800,256]{1,0:T(8,128)S(1)}, f32[800,256]{1,0:T(8,128)S(1)}) custom-call(s32[8]{0:T(128)S(1)} %concatenate.3.table, bf16[800,384]{1,0:T(8,128)(2,1)S(1)} %copy-done.4, bf16[800,384]{1,0:T(8,128)(2,1)S(1)} %copy-done.6, bf16[4,256,256]{2,1,0:T(8,128)(2,1)S(1)} %shard_map.78.near, bf16[128,1920]{1,0:T(8,128)(2,1)S(1)} %copy-done.8, ...), custom_call_target="tpu_custom_call" | custom-call | flops 1000 | bytes 1000 | tf_op jit(solution)/shard_map/pallas_call | solution.py:396
  51.9 0.9 copy-done.11
  52.8 1.2 %add_convert_fusion = f16[800,256]{1,0:T(8,128)(2,1)S(1)} fusion(f32[800,256]{1,0:T(8,128)S(1)} %get-tuple-element.32, f16[800,256]{1,0:T(8,128)(2,1)} %collective-permute-done.8, pred[]{:T(512)S(6)} %or.3), kind=kLoop, calls=%fused_computation.3 | loop fusion | flops 819200 | bytes 1638401 | tf_op jit(solution)/shard_map/convert_element_type | solution.py:454
  54.3 0.7 collective-permute-done.9
  55.0 1.4 %add_add_fusion = f32[800,256]{1,0:T(8,128)S(1)} fusion(f16[800,256]{1,0:T(8,128)(2,1)} %collective-permute-done.10, f16[800,256]{1,0:T(8,128)(2,1)} %collective-permute-done.9, f32[800,256]{1,0:T(8,128)S(1)} %copy-done.12, f16[800,256]{1,0:T(8,128)(2,1)} %collective-permute-done.8, pred[]{:T(512)S(6)} %not.3), kind=kLoop, calls=%fused_computation.2 | loop fusion | flops 1433600 | bytes 2867201 | tf_op jit(solution)/shard_map/add | solution.py:456
  56.4 13.1 %collective-permute-done.11 = f16[800,256]{1,0:T(8,128)(2,1)} collective-permute-done((f16[800,256]{1,0:T(8,128)(2,1)S(1)}, f16[800,256]{1,0:T(8,128)(2,1)}, u32[]{:S(2)}, u32[]{:S(2)}) %collective-permute-start.11) | collective-permute-done | bytes 409632 | tf_op jit(solution)/shard_map/ppermute | solution.py:444
  69.5 1.1 %convert_add_fusion.mixed = f32[800,256]{1,0:T(8,128)S(1)} fusion(f32[800,256]{1,0:T(8,128)S(1)} %add_add_fusion, f16[800,256]{1,0:T(8,128)(2,1)} %collective-permute-done.11), kind=kLoop, calls=%fused_computation.1 | loop fusion | flops 409600 | bytes 2048000 | tf_op jit(solution)/shard_map/add | solution.py:458
  70.5 0.4 shard_map.82
  71.0 0.3 shard_map.83
  71.3 1.3 %collective-permute-start.18 = (bf16[2,128,128]{2,1,0:T(8,128)(2,1)S(1)}, bf16[2,128,128]{2,1,0:T(8,128)(2,1)S(1)}, u32[]{:S(2)}, u32[]{:S(2)}) collective-permute-start(bf16[2,128,128]{2,1,0:T(8,128)(2,1)S(1)} %get-tuple-element.40), channel_id=1, source_target_pairs={{0,1},{1,0},{2,3},{3,2},{4,5},{5,4},{6,7},{7,6},{8,9},{9,8},{10,11... | collective-permute-start | bytes 196616 | tf_op jit(solution)/shard_map/ppermute | solution.py:143
  72.8 2.3 %collective-permute-start.13 = (f16[4,16,800]{2,1,0:T(8,128)(2,1)S(1)}, f16[4,16,800]{2,1,0:T(8,128)(2,1)S(1)}, u32[]{:S(2)}, u32[]{:S(2)}) collective-permute-start(f16[4,16,800]{2,1,0:T(8,128)(2,1)S(1)} %get-tuple-element.48), channel_id=1, source_target_pairs={{0,16},{2,18},{4,20},{6,22},{8,24},{10,26},{12,28},{14,30},{16,0},... | collective-permute-start | bytes 307208 | tf_op jit(solution)/shard_map/ppermute | solution.py:444
  75.1 1.2 %collective-permute-start.14 = (f16[4,16,800]{2,1,0:T(8,128)(2,1)S(1)}, f16[4,16,800]{2,1,0:T(8,128)(2,1)S(1)}, u32[]{:S(2)}, u32[]{:S(2)}) collective-permute-start(f16[4,16,800]{2,1,0:T(8,128)(2,1)S(1)} %get-tuple-element.47), channel_id=1, source_target_pairs={{0,24},{2,26},{4,28},{6,30},{8,16},{10,18},{12,20},{14,22},{16,8},... | collective-permute-start | bytes 307208 | tf_op jit(solution)/shard_map/ppermute | solution.py:444
  76.4 3.3 %shard_map.85 = bf16[16,16,800]{2,1,0:T(8,128)(2,1)} custom-call(f32[2,128,128]{2,1,0:T(8,128)S(1)} %get-tuple-element.37.near, bf16[2,128,128]{2,1,0:T(8,128)(2,1)S(1)} %collective-permute-done.18.far, f32[256,800]{1,0:T(8,128)S(1)} %get-tuple-element.41.turned), custom_call_target="tpu_custom_call" | custom-call | tf_op jit(solution)/shard_map/pallas_call | solution.py:474
  79.6 7.2 %all-to-all-start = ((bf16[16,16,800]{2,1,0:T(8,128)(2,1)}), bf16[16,16,800]{2,1,0:T(8,128)(2,1)S(1)}, u32[]{:S(2)}, u32[]{:S(2)}) async-start(bf16[16,16,800]{2,1,0:T(8,128)(2,1)} %shard_map.85), calls=%async_computation | async-start | bytes 917504 | tf_op jit(solution)/shard_map/all_to_all | solution.py:502
  87.1 0.2 collective-permute-start.15
  87.3 1.7 %collective-permute-start.16 = (f16[4,16,800]{2,1,0:T(8,128)(2,1)S(1)}, f16[4,16,800]{2,1,0:T(8,128)(2,1)S(1)}, u32[]{:S(2)}, u32[]{:S(2)}) collective-permute-start(f16[4,16,800]{2,1,0:T(8,128)(2,1)S(1)} %pad_maximum_fusion.1), channel_id=1, source_target_pairs={{0,4},{2,6},{4,0},{6,2},{8,12},{10,14},{12,8},{14,10},{16,20},{18,... | collective-permute-start | bytes 307208 | tf_op jit(solution)/shard_map/ppermute | solution.py:490
  89.0 0.5 collective-permute-start.17
  89.5 5.2 %collective-permute-done.16 = f16[4,16,800]{2,1,0:T(8,128)(2,1)S(1)} collective-permute-done((f16[4,16,800]{2,1,0:T(8,128)(2,1)S(1)}, f16[4,16,800]{2,1,0:T(8,128)(2,1)S(1)}, u32[]{:S(2)}, u32[]{:S(2)}) %collective-permute-start.16) | collective-permute-done | bytes 102432 | tf_op jit(solution)/shard_map/ppermute | solution.py:490
  94.7 3.9 %collective-permute-done.17 = f16[4,16,800]{2,1,0:T(8,128)(2,1)S(1)} collective-permute-done((f16[4,16,800]{2,1,0:T(8,128)(2,1)S(1)}, f16[4,16,800]{2,1,0:T(8,128)(2,1)S(1)}, u32[]{:S(2)}, u32[]{:S(2)}) %collective-permute-start.17) | collective-permute-done | bytes 102432 | tf_op jit(solution)/shard_map/ppermute | solution.py:490
  98.7 1.9 %shard_map.84 = f32[2,800,120]{2,1,0:T(8,128)} custom-call(s32[3]{0:T(128)S(1)} %pad_add_fusion.here, f32[4,4,16,800]{3,2,1,0:T(8,128)S(1)} %maximum_convert_fusion.mixed_back, f32[2,800,120]{2,1,0:T(8,128)S(1)} %bitcast.40), custom_call_target="tpu_custom_call" | custom-call | flops 10000000000 | bytes 2000000 | tf_op jit(solution)/shard_map/pallas_call | solution.py:495
  100.7 1.2 %shard_map.86 = f32[2,800,120]{2,1,0:T(8,128)} custom-call(bf16[4,2,2,16,800]{4,3,2,1,0:T(8,128)(2,1)S(1)} %bitcast.36, f32[2,800,120]{2,1,0:T(8,128)S(1)} %bitcast.37), custom_call_target="tpu_custom_call" | custom-call | tf_op jit(solution)/shard_map/pallas_call | solution.py:503
  (57 shorter events, 1.2 us)
Async XLA Ops:
  0.6 1.6 %copy-start = (bf16[2,256,1920]{2,1,0:T(8,128)(2,1)S(1)}, bf16[2,256,1920]{2,1,0:T(8,128)(2,1)}, u32[]{:S(2)}) copy-start(bf16[2,256,1920]{2,1,0:T(8,128)(2,1)} %param.6) | copy-start | bytes 5898244
  2.2 13.2 %collective-permute-start.1 = (bf16[128,1920]{1,0:T(8,128)(2,1)S(1)}, bf16[128,1920]{1,0:T(8,128)(2,1)}, u32[]{:S(2)}, u32[]{:S(2)}) collective-permute-start(bf16[128,1920]{1,0:T(8,128)(2,1)S(1)} %dynamic-slice_bitcast_fusion.1), channel_id=1, source_target_pairs={{0,4},{2,6},{4,0},{6,2},{8,12},{10,14},{12,8},{14,10},{16,20},{18,... | collective-permute-start | bytes 1474568 | tf_op jit(solution)/shard_map/ppermute | solution.py:139
  4.4 16.6 %collective-permute-start.3 = (bf16[256,1920]{1,0:T(8,128)(2,1)S(1)}, bf16[256,1920]{1,0:T(8,128)(2,1)}, u32[]{:S(2)}, u32[]{:S(2)}) collective-permute-start(bf16[256,1920]{1,0:T(8,128)(2,1)S(1)} %dynamic-slice_bitcast_fusion.ctx0), channel_id=1, source_target_pairs={{0,2},{2,0},{4,6},{6,4},{8,10},{10,8},{12,14},{14,12},{16,18},{18,... | collective-permute-start | bytes 2949128 | tf_op jit(solution)/shard_map/ppermute | solution.py:135
  6.9 1.1 %copy-start.14 = (bf16[2,256,800]{1,2,0:T(8,128)(2,1)S(1)}, bf16[2,256,800]{1,2,0:T(8,128)(2,1)}, u32[]{:S(2)}) copy-start(bf16[2,256,800]{1,2,0:T(8,128)(2,1)} %param.7) | copy-start | bytes 2457604
  8.0 1.1 %copy-start.15 = (f32[2,120,800]{1,2,0:T(8,128)S(1)}, f32[2,120,800]{1,2,0:T(8,128)}, u32[]{:S(2)}) copy-start(f32[2,120,800]{1,2,0:T(8,128)} %param.9) | copy-start | bytes 2304004
  9.9 11.1 %collective-permute-start.4 = (bf16[800,384]{1,0:T(8,128)(2,1)S(1)}, bf16[800,384]{1,0:T(8,128)(2,1)S(1)}, u32[]{:S(2)}, u32[]{:S(2)}) collective-permute-start(bf16[800,384]{1,0:T(8,128)(2,1)S(1)} %get-tuple-element.24.ext0), channel_id=1, source_target_pairs={{0,2},{2,0},{4,6},{6,4},{8,10},{10,8},{12,14},{14,12},{16,18},{18,... | collective-permute-start | bytes 1843208 | tf_op jit(solution)/shard_map/ppermute | solution.py:135
  10.1 18.4 %collective-permute-start = (bf16[800,384]{1,0:T(8,128)(2,1)S(1)}, bf16[800,384]{1,0:T(8,128)(2,1)S(1)}, u32[]{:S(2)}, u32[]{:S(2)}) collective-permute-start(bf16[800,384]{1,0:T(8,128)(2,1)S(1)} %get-tuple-element.23), channel_id=1, source_target_pairs={{0,4},{2,6},{4,0},{6,2},{8,12},{10,14},{12,8},{14,10},{16,20},{18,... | collective-permute-start | bytes 1843208 | tf_op jit(solution)/shard_map/ppermute | solution.py:139
  15.4 3.8 %collective-permute-start.2 = (bf16[128,1920]{1,0:T(8,128)(2,1)}, bf16[128,1920]{1,0:T(8,128)(2,1)S(1)}, u32[]{:S(2)}, u32[]{:S(2)}) collective-permute-start(bf16[128,1920]{1,0:T(8,128)(2,1)} %collective-permute-done.1.first), channel_id=1, source_target_pairs={{0,2},{2,0},{4,6},{6,4},{8,10},{10,8},{12,14},{14,12},{16,18},{18,... | collective-permute-start | bytes 1474568 | tf_op jit(solution)/shard_map/ppermute | solution.py:135
  17.5 13.6 %collective-permute-start.6 = (bf16[128,1920]{1,0:T(8,128)(2,1)}, bf16[128,1920]{1,0:T(8,128)(2,1)S(1)}, u32[]{:S(2)}, u32[]{:S(2)}) collective-permute-start(bf16[128,1920]{1,0:T(8,128)(2,1)} %collective-permute-done.1.first), channel_id=1, source_target_pairs={{0,1},{1,0},{2,3},{3,2},{4,5},{5,4},{6,7},{7,6},{8,9},{9,8},{10,11... | collective-permute-start | bytes 1474568 | tf_op jit(solution)/shard_map/ppermute | solution.py:143
  24.8 10.1 %copy-start.1 = (f32[4,800,256]{2,1,0:T(8,128)}, f32[4,800,256]{2,1,0:T(8,128)S(1)}, u32[]{:S(2)}) copy-start(f32[4,800,256]{2,1,0:T(8,128)S(1)} %shard_map.79.own) | copy-start | bytes 9830404
  28.5 6.4 %copy-start.3 = (bf16[800,384]{1,0:T(8,128)(2,1)}, bf16[800,384]{1,0:T(8,128)(2,1)S(1)}, u32[]{:S(2)}) copy-start(bf16[800,384]{1,0:T(8,128)(2,1)S(1)} %collective-permute-done.ext2) | copy-start | bytes 1843204
  28.5 4.6 %collective-permute-start.5 = (bf16[800,384]{1,0:T(8,128)(2,1)S(1)}, bf16[800,384]{1,0:T(8,128)(2,1)S(1)}, u32[]{:S(2)}, u32[]{:S(2)}) collective-permute-start(bf16[800,384]{1,0:T(8,128)(2,1)S(1)} %collective-permute-done.ext2), channel_id=1, source_target_pairs={{0,2},{2,0},{4,6},{6,4},{8,10},{10,8},{12,14},{14,12},{16,18},{18,... | collective-permute-start | bytes 1843208 | tf_op jit(solution)/shard_map/ppermute | solution.py:135
  31.0 3.9 %copy-start.7 = (bf16[128,1920]{1,0:T(8,128)(2,1)}, bf16[128,1920]{1,0:T(8,128)(2,1)S(1)}, u32[]{:S(2)}) copy-start(bf16[128,1920]{1,0:T(8,128)(2,1)S(1)} %collective-permute-done.6.far0) | copy-start | bytes 1474564
  31.0 2.1 %collective-permute-start.7 = (bf16[128,1920]{1,0:T(8,128)(2,1)S(1)}, bf16[128,1920]{1,0:T(8,128)(2,1)S(1)}, u32[]{:S(2)}, u32[]{:S(2)}) collective-permute-start(bf16[128,1920]{1,0:T(8,128)(2,1)S(1)} %collective-permute-done.6.far0), channel_id=1, source_target_pairs={{0,2},{2,0},{4,6},{6,4},{8,10},{10,8},{12,14},{14,12},{16,18},{18,... | collective-permute-start | bytes 1474568 | tf_op jit(solution)/shard_map/ppermute | solution.py:135
  33.1 1.8 %copy-start.9 = (bf16[128,1920]{1,0:T(8,128)(2,1)}, bf16[128,1920]{1,0:T(8,128)(2,1)S(1)}, u32[]{:S(2)}) copy-start(bf16[128,1920]{1,0:T(8,128)(2,1)S(1)} %collective-permute-done.7.far1) | copy-start | bytes 1474564
  33.1 1.8 %copy-start.5 = (bf16[800,384]{1,0:T(8,128)(2,1)}, bf16[800,384]{1,0:T(8,128)(2,1)S(1)}, u32[]{:S(2)}) copy-start(bf16[800,384]{1,0:T(8,128)(2,1)S(1)} %collective-permute-done.5.ext3) | copy-start | bytes 1843204
  34.9 10.1 %copy-start.4 = (bf16[800,384]{1,0:T(8,128)(2,1)S(1)}, bf16[800,384]{1,0:T(8,128)(2,1)}, u32[]{:S(2)}) copy-start(bf16[800,384]{1,0:T(8,128)(2,1)} %copy-done.3) | copy-start | bytes 1843204
  35.8 17.0 %collective-permute-start.8 = (f16[800,256]{1,0:T(8,128)(2,1)}, f16[800,256]{1,0:T(8,128)(2,1)}, u32[]{:S(2)}, u32[]{:S(2)}) collective-permute-start(f16[800,256]{1,0:T(8,128)(2,1)} %convert_element_type.30), channel_id=1, source_target_pairs={{0,8},{2,10},{4,12},{6,14},{8,0},{10,2},{12,4},{14,6},{16,24},{18,... | collective-permute-start | bytes 1228808 | tf_op jit(solution)/shard_map/ppermute | solution.py:444
  38.2 16.1 %collective-permute-start.10 = (f16[800,256]{1,0:T(8,128)(2,1)}, f16[800,256]{1,0:T(8,128)(2,1)}, u32[]{:S(2)}, u32[]{:S(2)}) collective-permute-start(f16[800,256]{1,0:T(8,128)(2,1)} %convert_element_type.34), channel_id=1, source_target_pairs={{8,16},{10,18},{12,20},{14,22},{16,8},{18,10},{20,12},{22,14},{9,1... | collective-permute-start | bytes 1228808 | tf_op jit(solution)/shard_map/ppermute | solution.py:444
  39.6 15.3 %collective-permute-start.9 = (f16[800,256]{1,0:T(8,128)(2,1)}, f16[800,256]{1,0:T(8,128)(2,1)}, u32[]{:S(2)}, u32[]{:S(2)}) collective-permute-start(f16[800,256]{1,0:T(8,128)(2,1)} %convert_element_type.34), channel_id=1, source_target_pairs={{0,16},{2,18},{4,20},{6,22},{24,8},{26,10},{28,12},{30,14},{1,17},... | collective-permute-start | bytes 1228808 | tf_op jit(solution)/shard_map/ppermute | solution.py:444
  45.1 1.9 %copy-start.2 = (f32[4,800,256]{2,1,0:T(8,128)S(1)}, f32[4,800,256]{2,1,0:T(8,128)}, u32[]{:S(2)}) copy-start(f32[4,800,256]{2,1,0:T(8,128)} %copy-done.1) | copy-start | bytes 9830404
  47.0 1.1 %copy-start.6 = (bf16[800,384]{1,0:T(8,128)(2,1)S(1)}, bf16[800,384]{1,0:T(8,128)(2,1)}, u32[]{:S(2)}) copy-start(bf16[800,384]{1,0:T(8,128)(2,1)} %copy-done.5) | copy-start | bytes 1843204
  48.1 1.0 %copy-start.8 = (bf16[128,1920]{1,0:T(8,128)(2,1)S(1)}, bf16[128,1920]{1,0:T(8,128)(2,1)}, u32[]{:S(2)}) copy-start(bf16[128,1920]{1,0:T(8,128)(2,1)} %copy-done.7) | copy-start | bytes 1474564
  49.1 1.0 %copy-start.10 = (bf16[128,1920]{1,0:T(8,128)(2,1)S(1)}, bf16[128,1920]{1,0:T(8,128)(2,1)}, u32[]{:S(2)}) copy-start(bf16[128,1920]{1,0:T(8,128)(2,1)} %copy-done.9) | copy-start | bytes 1474564
  51.9 0.9 copy-start.11
  52.8 2.1 %copy-start.12 = (f32[800,256]{1,0:T(8,128)S(1)}, f32[800,256]{1,0:T(8,128)}, u32[]{:S(2)}) copy-start(f32[800,256]{1,0:T(8,128)} %copy-done.11) | copy-start | bytes 2457604
  54.1 15.4 %collective-permute-start.11 = (f16[800,256]{1,0:T(8,128)(2,1)S(1)}, f16[800,256]{1,0:T(8,128)(2,1)}, u32[]{:S(2)}, u32[]{:S(2)}) collective-permute-start(f16[800,256]{1,0:T(8,128)(2,1)S(1)} %add_convert_fusion), channel_id=1, source_target_pairs={{0,8},{2,10},{4,12},{6,14},{8,24},{10,26},{12,28},{14,30},{24,16},... | collective-permute-start | bytes 1228808 | tf_op jit(solution)/shard_map/ppermute | solution.py:444
  71.3 5.1 %collective-permute-start.18 = (bf16[2,128,128]{2,1,0:T(8,128)(2,1)S(1)}, bf16[2,128,128]{2,1,0:T(8,128)(2,1)S(1)}, u32[]{:S(2)}, u32[]{:S(2)}) collective-permute-start(bf16[2,128,128]{2,1,0:T(8,128)(2,1)S(1)} %get-tuple-element.40), channel_id=1, source_target_pairs={{0,1},{1,0},{2,3},{3,2},{4,5},{5,4},{6,7},{7,6},{8,9},{9,8},{10,11... | collective-permute-start | bytes 196616 | tf_op jit(solution)/shard_map/ppermute | solution.py:143
  72.7 14.1 %collective-permute-start.12 = (f16[4,16,800]{2,1,0:T(8,128)(2,1)S(1)}, f16[4,16,800]{2,1,0:T(8,128)(2,1)S(1)}, u32[]{:S(2)}, u32[]{:S(2)}) collective-permute-start(f16[4,16,800]{2,1,0:T(8,128)(2,1)S(1)} %get-tuple-element.46), channel_id=1, source_target_pairs={{0,8},{2,10},{4,12},{6,14},{8,0},{10,2},{12,4},{14,6},{16,24},{18,... | collective-permute-start | bytes 307208 | tf_op jit(solution)/shard_map/ppermute | solution.py:444
  72.8 14.1 %collective-permute-start.13 = (f16[4,16,800]{2,1,0:T(8,128)(2,1)S(1)}, f16[4,16,800]{2,1,0:T(8,128)(2,1)S(1)}, u32[]{:S(2)}, u32[]{:S(2)}) collective-permute-start(f16[4,16,800]{2,1,0:T(8,128)(2,1)S(1)} %get-tuple-element.48), channel_id=1, source_target_pairs={{0,16},{2,18},{4,20},{6,22},{8,24},{10,26},{12,28},{14,30},{16,0},... | collective-permute-start | bytes 307208 | tf_op jit(solution)/shard_map/ppermute | solution.py:444
  75.1 11.9 %collective-permute-start.14 = (f16[4,16,800]{2,1,0:T(8,128)(2,1)S(1)}, f16[4,16,800]{2,1,0:T(8,128)(2,1)S(1)}, u32[]{:S(2)}, u32[]{:S(2)}) collective-permute-start(f16[4,16,800]{2,1,0:T(8,128)(2,1)S(1)} %get-tuple-element.47), channel_id=1, source_target_pairs={{0,24},{2,26},{4,28},{6,30},{8,16},{10,18},{12,20},{14,22},{16,8},... | collective-permute-start | bytes 307208 | tf_op jit(solution)/shard_map/ppermute | solution.py:444
  79.6 21.0 %all-to-all-start = ((bf16[16,16,800]{2,1,0:T(8,128)(2,1)}), bf16[16,16,800]{2,1,0:T(8,128)(2,1)S(1)}, u32[]{:S(2)}, u32[]{:S(2)}) async-start(bf16[16,16,800]{2,1,0:T(8,128)(2,1)} %shard_map.85), calls=%async_computation | async-start | bytes 917504 | tf_op jit(solution)/shard_map/all_to_all | solution.py:502
  86.8 11.9 %copy-start.16 = (f32[2,120,800]{1,2,0:T(8,128)S(1)}, f32[2,120,800]{1,2,0:T(8,128)}, u32[]{:S(2)}) copy-start(f32[2,120,800]{1,2,0:T(8,128)} %param.9) | copy-start | bytes 2304004
  87.1 2.5 %collective-permute-start.15 = (f16[4,16,800]{2,1,0:T(8,128)(2,1)S(1)}, f16[4,16,800]{2,1,0:T(8,128)(2,1)S(1)}, u32[]{:S(2)}, u32[]{:S(2)}) collective-permute-start(f16[4,16,800]{2,1,0:T(8,128)(2,1)S(1)} %pad_maximum_fusion), channel_id=1, source_target_pairs={{0,2},{2,0},{4,6},{6,4},{8,10},{10,8},{12,14},{14,12},{16,18},{18,... | collective-permute-start | bytes 307208 | tf_op jit(solution)/shard_map/ppermute | solution.py:490
  87.3 7.5 %collective-permute-start.16 = (f16[4,16,800]{2,1,0:T(8,128)(2,1)S(1)}, f16[4,16,800]{2,1,0:T(8,128)(2,1)S(1)}, u32[]{:S(2)}, u32[]{:S(2)}) collective-permute-start(f16[4,16,800]{2,1,0:T(8,128)(2,1)S(1)} %pad_maximum_fusion.1), channel_id=1, source_target_pairs={{0,4},{2,6},{4,0},{6,2},{8,12},{10,14},{12,8},{14,10},{16,20},{18,... | collective-permute-start | bytes 307208 | tf_op jit(solution)/shard_map/ppermute | solution.py:490
  89.0 9.6 %collective-permute-start.17 = (f16[4,16,800]{2,1,0:T(8,128)(2,1)S(1)}, f16[4,16,800]{2,1,0:T(8,128)(2,1)S(1)}, u32[]{:S(2)}, u32[]{:S(2)}) collective-permute-start(f16[4,16,800]{2,1,0:T(8,128)(2,1)S(1)} %pad_maximum_fusion.2), channel_id=1, source_target_pairs={{0,6},{2,4},{4,2},{6,0},{8,14},{10,12},{12,10},{14,8},{16,22},{18,... | collective-permute-start | bytes 307208 | tf_op jit(solution)/shard_map/ppermute | solution.py:490
  98.7 2.0 %copy-start.13 = (f32[2,120,800]{1,2,0:T(8,128)S(1)}, f32[2,120,800]{1,2,0:T(8,128)}, u32[]{:S(2)}) copy-start(f32[2,120,800]{1,2,0:T(8,128)} %param.10) | copy-start | bytes 2304004

commit v7 on v6

--- a/solution.py
+++ b/solution.py
@@ -284,7 +284,12 @@
 
 
 def square_dot(left, right):
-    return jnp.dot(left, right, precision=lax.Precision.HIGHEST, preferred_element_type=F32)
+    left_high, right_high = left.astype(BF16), right.astype(BF16)
+    left_low = (left - left_high.astype(F32)).astype(BF16)
+    right_low = (right - right_high.astype(F32)).astype(BF16)
+    lefts = jnp.concatenate([left_high, left_low, left_high], axis=1)
+    rights = jnp.concatenate([right_high, right_high, right_low], axis=0)
+    return contract(lefts, rights, ((1,), (0,)))
 
 
 def ortho_kernel(near, far, turned, out_ref, *, spread):

time: 103 us -> 102 us (level)
  transfers between devices with their start and end apart: 20 -> 20, of which waited for: 8 -> 8; matrix products, arithmetic and copies ran while one was open for 5% -> 5% of each run, Pallas kernels for 13% -> 12%
where the time goes in v7:
time: 102 us; the launch traced here: 101 us
  waiting for transfers between devices  34.6 us (34%)
  starting transfers between devices  31.8 us (31%)
  Pallas kernels  16.3 us (16%)
  local copies, waits for them, and re-layouts  10.8 us (11%)
  other arithmetic  5.84 us (6%)
  between operations  1.71 us (2%)
    ppermute x7, waiting for transfers between devices, along_z(): return lax.ppermute(value, 'dp', pairs)  13.8 us
    ppermute x7, starting transfers between devices, along_z(): return lax.ppermute(value, 'dp', pairs)  12.1 us
    unnamed x34, local copies, waits for them, and re-layouts  9.77 us
    pallas_call x4, Pallas kernels, planned(): pl.pallas_call(kernel, in_specs=[smem] + [vmem] * len(args), out_shape=ou...  9.1 us
    ppermute x3, waiting for transfers between devices, block_plan(): piece = lax.ppermute(piece, 'dp', [(k, k ^ apart) for k in range(owners)])  9.04 us
    ppermute x2, waiting for transfers between devices, swap_y(): lax.ppermute(value, 'dp', [(dp_index(z, y, c), dp_index(z, 1 - y, c)) for...  8.95 us
    all_to_all x1, starting transfers between devices, block_plan(): lax.all_to_all(ortho_send, 'dp', 0, 0)  7.2 us
    ppermute x5, starting transfers between devices, swap_core(): lax.ppermute(value, 'dp', [(dp_index(z, y, c), dp_index(z, y, 1 - c)) for...  5 us
  transfers between devices with their start and end apart: 20, of which 8 were waited for; matrix products, arithmetic and copies ran while one was open for 5% of the time, Pallas kernels for 12%

profile of v7, /device:TPU:1, one launch (start us, length us, event | category | flops | bytes accessed | tf_op | source)
XLA Modules:
  0.0 101.1 jit_solution(13815802266330326821)
XLA Ops:
  0.7 1.5 %copy-done = bf16[2,256,1920]{2,1,0:T(8,128)(2,1)S(1)} copy-done((bf16[2,256,1920]{2,1,0:T(8,128)(2,1)S(1)}, bf16[2,256,1920]{2,1,0:T(8,128)(2,1)}, u32[]{:S(2)}) %copy-start) | copy-done | bytes 1966104
  2.2 2.1 %collective-permute-start.1 = (bf16[128,1920]{1,0:T(8,128)(2,1)S(1)}, bf16[128,1920]{1,0:T(8,128)(2,1)}, u32[]{:S(2)}, u32[]{:S(2)}) collective-permute-start(bf16[128,1920]{1,0:T(8,128)(2,1)S(1)} %dynamic-slice_bitcast_fusion.1), channel_id=1, source_target_pairs={{0,4},{2,6},{4,0},{6,2},{8,12},{10,14},{12,8},{14,10},{16,20},{18,... | collective-permute-start | bytes 1474568 | tf_op jit(solution)/shard_map/ppermute | solution.py:139
  4.4 1.0 %collective-permute-start.3 = (bf16[256,1920]{1,0:T(8,128)(2,1)S(1)}, bf16[256,1920]{1,0:T(8,128)(2,1)}, u32[]{:S(2)}, u32[]{:S(2)}) collective-permute-start(bf16[256,1920]{1,0:T(8,128)(2,1)S(1)} %dynamic-slice_bitcast_fusion.ctx0), channel_id=1, source_target_pairs={{0,2},{2,0},{4,6},{6,4},{8,10},{10,8},{12,14},{14,12},{16,18},{18,... | collective-permute-start | bytes 2949128 | tf_op jit(solution)/shard_map/ppermute | solution.py:135
  5.4 0.7 fusion
  6.9 1.1 %copy-done.14 = bf16[2,256,800]{1,2,0:T(8,128)(2,1)S(1)} copy-done((bf16[2,256,800]{1,2,0:T(8,128)(2,1)S(1)}, bf16[2,256,800]{1,2,0:T(8,128)(2,1)}, u32[]{:S(2)}) %copy-start.14) | copy-done | bytes 819224
  8.0 1.1 %copy-done.15 = f32[2,120,800]{1,2,0:T(8,128)S(1)} copy-done((f32[2,120,800]{1,2,0:T(8,128)S(1)}, f32[2,120,800]{1,2,0:T(8,128)}, u32[]{:S(2)}) %copy-start.15) | copy-done | bytes 768024
  9.2 0.8 shard_map.77
  10.1 5.3 %collective-permute-done.1.first = bf16[128,1920]{1,0:T(8,128)(2,1)} collective-permute-done((bf16[128,1920]{1,0:T(8,128)(2,1)S(1)}, bf16[128,1920]{1,0:T(8,128)(2,1)}, u32[]{:S(2)}, u32[]{:S(2)}) %collective-permute-start.1) | collective-permute-done | bytes 491552 | tf_op jit(solution)/shard_map/ppermute | solution.py:139
  15.4 2.1 %collective-permute-start.2 = (bf16[128,1920]{1,0:T(8,128)(2,1)}, bf16[128,1920]{1,0:T(8,128)(2,1)S(1)}, u32[]{:S(2)}, u32[]{:S(2)}) collective-permute-start(bf16[128,1920]{1,0:T(8,128)(2,1)} %collective-permute-done.1.first), channel_id=1, source_target_pairs={{0,2},{2,0},{4,6},{6,4},{8,10},{10,8},{12,14},{14,12},{16,18},{18,... | collective-permute-start | bytes 1474568 | tf_op jit(solution)/shard_map/ppermute | solution.py:135
  17.5 1.7 %collective-permute-start.6 = (bf16[128,1920]{1,0:T(8,128)(2,1)}, bf16[128,1920]{1,0:T(8,128)(2,1)S(1)}, u32[]{:S(2)}, u32[]{:S(2)}) collective-permute-start(bf16[128,1920]{1,0:T(8,128)(2,1)} %collective-permute-done.1.first), channel_id=1, source_target_pairs={{0,1},{1,0},{2,3},{3,2},{4,5},{5,4},{6,7},{7,6},{8,9},{9,8},{10,11... | collective-permute-start | bytes 1474568 | tf_op jit(solution)/shard_map/ppermute | solution.py:143
  19.2 1.8 %shard_map.78.near = bf16[4,256,256]{2,1,0:T(8,128)(2,1)S(1)} custom-call(s32[8]{0:T(128)S(1)} %concatenate.3.table, bf16[128,1920]{1,0:T(8,128)(2,1)} %collective-permute-done.1.first, bf16[128,1920]{1,0:T(8,128)(2,1)S(1)} %collective-permute-done.2.second), custom_call_target="tpu_custom_call" | custom-call | flops 1000 | bytes 1000 | tf_op jit(solution)/shard_map/pallas_call | solution.py:401
  21.1 3.7 %shard_map.79.own = f32[4,800,256]{2,1,0:T(8,128)S(1)} custom-call(s32[8]{0:T(128)S(1)} %concatenate.3.table, bf16[256,1920]{1,0:T(8,128)(2,1)S(1)} %dynamic-slice_bitcast_fusion.ctx0, bf16[256,1920]{1,0:T(8,128)(2,1)} %collective-permute-done.3.ctx1, bf16[800,384]{1,0:T(8,128)(2,1)S(1)} %get-tuple-element.24.ext0, ...), custom_call_target="tpu_custom_call" | custom-call | flops 1000 | bytes 1000 | tf_op jit(solution)/shard_map/pallas_call | solution.py:401
  24.8 3.7 %collective-permute-done.ext2 = bf16[800,384]{1,0:T(8,128)(2,1)S(1)} collective-permute-done((bf16[800,384]{1,0:T(8,128)(2,1)S(1)}, bf16[800,384]{1,0:T(8,128)(2,1)S(1)}, u32[]{:S(2)}, u32[]{:S(2)}) %collective-permute-start) | collective-permute-done | bytes 614432 | tf_op jit(solution)/shard_map/ppermute | solution.py:139
  28.5 1.2 %collective-permute-start.5 = (bf16[800,384]{1,0:T(8,128)(2,1)S(1)}, bf16[800,384]{1,0:T(8,128)(2,1)S(1)}, u32[]{:S(2)}, u32[]{:S(2)}) collective-permute-start(bf16[800,384]{1,0:T(8,128)(2,1)S(1)} %collective-permute-done.ext2), channel_id=1, source_target_pairs={{0,2},{2,0},{4,6},{6,4},{8,10},{10,8},{12,14},{14,12},{16,18},{18,... | collective-permute-start | bytes 1843208 | tf_op jit(solution)/shard_map/ppermute | solution.py:135
  29.7 1.3 %collective-permute-done.6.far0 = bf16[128,1920]{1,0:T(8,128)(2,1)S(1)} collective-permute-done((bf16[128,1920]{1,0:T(8,128)(2,1)}, bf16[128,1920]{1,0:T(8,128)(2,1)S(1)}, u32[]{:S(2)}, u32[]{:S(2)}) %collective-permute-start.6) | collective-permute-done | bytes 491552 | tf_op jit(solution)/shard_map/ppermute | solution.py:143
  31.0 0.6 collective-permute-start.7
  31.6 1.5 %collective-permute-done.7.far1 = bf16[128,1920]{1,0:T(8,128)(2,1)S(1)} collective-permute-done((bf16[128,1920]{1,0:T(8,128)(2,1)S(1)}, bf16[128,1920]{1,0:T(8,128)(2,1)S(1)}, u32[]{:S(2)}, u32[]{:S(2)}) %collective-permute-start.7) | collective-permute-done | bytes 491552 | tf_op jit(solution)/shard_map/ppermute | solution.py:135
  33.1 1.8 %shard_map.81 = (f32[800,256]{1,0:T(8,128)S(1)}, f32[800,256]{1,0:T(8,128)S(1)}) custom-call(s32[8]{0:T(128)S(1)} %concatenate.3.table, bf16[800,384]{1,0:T(8,128)(2,1)S(1)} %collective-permute-done.ext2, bf16[800,384]{1,0:T(8,128)(2,1)S(1)} %collective-permute-done.5.ext3, bf16[4,256,256]{2,1,0:T(8,128)(2,1)S(1)} %shard_map.78.near, ...), custom_call_target="tpu_custom_call" | custom-call | flops 1000 | bytes 1000 | tf_op jit(solution)/shard_map/pallas_call | solution.py:401
  34.9 0.8 convert_element_type.30
  35.8 1.6 %collective-permute-start.8 = (f16[800,256]{1,0:T(8,128)(2,1)}, f16[800,256]{1,0:T(8,128)(2,1)}, u32[]{:S(2)}, u32[]{:S(2)}) collective-permute-start(f16[800,256]{1,0:T(8,128)(2,1)} %convert_element_type.30), channel_id=1, source_target_pairs={{0,8},{2,10},{4,12},{6,14},{8,0},{10,2},{12,4},{14,6},{16,24},{18,... | collective-permute-start | bytes 1228808 | tf_op jit(solution)/shard_map/ppermute | solution.py:449
  37.3 0.8 convert_element_type.34
  38.2 1.4 %collective-permute-start.10 = (f16[800,256]{1,0:T(8,128)(2,1)}, f16[800,256]{1,0:T(8,128)(2,1)}, u32[]{:S(2)}, u32[]{:S(2)}) collective-permute-start(f16[800,256]{1,0:T(8,128)(2,1)} %convert_element_type.34), channel_id=1, source_target_pairs={{8,16},{10,18},{12,20},{14,22},{16,8},{18,10},{20,12},{22,14},{9,1... | collective-permute-start | bytes 1228808 | tf_op jit(solution)/shard_map/ppermute | solution.py:449
  39.6 5.5 %collective-permute-start.9 = (f16[800,256]{1,0:T(8,128)(2,1)}, f16[800,256]{1,0:T(8,128)(2,1)}, u32[]{:S(2)}, u32[]{:S(2)}) collective-permute-start(f16[800,256]{1,0:T(8,128)(2,1)} %convert_element_type.34), channel_id=1, source_target_pairs={{0,16},{2,18},{4,20},{6,22},{24,8},{26,10},{28,12},{30,14},{1,17},... | collective-permute-start | bytes 1228808 | tf_op jit(solution)/shard_map/ppermute | solution.py:449
  45.1 1.9 %copy-done.2 = f32[4,800,256]{2,1,0:T(8,128)S(1)} copy-done((f32[4,800,256]{2,1,0:T(8,128)S(1)}, f32[4,800,256]{2,1,0:T(8,128)}, u32[]{:S(2)}) %copy-start.2) | copy-done | bytes 3276824
  47.0 1.1 %copy-done.6 = bf16[800,384]{1,0:T(8,128)(2,1)S(1)} copy-done((bf16[800,384]{1,0:T(8,128)(2,1)S(1)}, bf16[800,384]{1,0:T(8,128)(2,1)}, u32[]{:S(2)}) %copy-start.6) | copy-done | bytes 614424
  48.1 1.0 %copy-done.8 = bf16[128,1920]{1,0:T(8,128)(2,1)S(1)} copy-done((bf16[128,1920]{1,0:T(8,128)(2,1)S(1)}, bf16[128,1920]{1,0:T(8,128)(2,1)}, u32[]{:S(2)}) %copy-start.8) | copy-done | bytes 491544
  49.1 1.0 %copy-done.10 = bf16[128,1920]{1,0:T(8,128)(2,1)S(1)} copy-done((bf16[128,1920]{1,0:T(8,128)(2,1)S(1)}, bf16[128,1920]{1,0:T(8,128)(2,1)}, u32[]{:S(2)}) %copy-start.10) | copy-done | bytes 491544
  50.1 1.8 %shard_map.80 = (f32[800,256]{1,0:T(8,128)S(1)}, f32[800,256]{1,0:T(8,128)S(1)}) custom-call(s32[8]{0:T(128)S(1)} %concatenate.3.table, bf16[800,384]{1,0:T(8,128)(2,1)S(1)} %copy-done.4, bf16[800,384]{1,0:T(8,128)(2,1)S(1)} %copy-done.6, bf16[4,256,256]{2,1,0:T(8,128)(2,1)S(1)} %shard_map.78.near, bf16[128,1920]{1,0:T(8,128)(2,1)S(1)} %copy-done.8, ...), custom_call_target="tpu_custom_call" | custom-call | flops 1000 | bytes 1000 | tf_op jit(solution)/shard_map/pallas_call | solution.py:401
  51.9 0.9 copy-done.11
  52.8 1.2 %add_convert_fusion = f16[800,256]{1,0:T(8,128)(2,1)S(1)} fusion(f32[800,256]{1,0:T(8,128)S(1)} %get-tuple-element.32, f16[800,256]{1,0:T(8,128)(2,1)} %collective-permute-done.8, pred[]{:T(512)S(6)} %or.3), kind=kLoop, calls=%fused_computation.3 | loop fusion | flops 819200 | bytes 1638401 | tf_op jit(solution)/shard_map/convert_element_type | solution.py:459
  54.3 0.7 collective-permute-done.9
  55.0 1.4 %add_add_fusion = f32[800,256]{1,0:T(8,128)S(1)} fusion(f16[800,256]{1,0:T(8,128)(2,1)} %collective-permute-done.10, f16[800,256]{1,0:T(8,128)(2,1)} %collective-permute-done.9, f32[800,256]{1,0:T(8,128)S(1)} %copy-done.12, f16[800,256]{1,0:T(8,128)(2,1)} %collective-permute-done.8, pred[]{:T(512)S(6)} %not.3), kind=kLoop, calls=%fused_computation.2 | loop fusion | flops 1433600 | bytes 2867201 | tf_op jit(solution)/shard_map/add | solution.py:461
  56.4 13.1 %collective-permute-done.11 = f16[800,256]{1,0:T(8,128)(2,1)} collective-permute-done((f16[800,256]{1,0:T(8,128)(2,1)S(1)}, f16[800,256]{1,0:T(8,128)(2,1)}, u32[]{:S(2)}, u32[]{:S(2)}) %collective-permute-start.11) | collective-permute-done | bytes 409632 | tf_op jit(solution)/shard_map/ppermute | solution.py:449
  69.5 1.1 %convert_add_fusion.mixed = f32[800,256]{1,0:T(8,128)S(1)} fusion(f32[800,256]{1,0:T(8,128)S(1)} %add_add_fusion, f16[800,256]{1,0:T(8,128)(2,1)} %collective-permute-done.11), kind=kLoop, calls=%fused_computation.1 | loop fusion | flops 409600 | bytes 2048000 | tf_op jit(solution)/shard_map/add | solution.py:463
  70.5 0.4 shard_map.82
  71.0 0.3 shard_map.83
  71.3 1.3 %collective-permute-start.18 = (bf16[2,128,128]{2,1,0:T(8,128)(2,1)S(1)}, bf16[2,128,128]{2,1,0:T(8,128)(2,1)S(1)}, u32[]{:S(2)}, u32[]{:S(2)}) collective-permute-start(bf16[2,128,128]{2,1,0:T(8,128)(2,1)S(1)} %get-tuple-element.40), channel_id=1, source_target_pairs={{0,1},{1,0},{2,3},{3,2},{4,5},{5,4},{6,7},{7,6},{8,9},{9,8},{10,11... | collective-permute-start | bytes 196616 | tf_op jit(solution)/shard_map/ppermute | solution.py:143
  72.8 2.3 %collective-permute-start.13 = (f16[4,16,800]{2,1,0:T(8,128)(2,1)S(1)}, f16[4,16,800]{2,1,0:T(8,128)(2,1)S(1)}, u32[]{:S(2)}, u32[]{:S(2)}) collective-permute-start(f16[4,16,800]{2,1,0:T(8,128)(2,1)S(1)} %get-tuple-element.48), channel_id=1, source_target_pairs={{0,16},{2,18},{4,20},{6,22},{8,24},{10,26},{12,28},{14,30},{16,0},... | collective-permute-start | bytes 307208 | tf_op jit(solution)/shard_map/ppermute | solution.py:449
  75.1 1.2 %collective-permute-start.14 = (f16[4,16,800]{2,1,0:T(8,128)(2,1)S(1)}, f16[4,16,800]{2,1,0:T(8,128)(2,1)S(1)}, u32[]{:S(2)}, u32[]{:S(2)}) collective-permute-start(f16[4,16,800]{2,1,0:T(8,128)(2,1)S(1)} %get-tuple-element.47), channel_id=1, source_target_pairs={{0,24},{2,26},{4,28},{6,30},{8,16},{10,18},{12,20},{14,22},{16,8},... | collective-permute-start | bytes 307208 | tf_op jit(solution)/shard_map/ppermute | solution.py:449
  76.4 2.5 %shard_map.85 = bf16[16,16,800]{2,1,0:T(8,128)(2,1)} custom-call(f32[2,128,128]{2,1,0:T(8,128)S(1)} %get-tuple-element.37.near, bf16[2,128,128]{2,1,0:T(8,128)(2,1)S(1)} %collective-permute-done.18.far, f32[256,800]{1,0:T(8,128)S(1)} %get-tuple-element.41.turned), custom_call_target="tpu_custom_call" | custom-call | tf_op jit(solution)/shard_map/pallas_call | solution.py:479
  78.9 7.2 %all-to-all-start = ((bf16[16,16,800]{2,1,0:T(8,128)(2,1)}), bf16[16,16,800]{2,1,0:T(8,128)(2,1)S(1)}, u32[]{:S(2)}, u32[]{:S(2)}) async-start(bf16[16,16,800]{2,1,0:T(8,128)(2,1)} %shard_map.85), calls=%async_computation | async-start | bytes 917504 | tf_op jit(solution)/shard_map/all_to_all | solution.py:507
  86.3 0.2 collective-permute-start.15
  86.5 1.7 %collective-permute-start.16 = (f16[4,16,800]{2,1,0:T(8,128)(2,1)S(1)}, f16[4,16,800]{2,1,0:T(8,128)(2,1)S(1)}, u32[]{:S(2)}, u32[]{:S(2)}) collective-permute-start(f16[4,16,800]{2,1,0:T(8,128)(2,1)S(1)} %pad_maximum_fusion.1), channel_id=1, source_target_pairs={{0,4},{2,6},{4,0},{6,2},{8,12},{10,14},{12,8},{14,10},{16,20},{18,... | collective-permute-start | bytes 307208 | tf_op jit(solution)/shard_map/ppermute | solution.py:495
  88.2 0.5 collective-permute-start.17
  88.8 5.2 %collective-permute-done.16 = f16[4,16,800]{2,1,0:T(8,128)(2,1)S(1)} collective-permute-done((f16[4,16,800]{2,1,0:T(8,128)(2,1)S(1)}, f16[4,16,800]{2,1,0:T(8,128)(2,1)S(1)}, u32[]{:S(2)}, u32[]{:S(2)}) %collective-permute-start.16) | collective-permute-done | bytes 102432 | tf_op jit(solution)/shard_map/ppermute | solution.py:495
  93.9 3.9 %collective-permute-done.17 = f16[4,16,800]{2,1,0:T(8,128)(2,1)S(1)} collective-permute-done((f16[4,16,800]{2,1,0:T(8,128)(2,1)S(1)}, f16[4,16,800]{2,1,0:T(8,128)(2,1)S(1)}, u32[]{:S(2)}, u32[]{:S(2)}) %collective-permute-start.17) | collective-permute-done | bytes 102432 | tf_op jit(solution)/shard_map/ppermute | solution.py:495
  97.9 1.9 %shard_map.84 = f32[2,800,120]{2,1,0:T(8,128)} custom-call(s32[3]{0:T(128)S(1)} %pad_add_fusion.here, f32[4,4,16,800]{3,2,1,0:T(8,128)S(1)} %maximum_convert_fusion.mixed_back, f32[2,800,120]{2,1,0:T(8,128)S(1)} %bitcast.40), custom_call_target="tpu_custom_call" | custom-call | flops 10000000000 | bytes 2000000 | tf_op jit(solution)/shard_map/pallas_call | solution.py:500
  99.9 1.2 %shard_map.86 = f32[2,800,120]{2,1,0:T(8,128)} custom-call(bf16[4,2,2,16,800]{4,3,2,1,0:T(8,128)(2,1)S(1)} %bitcast.36, f32[2,800,120]{2,1,0:T(8,128)S(1)} %bitcast.37), custom_call_target="tpu_custom_call" | custom-call | tf_op jit(solution)/shard_map/pallas_call | solution.py:508
  (57 shorter events, 1.2 us)
Async XLA Ops:
  0.6 1.6 %copy-start = (bf16[2,256,1920]{2,1,0:T(8,128)(2,1)S(1)}, bf16[2,256,1920]{2,1,0:T(8,128)(2,1)}, u32[]{:S(2)}) copy-start(bf16[2,256,1920]{2,1,0:T(8,128)(2,1)} %param.6) | copy-start | bytes 5898244
  2.2 13.2 %collective-permute-start.1 = (bf16[128,1920]{1,0:T(8,128)(2,1)S(1)}, bf16[128,1920]{1,0:T(8,128)(2,1)}, u32[]{:S(2)}, u32[]{:S(2)}) collective-permute-start(bf16[128,1920]{1,0:T(8,128)(2,1)S(1)} %dynamic-slice_bitcast_fusion.1), channel_id=1, source_target_pairs={{0,4},{2,6},{4,0},{6,2},{8,12},{10,14},{12,8},{14,10},{16,20},{18,... | collective-permute-start | bytes 1474568 | tf_op jit(solution)/shard_map/ppermute | solution.py:139
  4.4 16.6 %collective-permute-start.3 = (bf16[256,1920]{1,0:T(8,128)(2,1)S(1)}, bf16[256,1920]{1,0:T(8,128)(2,1)}, u32[]{:S(2)}, u32[]{:S(2)}) collective-permute-start(bf16[256,1920]{1,0:T(8,128)(2,1)S(1)} %dynamic-slice_bitcast_fusion.ctx0), channel_id=1, source_target_pairs={{0,2},{2,0},{4,6},{6,4},{8,10},{10,8},{12,14},{14,12},{16,18},{18,... | collective-permute-start | bytes 2949128 | tf_op jit(solution)/shard_map/ppermute | solution.py:135
  6.9 1.1 %copy-start.14 = (bf16[2,256,800]{1,2,0:T(8,128)(2,1)S(1)}, bf16[2,256,800]{1,2,0:T(8,128)(2,1)}, u32[]{:S(2)}) copy-start(bf16[2,256,800]{1,2,0:T(8,128)(2,1)} %param.7) | copy-start | bytes 2457604
  8.0 1.1 %copy-start.15 = (f32[2,120,800]{1,2,0:T(8,128)S(1)}, f32[2,120,800]{1,2,0:T(8,128)}, u32[]{:S(2)}) copy-start(f32[2,120,800]{1,2,0:T(8,128)} %param.9) | copy-start | bytes 2304004
  9.9 11.1 %collective-permute-start.4 = (bf16[800,384]{1,0:T(8,128)(2,1)S(1)}, bf16[800,384]{1,0:T(8,128)(2,1)S(1)}, u32[]{:S(2)}, u32[]{:S(2)}) collective-permute-start(bf16[800,384]{1,0:T(8,128)(2,1)S(1)} %get-tuple-element.24.ext0), channel_id=1, source_target_pairs={{0,2},{2,0},{4,6},{6,4},{8,10},{10,8},{12,14},{14,12},{16,18},{18,... | collective-permute-start | bytes 1843208 | tf_op jit(solution)/shard_map/ppermute | solution.py:135
  10.1 18.4 %collective-permute-start = (bf16[800,384]{1,0:T(8,128)(2,1)S(1)}, bf16[800,384]{1,0:T(8,128)(2,1)S(1)}, u32[]{:S(2)}, u32[]{:S(2)}) collective-permute-start(bf16[800,384]{1,0:T(8,128)(2,1)S(1)} %get-tuple-element.23), channel_id=1, source_target_pairs={{0,4},{2,6},{4,0},{6,2},{8,12},{10,14},{12,8},{14,10},{16,20},{18,... | collective-permute-start | bytes 1843208 | tf_op jit(solution)/shard_map/ppermute | solution.py:139
  15.4 3.8 %collective-permute-start.2 = (bf16[128,1920]{1,0:T(8,128)(2,1)}, bf16[128,1920]{1,0:T(8,128)(2,1)S(1)}, u32[]{:S(2)}, u32[]{:S(2)}) collective-permute-start(bf16[128,1920]{1,0:T(8,128)(2,1)} %collective-permute-done.1.first), channel_id=1, source_target_pairs={{0,2},{2,0},{4,6},{6,4},{8,10},{10,8},{12,14},{14,12},{16,18},{18,... | collective-permute-start | bytes 1474568 | tf_op jit(solution)/shard_map/ppermute | solution.py:135
  17.5 13.6 %collective-permute-start.6 = (bf16[128,1920]{1,0:T(8,128)(2,1)}, bf16[128,1920]{1,0:T(8,128)(2,1)S(1)}, u32[]{:S(2)}, u32[]{:S(2)}) collective-permute-start(bf16[128,1920]{1,0:T(8,128)(2,1)} %collective-permute-done.1.first), channel_id=1, source_target_pairs={{0,1},{1,0},{2,3},{3,2},{4,5},{5,4},{6,7},{7,6},{8,9},{9,8},{10,11... | collective-permute-start | bytes 1474568 | tf_op jit(solution)/shard_map/ppermute | solution.py:143
  24.8 10.1 %copy-start.1 = (f32[4,800,256]{2,1,0:T(8,128)}, f32[4,800,256]{2,1,0:T(8,128)S(1)}, u32[]{:S(2)}) copy-start(f32[4,800,256]{2,1,0:T(8,128)S(1)} %shard_map.79.own) | copy-start | bytes 9830404
  28.5 6.4 %copy-start.3 = (bf16[800,384]{1,0:T(8,128)(2,1)}, bf16[800,384]{1,0:T(8,128)(2,1)S(1)}, u32[]{:S(2)}) copy-start(bf16[800,384]{1,0:T(8,128)(2,1)S(1)} %collective-permute-done.ext2) | copy-start | bytes 1843204
  28.5 4.6 %collective-permute-start.5 = (bf16[800,384]{1,0:T(8,128)(2,1)S(1)}, bf16[800,384]{1,0:T(8,128)(2,1)S(1)}, u32[]{:S(2)}, u32[]{:S(2)}) collective-permute-start(bf16[800,384]{1,0:T(8,128)(2,1)S(1)} %collective-permute-done.ext2), channel_id=1, source_target_pairs={{0,2},{2,0},{4,6},{6,4},{8,10},{10,8},{12,14},{14,12},{16,18},{18,... | collective-permute-start | bytes 1843208 | tf_op jit(solution)/shard_map/ppermute | solution.py:135
  31.0 3.9 %copy-start.7 = (bf16[128,1920]{1,0:T(8,128)(2,1)}, bf16[128,1920]{1,0:T(8,128)(2,1)S(1)}, u32[]{:S(2)}) copy-start(bf16[128,1920]{1,0:T(8,128)(2,1)S(1)} %collective-permute-done.6.far0) | copy-start | bytes 1474564
  31.0 2.1 %collective-permute-start.7 = (bf16[128,1920]{1,0:T(8,128)(2,1)S(1)}, bf16[128,1920]{1,0:T(8,128)(2,1)S(1)}, u32[]{:S(2)}, u32[]{:S(2)}) collective-permute-start(bf16[128,1920]{1,0:T(8,128)(2,1)S(1)} %collective-permute-done.6.far0), channel_id=1, source_target_pairs={{0,2},{2,0},{4,6},{6,4},{8,10},{10,8},{12,14},{14,12},{16,18},{18,... | collective-permute-start | bytes 1474568 | tf_op jit(solution)/shard_map/ppermute | solution.py:135
  33.1 1.8 %copy-start.9 = (bf16[128,1920]{1,0:T(8,128)(2,1)}, bf16[128,1920]{1,0:T(8,128)(2,1)S(1)}, u32[]{:S(2)}) copy-start(bf16[128,1920]{1,0:T(8,128)(2,1)S(1)} %collective-permute-done.7.far1) | copy-start | bytes 1474564
  33.1 1.8 %copy-start.5 = (bf16[800,384]{1,0:T(8,128)(2,1)}, bf16[800,384]{1,0:T(8,128)(2,1)S(1)}, u32[]{:S(2)}) copy-start(bf16[800,384]{1,0:T(8,128)(2,1)S(1)} %collective-permute-done.5.ext3) | copy-start | bytes 1843204
  34.9 10.1 %copy-start.4 = (bf16[800,384]{1,0:T(8,128)(2,1)S(1)}, bf16[800,384]{1,0:T(8,128)(2,1)}, u32[]{:S(2)}) copy-start(bf16[800,384]{1,0:T(8,128)(2,1)} %copy-done.3) | copy-start | bytes 1843204
  35.8 17.0 %collective-permute-start.8 = (f16[800,256]{1,0:T(8,128)(2,1)}, f16[800,256]{1,0:T(8,128)(2,1)}, u32[]{:S(2)}, u32[]{:S(2)}) collective-permute-start(f16[800,256]{1,0:T(8,128)(2,1)} %convert_element_type.30), channel_id=1, source_target_pairs={{0,8},{2,10},{4,12},{6,14},{8,0},{10,2},{12,4},{14,6},{16,24},{18,... | collective-permute-start | bytes 1228808 | tf_op jit(solution)/shard_map/ppermute | solution.py:449
  38.2 16.1 %collective-permute-start.10 = (f16[800,256]{1,0:T(8,128)(2,1)}, f16[800,256]{1,0:T(8,128)(2,1)}, u32[]{:S(2)}, u32[]{:S(2)}) collective-permute-start(f16[800,256]{1,0:T(8,128)(2,1)} %convert_element_type.34), channel_id=1, source_target_pairs={{8,16},{10,18},{12,20},{14,22},{16,8},{18,10},{20,12},{22,14},{9,1... | collective-permute-start | bytes 1228808 | tf_op jit(solution)/shard_map/ppermute | solution.py:449
  39.6 15.3 %collective-permute-start.9 = (f16[800,256]{1,0:T(8,128)(2,1)}, f16[800,256]{1,0:T(8,128)(2,1)}, u32[]{:S(2)}, u32[]{:S(2)}) collective-permute-start(f16[800,256]{1,0:T(8,128)(2,1)} %convert_element_type.34), channel_id=1, source_target_pairs={{0,16},{2,18},{4,20},{6,22},{24,8},{26,10},{28,12},{30,14},{1,17},... | collective-permute-start | bytes 1228808 | tf_op jit(solution)/shard_map/ppermute | solution.py:449
  45.1 1.9 %copy-start.2 = (f32[4,800,256]{2,1,0:T(8,128)S(1)}, f32[4,800,256]{2,1,0:T(8,128)}, u32[]{:S(2)}) copy-start(f32[4,800,256]{2,1,0:T(8,128)} %copy-done.1) | copy-start | bytes 9830404
  47.0 1.1 %copy-start.6 = (bf16[800,384]{1,0:T(8,128)(2,1)S(1)}, bf16[800,384]{1,0:T(8,128)(2,1)}, u32[]{:S(2)}) copy-start(bf16[800,384]{1,0:T(8,128)(2,1)} %copy-done.5) | copy-start | bytes 1843204
  48.1 1.0 %copy-start.8 = (bf16[128,1920]{1,0:T(8,128)(2,1)S(1)}, bf16[128,1920]{1,0:T(8,128)(2,1)}, u32[]{:S(2)}) copy-start(bf16[128,1920]{1,0:T(8,128)(2,1)} %copy-done.7) | copy-start | bytes 1474564
  49.1 1.0 %copy-start.10 = (bf16[128,1920]{1,0:T(8,128)(2,1)S(1)}, bf16[128,1920]{1,0:T(8,128)(2,1)}, u32[]{:S(2)}) copy-start(bf16[128,1920]{1,0:T(8,128)(2,1)} %copy-done.9) | copy-start | bytes 1474564
  51.9 0.9 copy-start.11
  52.8 2.1 %copy-start.12 = (f32[800,256]{1,0:T(8,128)S(1)}, f32[800,256]{1,0:T(8,128)}, u32[]{:S(2)}) copy-start(f32[800,256]{1,0:T(8,128)} %copy-done.11) | copy-start | bytes 2457604
  54.1 15.4 %collective-permute-start.11 = (f16[800,256]{1,0:T(8,128)(2,1)S(1)}, f16[800,256]{1,0:T(8,128)(2,1)}, u32[]{:S(2)}, u32[]{:S(2)}) collective-permute-start(f16[800,256]{1,0:T(8,128)(2,1)S(1)} %add_convert_fusion), channel_id=1, source_target_pairs={{0,8},{2,10},{4,12},{6,14},{8,24},{10,26},{12,28},{14,30},{24,16},... | collective-permute-start | bytes 1228808 | tf_op jit(solution)/shard_map/ppermute | solution.py:449
  71.3 5.1 %collective-permute-start.18 = (bf16[2,128,128]{2,1,0:T(8,128)(2,1)S(1)}, bf16[2,128,128]{2,1,0:T(8,128)(2,1)S(1)}, u32[]{:S(2)}, u32[]{:S(2)}) collective-permute-start(bf16[2,128,128]{2,1,0:T(8,128)(2,1)S(1)} %get-tuple-element.40), channel_id=1, source_target_pairs={{0,1},{1,0},{2,3},{3,2},{4,5},{5,4},{6,7},{7,6},{8,9},{9,8},{10,11... | collective-permute-start | bytes 196616 | tf_op jit(solution)/shard_map/ppermute | solution.py:143
  72.7 13.4 %collective-permute-start.12 = (f16[4,16,800]{2,1,0:T(8,128)(2,1)S(1)}, f16[4,16,800]{2,1,0:T(8,128)(2,1)S(1)}, u32[]{:S(2)}, u32[]{:S(2)}) collective-permute-start(f16[4,16,800]{2,1,0:T(8,128)(2,1)S(1)} %get-tuple-element.46), channel_id=1, source_target_pairs={{0,8},{2,10},{4,12},{6,14},{8,0},{10,2},{12,4},{14,6},{16,24},{18,... | collective-permute-start | bytes 307208 | tf_op jit(solution)/shard_map/ppermute | solution.py:449
  72.8 13.3 %collective-permute-start.13 = (f16[4,16,800]{2,1,0:T(8,128)(2,1)S(1)}, f16[4,16,800]{2,1,0:T(8,128)(2,1)S(1)}, u32[]{:S(2)}, u32[]{:S(2)}) collective-permute-start(f16[4,16,800]{2,1,0:T(8,128)(2,1)S(1)} %get-tuple-element.48), channel_id=1, source_target_pairs={{0,16},{2,18},{4,20},{6,22},{8,24},{10,26},{12,28},{14,30},{16,0},... | collective-permute-start | bytes 307208 | tf_op jit(solution)/shard_map/ppermute | solution.py:449
  75.1 11.1 %collective-permute-start.14 = (f16[4,16,800]{2,1,0:T(8,128)(2,1)S(1)}, f16[4,16,800]{2,1,0:T(8,128)(2,1)S(1)}, u32[]{:S(2)}, u32[]{:S(2)}) collective-permute-start(f16[4,16,800]{2,1,0:T(8,128)(2,1)S(1)} %get-tuple-element.47), channel_id=1, source_target_pairs={{0,24},{2,26},{4,28},{6,30},{8,16},{10,18},{12,20},{14,22},{16,8},... | collective-permute-start | bytes 307208 | tf_op jit(solution)/shard_map/ppermute | solution.py:449
  78.9 21.0 %all-to-all-start = ((bf16[16,16,800]{2,1,0:T(8,128)(2,1)}), bf16[16,16,800]{2,1,0:T(8,128)(2,1)S(1)}, u32[]{:S(2)}, u32[]{:S(2)}) async-start(bf16[16,16,800]{2,1,0:T(8,128)(2,1)} %shard_map.85), calls=%async_computation | async-start | bytes 917504 | tf_op jit(solution)/shard_map/all_to_all | solution.py:507
  86.1 11.9 %copy-start.16 = (f32[2,120,800]{1,2,0:T(8,128)S(1)}, f32[2,120,800]{1,2,0:T(8,128)}, u32[]{:S(2)}) copy-start(f32[2,120,800]{1,2,0:T(8,128)} %param.9) | copy-start | bytes 2304004
  86.3 2.5 %collective-permute-start.15 = (f16[4,16,800]{2,1,0:T(8,128)(2,1)S(1)}, f16[4,16,800]{2,1,0:T(8,128)(2,1)S(1)}, u32[]{:S(2)}, u32[]{:S(2)}) collective-permute-start(f16[4,16,800]{2,1,0:T(8,128)(2,1)S(1)} %pad_maximum_fusion), channel_id=1, source_target_pairs={{0,2},{2,0},{4,6},{6,4},{8,10},{10,8},{12,14},{14,12},{16,18},{18,... | collective-permute-start | bytes 307208 | tf_op jit(solution)/shard_map/ppermute | solution.py:495
  86.5 7.5 %collective-permute-start.16 = (f16[4,16,800]{2,1,0:T(8,128)(2,1)S(1)}, f16[4,16,800]{2,1,0:T(8,128)(2,1)S(1)}, u32[]{:S(2)}, u32[]{:S(2)}) collective-permute-start(f16[4,16,800]{2,1,0:T(8,128)(2,1)S(1)} %pad_maximum_fusion.1), channel_id=1, source_target_pairs={{0,4},{2,6},{4,0},{6,2},{8,12},{10,14},{12,8},{14,10},{16,20},{18,... | collective-permute-start | bytes 307208 | tf_op jit(solution)/shard_map/ppermute | solution.py:495
  88.2 9.6 %collective-permute-start.17 = (f16[4,16,800]{2,1,0:T(8,128)(2,1)S(1)}, f16[4,16,800]{2,1,0:T(8,128)(2,1)S(1)}, u32[]{:S(2)}, u32[]{:S(2)}) collective-permute-start(f16[4,16,800]{2,1,0:T(8,128)(2,1)S(1)} %pad_maximum_fusion.2), channel_id=1, source_target_pairs={{0,6},{2,4},{4,2},{6,0},{8,14},{10,12},{12,10},{14,8},{16,22},{18,... | collective-permute-start | bytes 307208 | tf_op jit(solution)/shard_map/ppermute | solution.py:495
  97.9 1.9 %copy-start.13 = (f32[2,120,800]{1,2,0:T(8,128)S(1)}, f32[2,120,800]{1,2,0:T(8,128)}, u32[]{:S(2)}) copy-start(f32[2,120,800]{1,2,0:T(8,128)} %param.10) | copy-start | bytes 2304004
